TPU v7x, 32 devices: a whole 2x2x4 slice. The times are simulated.
32 devices in a mesh: seq: 32 (over z, y, x, core).
Axes of the slice: x: 2, y: 2, z: 4, core: 2. Of those that a mesh axis runs over, the one named last changes fastest.
Arguments:
- tokens_in: bfloat16 [8192, 1024], P('seq'), may hold values from -6 to 6
- cotangent: bfloat16 [8192, 1024], P('seq'), may hold values from -6 to 6
- pad_mask: int32 [8192], P('seq'), may hold values 0 or 1
- doc_lengths: int32 [7], replicated, may hold values from 64 to 7745, as said below
- masters: float32 [480, 32, 1024], P('seq')
- moment_one: float32 [480, 32, 1024], P('seq'), may hold values from -16 to 16
- moment_two: float32 [480, 32, 1024], P('seq'), may hold values from 0.4096 to 6.5536
- block_slot: int32 [416], replicated, may hold values from 0 to 479, as said below
- vectors: float32 [11, 1024], replicated
- vector_one: float32 [11, 1024], replicated, may hold values from -28 to 28
- vector_two: float32 [11, 1024], replicated, may hold values from 0.8192 to 16.384
Outputs:
- layer_out: bfloat16 [8192, 1024], P('seq')
- input_grad: float32 [8192, 1024], P('seq')
- new_moment_one: float32 [480, 32, 1024], P('seq')
- new_moment_two: float32 [480, 32, 1024], P('seq')
- new_masters: float32 [480, 32, 1024], P('seq')
- new_vector_one: float32 [11, 1024], replicated
- new_vector_two: float32 [11, 1024], replicated
- new_vectors: float32 [11, 1024], replicated
Inputs may be any that keep to these rules, and one draw needn't show every extreme that they name: `doc_lengths`: the 7 documents fill all 8192 tokens; the fourth begins among the first 256 tokens, ends among the last 256 and has exactly 7745 tokens; every other one has 64 tokens or more. `block_slot`: distinct slot numbers; all 15 slots of some device are named.
All inputs are finite; a program needn't handle non-finite values. No bound on the sum of `pad_mask` on one device may be relied on, other than what follows from the above.
Results may differ from a plain program's by a relative error of at most 0.01.
Values may be sent and summed in bfloat16 or wider, within the bound.
A program may use at most 384 MiB of HBM per device.

v0:
```python
import math

import jax
import jax.numpy as jnp
from jax import lax
from jax.sharding import PartitionSpec as P

EMBED_SIZE = 1024
FF = 4096
BLOCK_ROWS = 32
ROWS_ALL = 13312
BLOCKS = 416
STEP = 10


NEGATIVE = -1e30
NORM_EPS = 1e-05
BETA_ONE = 0.9
BETA_TWO = 0.999
ADAM_EPS = 1e-08
MATRIX_RATE = 0.05
WEIGHT_DECAY = 0.01
VECTOR_RATE = (0.25, 0.25, 0.25, 0.25, 0.25, 2.0, 0.25, 0.25, 0.25, 0.25, 0.25)


def shifted(block, axis, distance):
    devices = range(lax.axis_size(axis))
    route = [(i - distance, i) for i in devices if i - distance in devices]
    return lax.ppermute(block, axis, route)


def product(left_side, right_side):
    return jnp.dot(left_side, right_side, preferred_element_type=jnp.float32)


def product_back(left_side, right_side):
    return lax.dot_general(
        left_side, right_side, (((1,), (1,)), ((), ())), preferred_element_type=jnp.float32
    )


def product_left(left_side, right_side):
    return lax.dot_general(
        left_side, right_side, (((0,), (0,)), ((), ())), preferred_element_type=jnp.float32
    )


def norm_forward(values, gain_row, bias_row):
    mean_row = jnp.mean(values, axis=1, keepdims=True)
    centered = values - mean_row
    inverse = lax.rsqrt(jnp.mean(centered * centered, axis=1, keepdims=True) + NORM_EPS)
    unit_rows = centered * inverse
    return (unit_rows * gain_row + bias_row, unit_rows, inverse)


def norm_backward(grad_out, unit_rows, inverse, gain_row):
    scaled = grad_out * gain_row
    inner = (
        scaled
        - jnp.mean(scaled, axis=1, keepdims=True)
        - unit_rows * jnp.mean(scaled * unit_rows, axis=1, keepdims=True)
    )
    return (inner * inverse, jnp.sum(grad_out * unit_rows, axis=0), jnp.sum(grad_out, axis=0))


def split_rows(gathered, block_slot):
    weight_rows = gathered[block_slot].reshape(ROWS_ALL, EMBED_SIZE)
    return (
        weight_rows[:EMBED_SIZE],
        weight_rows[EMBED_SIZE : 2 * EMBED_SIZE],
        weight_rows[2 * EMBED_SIZE : 3 * EMBED_SIZE],
        weight_rows[3 * EMBED_SIZE : 4 * EMBED_SIZE],
        weight_rows[4 * EMBED_SIZE : 5 * EMBED_SIZE],
        weight_rows[5 * EMBED_SIZE : 5 * EMBED_SIZE + FF],
        weight_rows[5 * EMBED_SIZE + FF :],
    )


def local_pass(key_rows, value_rows, starts, decay_rate, time_first):
    tokens, features = key_rows.shape
    block_size = math.gcd(tokens, 128)
    block_count = tokens // block_size
    position = jnp.arange(block_size, dtype=jnp.float32)
    causal = (position[None, :] < position[:, None]).astype(jnp.float32)

    def block_step(carry_state, pieces):
        num_state, den_state, max_state = carry_state
        key_block, value_block, start_block = pieces
        doc_index = jnp.cumsum(start_block)
        same_doc = (doc_index[:, None] == doc_index[None, :]).astype(jnp.float32) * causal
        carried = (doc_index == 0.0)[:, None]
        top_key = jnp.max(key_block, axis=0)
        weight_in = jnp.exp(
            key_block - top_key - (block_size - 1.0 - position)[:, None] * decay_rate
        )
        partial_value = jnp.dot(
            same_doc,
            jnp.concatenate([weight_in * value_block, weight_in], axis=1),
            precision=lax.Precision.HIGHEST,
            preferred_element_type=jnp.float32,
        )
        inner_log = top_key + (block_size - position)[:, None] * decay_rate
        carry_log = jnp.where(carried, max_state - position[:, None] * decay_rate, NEGATIVE)
        own_log = time_first + key_block
        top_log = jnp.maximum(jnp.maximum(inner_log, carry_log), own_log)
        inner_weight = jnp.exp(inner_log - top_log)
        carry_weight = jnp.exp(carry_log - top_log)
        own_weight = jnp.exp(own_log - top_log)
        numerator = (
            inner_weight * partial_value[:, :features]
            + carry_weight * num_state
            + own_weight * value_block
        )
        denominator = (
            inner_weight * partial_value[:, features:] + carry_weight * den_state + own_weight
        )
        last_doc = (doc_index == doc_index[block_size - 1]).astype(jnp.float32)[:, None]
        end_log = jnp.where(
            doc_index[block_size - 1] == 0.0, max_state - block_size * decay_rate, NEGATIVE
        )
        new_max = jnp.maximum(top_key, end_log)
        inner_scale = jnp.exp(top_key - new_max)
        carry_scale = jnp.exp(end_log - new_max)
        new_num = (
            inner_scale * jnp.sum(last_doc * weight_in * value_block, axis=0)
            + carry_scale * num_state
        )
        new_den = inner_scale * jnp.sum(last_doc * weight_in, axis=0) + carry_scale * den_state
        return ((new_num, new_den, new_max), (numerator, denominator, top_log))

    zeros_row = jnp.zeros((features,), jnp.float32)
    initial = (zeros_row, zeros_row, jnp.full((features,), NEGATIVE, jnp.float32))
    pieces = (
        key_rows.reshape(block_count, block_size, features),
        value_rows.reshape(block_count, block_size, features),
        starts.reshape(block_count, block_size),
    )
    summary, (numerator, denominator, top_log) = lax.scan(block_step, initial, pieces)
    return (
        numerator.reshape(tokens, features),
        denominator.reshape(tokens, features),
        top_log.reshape(tokens, features),
        summary,
    )


def with_state(
    numerator, denominator, top_log, state_num, state_den, state_max, carried_dev, decay_rate
):
    steps = jnp.arange(numerator.shape[0], dtype=jnp.float32)[:, None]
    carry_log = jnp.where(carried_dev, state_max - steps * decay_rate, NEGATIVE)
    joint_max = jnp.maximum(top_log, carry_log)
    local_weight = jnp.exp(top_log - joint_max)
    carry_weight = jnp.exp(carry_log - joint_max)
    return (local_weight * numerator + carry_weight * state_num) / (
        local_weight * denominator + carry_weight * state_den
    )


def adam_update(weight, first_moment, second_moment, gradient, step_rate, feature_fade_speed):
    first_moment = BETA_ONE * first_moment + (1.0 - BETA_ONE) * gradient
    second_moment = BETA_TWO * second_moment + (1.0 - BETA_TWO) * gradient * gradient
    first_fixed = first_moment / (1.0 - BETA_ONE**STEP)
    second_fixed = second_moment / (1.0 - BETA_TWO**STEP)
    weight = weight - step_rate * (
        first_fixed / (jnp.sqrt(second_fixed) + ADAM_EPS) + feature_fade_speed * weight
    )
    return (first_moment, second_moment, weight)


def body(
    tokens_in,
    cotangent,
    pad_mask,
    doc_lengths,
    masters,
    moment_one,
    moment_two,
    block_slot,
    vectors,
    vector_one,
    vector_two,
):
    tokens = tokens_in.shape[0]
    features = tokens_in.shape[1]
    devices = lax.axis_size("seq")
    device_place = lax.axis_index("seq")
    offsets = jnp.cumsum(doc_lengths) - doc_lengths
    positions = device_place * tokens + jnp.arange(tokens, dtype=jnp.int32)
    starts = jnp.sum((positions[:, None] == offsets[None, :]).astype(jnp.float32), axis=1)
    keep_rows = (1.0 - starts)[:, None]
    carried_dev = (jnp.cumsum(starts) == 0.0)[:, None]
    zeros_row = jnp.zeros((features,), jnp.float32)
    owned_rows = masters.astype(jnp.bfloat16)
    forward_rows = split_rows(lax.all_gather(owned_rows, "seq", axis=0, tiled=True), block_slot)
    key_w, value_w, recept_w, output_w, chan_recept_w, chan_key_w, chan_value_w = forward_rows
    inputs = tokens_in.astype(jnp.float32)
    normed, unit_one, inverse_one = norm_forward(inputs, vectors[0], vectors[1])
    rim_one = shifted(normed[tokens - 1 :], "seq", 1)
    previous = jnp.concatenate([rim_one, normed[:-1]], axis=0) * keep_rows
    in_key = (vectors[2] * normed + (1.0 - vectors[2]) * previous).astype(jnp.bfloat16)
    in_value = (vectors[3] * normed + (1.0 - vectors[3]) * previous).astype(jnp.bfloat16)
    in_recept = (vectors[4] * normed + (1.0 - vectors[4]) * previous).astype(jnp.bfloat16)
    key_rows = product(in_key, key_w)
    value_rows = product(in_value, value_w)
    receptance = product(in_recept, recept_w)
    decay_rate = jnp.exp(vectors[5])
    time_first = vectors[6]
    local_out, head_back = jax.vjp(
        lambda key_arg, value_arg, rate_arg, first_arg: local_pass(
            key_arg, value_arg, starts, rate_arg, first_arg
        ),
        key_rows,
        value_rows,
        decay_rate,
        time_first,
    )
    numerator, denominator, top_log, summary = local_out
    sum_num, sum_den, sum_max = summary
    reset_flag = jnp.max(starts)[None]
    count_row = jnp.full((1,), float(tokens), jnp.float32)
    empty_state = (
        zeros_row,
        zeros_row,
        jnp.full((features,), NEGATIVE, jnp.float32),
        jnp.zeros((1,), jnp.float32),
        jnp.zeros((1,), jnp.float32),
    )

    def merge_state(early, later):
        early_num, early_den, early_max, early_count, early_reset = early
        later_num, later_den, later_max, later_count, later_reset = later
        aged_max = early_max - later_count * decay_rate
        joint_max = jnp.maximum(aged_max, later_max)
        old_weight = jnp.exp(aged_max - joint_max)
        new_weight = jnp.exp(later_max - joint_max)
        restart = later_reset > 0.5
        return (
            jnp.where(restart, later_num, old_weight * early_num + new_weight * later_num),
            jnp.where(restart, later_den, old_weight * early_den + new_weight * later_den),
            jnp.where(restart, later_max, joint_max),
            early_count + later_count,
            jnp.maximum(early_reset, later_reset),
        )

    summaries = (
        lax.all_gather(sum_num[None], "seq", axis=0, tiled=True),
        lax.all_gather(sum_den[None], "seq", axis=0, tiled=True),
        lax.all_gather(sum_max[None], "seq", axis=0, tiled=True),
        lax.all_gather(count_row[None], "seq", axis=0, tiled=True),
        lax.all_gather(reset_flag[None], "seq", axis=0, tiled=True),
    )
    running = lax.associative_scan(merge_state, summaries)
    below_index = jnp.maximum(device_place - 1, 0)
    incoming = tuple(
        (
            jnp.where(
                device_place > 0,
                lax.dynamic_index_in_dim(column, below_index, 0, keepdims=False),
                blank_item,
            )
            for column, blank_item in zip(running, empty_state)
        )
    )
    in_num, in_den, in_max = (incoming[0], incoming[1], incoming[2])
    weighted, tail_back = jax.vjp(
        lambda numer_arg, denom_arg, top_arg, state_num, state_den, rate_arg: with_state(
            numer_arg, denom_arg, top_arg, state_num, state_den, in_max, carried_dev, rate_arg
        ),
        numerator,
        denominator,
        top_log,
        in_num,
        in_den,
        decay_rate,
    )
    gate_one = jax.nn.sigmoid(receptance)
    mixed = (gate_one * weighted).astype(jnp.bfloat16)
    resid = inputs + product(mixed, output_w)
    normed_two, unit_two, inverse_two = norm_forward(resid, vectors[7], vectors[8])
    rim_two = shifted(normed_two[tokens - 1 :], "seq", 1)
    previous_two = jnp.concatenate([rim_two, normed_two[:-1]], axis=0) * keep_rows
    chan_in_key = (vectors[9] * normed_two + (1.0 - vectors[9]) * previous_two).astype(jnp.bfloat16)
    chan_in_recept = (vectors[10] * normed_two + (1.0 - vectors[10]) * previous_two).astype(
        jnp.bfloat16
    )
    hidden_pre = product_back(chan_in_key, chan_key_w)
    squared = jnp.square(jax.nn.relu(hidden_pre)).astype(jnp.bfloat16)
    chan_value = product(squared, chan_value_w)
    gate_two = jax.nn.sigmoid(product(chan_in_recept, chan_recept_w))
    layer_out = (resid + gate_two * chan_value).astype(jnp.bfloat16)
    backward_rows = split_rows(lax.all_gather(owned_rows, "seq", axis=0, tiled=True), block_slot)
    (
        key_back,
        value_back,
        recept_back,
        output_back,
        chan_recept_back,
        chan_key_back,
        chan_value_back,
    ) = backward_rows
    out_grad = cotangent.astype(jnp.float32) * pad_mask.astype(jnp.float32)[:, None]
    grad_chan_value = (out_grad * gate_two).astype(jnp.bfloat16)
    grad_chan_gate = (out_grad * chan_value * gate_two * (1.0 - gate_two)).astype(jnp.bfloat16)
    grad_squared = product_back(grad_chan_value, chan_value_back)
    grad_hidden = (grad_squared * 2.0 * jax.nn.relu(hidden_pre)).astype(jnp.bfloat16)
    grad_chan_value_w = product_left(squared, grad_chan_value)
    grad_chan_key_w = product_left(grad_hidden, chan_in_key)
    grad_chan_recept_w = product_left(chan_in_recept, grad_chan_gate)
    grad_chan_in_key = product(grad_hidden, chan_key_back)
    grad_chan_in_recept = product_back(grad_chan_gate, chan_recept_back)
    grad_normed_two = vectors[9] * grad_chan_in_key + vectors[10] * grad_chan_in_recept
    grad_previous_two = (1.0 - vectors[9]) * grad_chan_in_key + (
        1.0 - vectors[10]
    ) * grad_chan_in_recept
    spread_two = normed_two - previous_two
    grad_chan_mix_key = jnp.sum(grad_chan_in_key * spread_two, axis=0)
    grad_chan_mix_recept = jnp.sum(grad_chan_in_recept * spread_two, axis=0)
    carried_two = grad_previous_two * keep_rows
    back_rim_two = shifted(carried_two[:1], "seq", -1)
    grad_normed_two = grad_normed_two + jnp.concatenate([carried_two[1:], back_rim_two], axis=0)
    grad_from_two, grad_gain_two, grad_bias_two = norm_backward(
        grad_normed_two, unit_two, inverse_two, vectors[7]
    )
    grad_resid = out_grad + grad_from_two
    grad_attn = grad_resid.astype(jnp.bfloat16)
    grad_output_w = product_left(mixed, grad_attn)
    grad_mixed = product_back(grad_attn, output_back)
    grad_weighted = grad_mixed * gate_one
    grad_recept = (grad_mixed * weighted * gate_one * (1.0 - gate_one)).astype(jnp.bfloat16)
    grad_numer, grad_denom, grad_top, grad_in_num, grad_in_den, grad_rate_tail = tail_back(
        grad_weighted
    )
    lift_scale = jnp.where(in_max > -1e29, jnp.exp(-in_max), 0.0)
    direct_num = grad_in_num * lift_scale
    direct_den = grad_in_den * lift_scale
    multiplier = (1.0 - reset_flag) * jnp.exp(-float(tokens) * decay_rate)
    blank_grad = (zeros_row, zeros_row, jnp.ones((features,), jnp.float32))

    def merge_grad(early, later):
        return (later[0] + later[2] * early[0], later[1] + later[2] * early[1], later[2] * early[2])

    terms_back = (
        lax.all_gather(direct_num[None], "seq", axis=0, tiled=True),
        lax.all_gather(direct_den[None], "seq", axis=0, tiled=True),
        lax.all_gather(multiplier[None], "seq", axis=0, tiled=True),
    )
    running_back = lax.associative_scan(merge_grad, tuple((column[::-1] for column in terms_back)))
    above_index = jnp.maximum(devices - 2 - device_place, 0)
    onward = tuple(
        (
            jnp.where(
                device_place < devices - 1,
                lax.dynamic_index_in_dim(column, above_index, 0, keepdims=False),
                blank_item,
            )
            for column, blank_item in zip(running_back, blank_grad)
        )
    )
    end_scale = jnp.exp(sum_max)
    out_num = onward[0] * end_scale
    out_den = onward[1] * end_scale
    out_max = (onward[0] * sum_num + onward[1] * sum_den) * end_scale
    grad_key_rows, grad_value_rows, grad_rate_head, grad_first = head_back(
        (grad_numer, grad_denom, grad_top, (out_num, out_den, out_max))
    )
    state_scale = jnp.exp(in_max)
    grad_rate_cross = (
        -float(tokens) * multiplier * (onward[0] * in_num + onward[1] * in_den) * state_scale
    )
    grad_decay = (grad_rate_tail + grad_rate_head + grad_rate_cross) * decay_rate
    grad_key_low = grad_key_rows.astype(jnp.bfloat16)
    grad_value_low = grad_value_rows.astype(jnp.bfloat16)
    grad_key_w = product_left(in_key, grad_key_low)
    grad_value_w = product_left(in_value, grad_value_low)
    grad_recept_w = product_left(in_recept, grad_recept)
    grad_in_key = product_back(grad_key_low, key_back)
    grad_in_value = product_back(grad_value_low, value_back)
    grad_in_recept = product_back(grad_recept, recept_back)
    grad_normed = (
        vectors[2] * grad_in_key + vectors[3] * grad_in_value + vectors[4] * grad_in_recept
    )
    grad_previous = (
        (1.0 - vectors[2]) * grad_in_key
        + (1.0 - vectors[3]) * grad_in_value
        + (1.0 - vectors[4]) * grad_in_recept
    )
    spread_one = normed - previous
    grad_mix_key = jnp.sum(grad_in_key * spread_one, axis=0)
    grad_mix_value = jnp.sum(grad_in_value * spread_one, axis=0)
    grad_mix_recept = jnp.sum(grad_in_recept * spread_one, axis=0)
    carried_one = grad_previous * keep_rows
    back_rim_one = shifted(carried_one[:1], "seq", -1)
    grad_normed = grad_normed + jnp.concatenate([carried_one[1:], back_rim_one], axis=0)
    grad_from_one, grad_gain_one, grad_bias_one = norm_backward(
        grad_normed, unit_one, inverse_one, vectors[0]
    )
    input_grad = grad_resid + grad_from_one
    row_grad = jnp.concatenate(
        [
            grad_key_w,
            grad_value_w,
            grad_recept_w,
            grad_output_w,
            grad_chan_recept_w,
            grad_chan_key_w,
            grad_chan_value_w,
        ],
        axis=0,
    )
    slot_total = masters.shape[0] * devices
    slot_grad = (
        jnp.zeros((slot_total, BLOCK_ROWS, EMBED_SIZE), jnp.float32)
        .at[block_slot]
        .set(row_grad.reshape(BLOCKS, BLOCK_ROWS, EMBED_SIZE))
    )
    owner_grad = lax.psum_scatter(slot_grad, "seq", scatter_dimension=0, tiled=True)
    stacked = jnp.stack(
        [
            grad_gain_one,
            grad_bias_one,
            grad_mix_key,
            grad_mix_value,
            grad_mix_recept,
            grad_decay,
            grad_first,
            grad_gain_two,
            grad_bias_two,
            grad_chan_mix_key,
            grad_chan_mix_recept,
        ]
    )
    vector_grad = lax.psum(stacked, "seq")
    new_one, new_two, new_master = adam_update(
        masters, moment_one, moment_two, owner_grad, MATRIX_RATE, WEIGHT_DECAY
    )
    vector_rates = jnp.array(VECTOR_RATE, jnp.float32)[:, None]
    vector_first, vector_second, vector_next = adam_update(
        vectors, vector_one, vector_two, vector_grad, vector_rates, 0.0
    )
    return (
        layer_out,
        input_grad,
        new_one,
        new_two,
        new_master,
        vector_first,
        vector_second,
        vector_next,
    )


def solution(mesh):
    placed = (
        P("seq", None),
        P("seq", None),
        P("seq"),
        P(),
        P("seq", None, None),
        P("seq", None, None),
        P("seq", None, None),
        P(),
        P(),
        P(),
        P(),
    )
    return jax.shard_map(
        body,
        mesh=mesh,
        in_specs=placed,
        out_specs=(
            P("seq", None),
            P("seq", None),
            P("seq", None, None),
            P("seq", None, None),
            P("seq", None, None),
            P(),
            P(),
            P(),
        ),
        check_vma=False,
    )
```

profile of v0, /device:TPU:0, one launch (start us, length us, event | category | flops | bytes accessed | tf_op | source)
XLA Modules:
  0.0 1396.7 jit_solution(9345689071777193525)
XLA Ops:
  7.2 2.7 convert_element_type.110
  12.6 2.3 collective-permute-start
  15.0 43.2 %all-reduce.55 = (f32[32]{0:T(128)S(1)}, f32[32]{0:T(128)S(1)}) all-reduce(f32[32]{0:T(128)S(1)} %dynamic-update-slice, f32[32]{0:T(128)S(1)} %dynamic-update-slice.1), channel_id=1, replica_groups=mesh['seq'=32] {'seq'}, use_global_device_ids=true, to_apply=%add.52 | all-reduce | flops 64 | bytes 512
  74.3 126.1 %all-gather.8.cloned.1.call-done = bf16[480,32,1024]{2,1,0:T(8,128)(2,1)} async-done(((bf16[15,32,1024]{2,1,0:T(8,128)(2,1)}), bf16[480,32,1024]{2,1,0:T(8,128)(2,1)}) %all-gather.8.cloned.1.call-update) | async-done | bytes 31457296 | tf_op jit(solution)/shard_map/all_gather | solution.py:195
  200.4 24.0 %gather_fusion = bf16[416,32,1024]{2,1,0:T(8,128)(2,1)} fusion(bf16[480,32,1024]{2,1,0:T(8,128)(2,1)} %all-gather.8.cloned.1.call-done, s32[1024]{0:T(1024)} %pad_clamp_fusion), kind=kCustom, calls=%fused_computation | custom fusion | bytes 54527616 | tf_op jit(solution)/shard_map/gather | solution.py:67
  224.4 7.0 fusion.185
  250.2 56.3 %while.107 = (s32[]{:T(128)}, f32[1024]{0:T(1024)S(1)}, f32[1024]{0:T(1024)S(1)}, f32[1024]{0:T(1024)S(1)}, f32[2,128,1024]{2,1,0:T(8,128)}, /*index=5*/f32[2,12...) while((s32[]{:T(128)}, f32[1024]{0:T(1024)S(1)}, ...), condition=%wide.region_10.11_spmd.clone.clone.clone.clone, body=%wide.region_4.10_spmd.clone.clone.clone.clone.sunk | while | flops 412256768 | bytes 58734408 | solution.py:138
  258.4 2.1 fusion.260
  270.9 3.0 bitcast_dynamic-update-slice_fusion.9
  273.9 1.9 multiply_dynamic-update-slice_fusion.2
  286.4 2.1 fusion.260
  299.0 3.0 bitcast_dynamic-update-slice_fusion.9
  302.1 1.9 multiply_dynamic-update-slice_fusion.2
  306.5 38.9 %all-gather.1 = f32[32768]{0:T(1024)S(1)} all-gather(f32[1024]{0:T(1024)S(1)} %get-tuple-element.1210), channel_id=3, replica_groups=mesh['seq'=32] {'seq'}, dimensions={0}, use_global_device_ids=true | all-gather | bytes 135168 | tf_op jit(solution)/shard_map/all_gather | solution.py:247
  346.2 37.0 %all-gather.2 = f32[32768]{0:T(1024)S(1)} all-gather(f32[1024]{0:T(1024)S(1)} %get-tuple-element.1212), channel_id=4, replica_groups=mesh['seq'=32] {'seq'}, dimensions={0}, use_global_device_ids=true | all-gather | bytes 135168 | tf_op jit(solution)/shard_map/all_gather | solution.py:248
  383.9 38.7 %all-gather = f32[32768]{0:T(1024)S(1)} all-gather(f32[1024]{0:T(1024)S(1)} %get-tuple-element.1208), channel_id=2, replica_groups=mesh['seq'=32] {'seq'}, dimensions={0}, use_global_device_ids=true | all-gather | bytes 135168 | tf_op jit(solution)/shard_map/all_gather | solution.py:249
  437.4 5.9 multiply_convert_fusion.4
  444.7 2.3 collective-permute-start.1
  447.0 9.8 fusion.184
  457.5 2.4 convolution_maximum_fusion
  459.9 7.4 fusion.119
  467.3 1.9 multiply_convert_fusion.2
  469.3 7.5 fusion.92
  476.8 4.0 fusion.193
  480.9 2.5 multiply_reduce_fusion.3
  484.7 39.2 %all-gather.4 = f32[32,1,1024]{2,1,0:T(1,128)S(1)} all-gather(f32[1,1,1024]{2,1,0:T(1,128)S(1)} %copy-done.119), channel_id=1, replica_groups=mesh['seq'=32] {'seq'}, dimensions={0}, use_global_device_ids=true | all-gather | bytes 135168 | tf_op jit(solution)/shard_map/all_gather | solution.py:346
  527.7 1.5 slice.777
  529.2 2.8 slice.788
  532.0 4.0 slice.778
  536.0 4.0 slice.782
  547.0 2.8 multiply_add_fusion.6
  549.8 3.3 multiply_reduce_fusion.6
  553.2 37.0 %all-gather.5 = f32[32,1,1024]{2,1,0:T(1,128)S(1)} all-gather(f32[1,1,1024]{2,1,0:T(1,128)S(1)} %get-tuple-element.2171), channel_id=1, replica_groups=mesh['seq'=32] {'seq'}, dimensions={0}, use_global_device_ids=true | all-gather | bytes 135168 | tf_op jit(solution)/shard_map/all_gather | solution.py:345
  591.5 38.3 %all-gather.3 = f32[32,1,1024]{2,1,0:T(1,128)S(1)} all-gather(f32[1,1,1024]{2,1,0:T(1,128)S(1)} %get-tuple-element.2172), channel_id=1, replica_groups=mesh['seq'=32] {'seq'}, dimensions={0}, use_global_device_ids=true | all-gather | bytes 135168 | tf_op jit(solution)/shard_map/all_gather | solution.py:344
  638.0 4.0 slice.817
  642.0 4.0 slice.776
  651.0 2.0 pad.208
  659.8 2.0 pad.220
  661.8 2.0 pad.210
  669.8 2.2 pad.211
  673.4 2.2 pad.222
  675.5 2.2 pad.212
  679.3 37.7 %while.106 = (s32[]{:T(128)}, f32[1024]{0:T(1024)S(1)}, f32[1024]{0:T(1024)S(1)}, f32[1024]{0:T(1024)S(1)}, f32[1024]{0:T(1024)S(1)}, /*index=5*/f32[1024]{0:T(1...) while((s32[]{:T(128)}, f32[1024]{0:T(1024)S(1)}, ...), condition=%wide.region_30.31_spmd.clone, body=%wide.region_20.30_spmd.clone.sunk | while | flops 410812672 | bytes 62910712 | solution.py:138
  688.9 2.8 fusion.249
  691.8 2.0 fusion.250
  707.7 2.8 fusion.249
  710.5 2.0 fusion.250
  717.0 4.0 convolution_dynamic-update-slice_fusion.6
  721.1 2.8 convolution_dynamic-update-slice_fusion.5
  724.0 3.1 convolution_dynamic-update-slice_fusion.4
  727.1 2.9 convolution_dynamic-update-slice_fusion.3
  730.0 2.8 convolution_dynamic-update-slice_fusion.2
  732.8 8.2 convolution_dynamic-update-slice_fusion.1
  741.0 8.2 convolution_dynamic-update-slice_fusion
  749.2 20.1 %broadcast_in_dim.463 = f32[480,32,1024]{2,1,0:T(8,128)} broadcast(f32[]{:T(128)} %constant.274.clone.1), dimensions={} | broadcast | bytes 62914564 | tf_op jit(solution)/shard_map/broadcast_in_dim | solution.py:413
  769.3 102.5 %scatter_fusion = f32[480,32,1024]{2,1,0:T(8,128)} fusion(f32[480,32,1024]{2,1,0:T(8,128)} %broadcast_in_dim.463, s32[416]{0:T(512)S(1)} %copy-done.114, f32[416,32,1024]{2,1,0:T(8,128)} %bitcast.659), kind=kCustom, calls=%fused_computation.1 | custom fusion | bytes 163579520 | tf_op jit(solution)/shard_map/scatter | solution.py:415
  871.9 1.5 copy-done.16
  873.5 2.5 fusion.195
  879.2 1.7 collective-permute-start.3
  882.5 2.2 fusion.111
  884.9 37.5 %psum.7 = f32[11,1024]{1,0:T(8,128)S(1)} all-reduce(f32[11,1024]{1,0:T(8,128)S(1)} %stack.47), channel_id=1, replica_groups=mesh['seq'=32] {'seq'}, use_global_device_ids=true, to_apply=%region_45.46 | all-reduce | flops 11264 | bytes 90112 | tf_op jit(solution)/shard_map/psum | solution.py:433
  923.2 2.9 fusion.110
  926.1 456.1 %reduce-scatter.4.cloned.1.call-done = f32[15,32,1024]{2,1,0:T(8,128)} async-done(((f32[480,32,1024]{2,1,0:T(8,128)}), f32[15,32,1024]{2,1,0:T(8,128)}) %reduce-scatter.4.cloned.1.call-update) | async-done | bytes 1966096
  1382.2 7.2 multiply_subtract_fusion.1
  (789 shorter events, 168.4 us)
Async XLA Ops:
  7.2 193.2 %all-gather.8.cloned.1.call-start = ((), (), s32[]{:S(2)}) async-start(), calls=%async_computation.1 | async-start | bytes 32440320 | tf_op jit(solution)/shard_map/all_gather | solution.py:195
  9.9 49.9 %copy-start.127 = (s32[416]{0:T(512)S(1)}, s32[416]{0:T(512)}, u32[]{:S(2)}) copy-start(s32[416]{0:T(512)} %param.23) | copy-start | bytes 4996
  9.9 59.1 %copy-start.128 = (s32[256]{0:T(256)S(1)}, s32[256]{0:T(256)}, u32[]{:S(2)}) copy-start(s32[256]{0:T(256)} %param.18) | copy-start | bytes 3076
  10.0 1372.3 %reduce-scatter.4.cloned.1.call-start = ((), (), s32[]{:S(2)}) async-start(), calls=%async_computation.2 | async-start | bytes 64880640
  10.2 64.0 %copy-start.89 = (f32[256]{0:T(256)}, f32[256]{0:T(256)S(1)}, u32[]{:S(2)}) copy-start(f32[256]{0:T(256)S(1)} %broadcast_multiply_fusion.6) | copy-start | bytes 3076
  10.5 63.7 %copy-start.111 = (f32[256]{0:T(256)}, f32[256]{0:T(256)S(1)}, u32[]{:S(2)}) copy-start(f32[256]{0:T(256)S(1)} %add_rsqrt_fusion.1) | copy-start | bytes 3076
  10.5 63.7 %copy-start.94 = (f32[1,1024]{1,0:T(1,128)}, f32[1,1024]{1,0:T(1,128)S(1)}, u32[]{:S(2)}) copy-start(f32[1,1024]{1,0:T(1,128)S(1)} %get-tuple-element.2125) | copy-start | bytes 12292
  10.5 63.7 %copy-start.96 = (f32[1,1024]{1,0:T(1,128)}, f32[1,1024]{1,0:T(1,128)S(1)}, u32[]{:S(2)}) copy-start(f32[1,1024]{1,0:T(1,128)S(1)} %get-tuple-element.2127) | copy-start | bytes 12292
  10.6 63.7 %copy-start.98 = (f32[1,1024]{1,0:T(1,128)}, f32[1,1024]{1,0:T(1,128)S(1)}, u32[]{:S(2)}) copy-start(f32[1,1024]{1,0:T(1,128)S(1)} %get-tuple-element.2123) | copy-start | bytes 12292
  10.6 63.7 %copy-start.100 = (f32[1,1024]{1,0:T(1,128)}, f32[1,1024]{1,0:T(1,128)S(1)}, u32[]{:S(2)}) copy-start(f32[1,1024]{1,0:T(1,128)S(1)} %get-tuple-element.2124) | copy-start | bytes 12292
  10.9 63.4 %copy-start.19 = (f32[256,1024]{1,0:T(8,128)}, f32[256,1024]{1,0:T(8,128)S(1)}, u32[]{:S(2)}) copy-start(f32[256,1024]{1,0:T(8,128)S(1)} %fusion.106) | copy-start | bytes 3145732
  11.3 48.4 %copy-start.122 = (f32[256]{0:T(256)}, f32[256]{0:T(256)S(1)}, u32[]{:S(2)}) copy-start(f32[256]{0:T(256)S(1)} %convert_reduce_fusion.3) | copy-start | bytes 3076
  11.9 62.4 %copy-start.91 = (f32[256]{0:T(256)}, f32[256]{0:T(256)S(1)}, u32[]{:S(2)}) copy-start(f32[256]{0:T(256)S(1)} %get-tuple-element.2174) | copy-start | bytes 3076
  12.6 60.9 %collective-permute-start = (f32[1,1024]{1,0:T(1,128)S(1)}, f32[1,1024]{1,0:T(1,128)S(1)}, u32[]{:S(2)}, u32[]{:S(2)}) collective-permute-start(f32[1,1024]{1,0:T(1,128)S(1)} %slice.864), channel_id=1, source_target_pairs={{0,1},{1,2},{2,3},{3,4},{4,5},{5,6},{6,7},{7,8},{8,9},{9,10},{10,1... | collective-permute-start | bytes 12296 | tf_op jit(solution)/shard_map/ppermute | solution.py:29
  60.5 164.0 %copy-start.39 = (bf16[2,128,1024]{2,1,0:T(8,128)(2,1)}, bf16[2,128,1024]{2,1,0:T(8,128)(2,1)S(1)}, u32[]{:S(2)}) copy-start(bf16[2,128,1024]{2,1,0:T(8,128)(2,1)S(1)} %fusion.186) | copy-start | bytes 1572868
  73.6 150.8 %copy-start.105 = (f32[1,1024]{1,0:T(1,128)}, f32[1,1024]{1,0:T(1,128)S(1)}, u32[]{:S(2)}) copy-start(f32[1,1024]{1,0:T(1,128)S(1)} %collective-permute-done) | copy-start | bytes 12292
  74.3 157.2 %copy-start.44 = (bf16[256,1024]{1,0:T(8,128)(2,1)}, bf16[256,1024]{1,0:T(8,128)(2,1)S(1)}, u32[]{:S(2)}) copy-start(bf16[256,1024]{1,0:T(8,128)(2,1)S(1)} %get-tuple-element.2093) | copy-start | bytes 1572868
  74.3 157.9 %copy-start.46 = (bf16[256,1024]{1,0:T(8,128)(2,1)}, bf16[256,1024]{1,0:T(8,128)(2,1)S(1)}, u32[]{:S(2)}) copy-start(bf16[256,1024]{1,0:T(8,128)(2,1)S(1)} %get-tuple-element.2094) | copy-start | bytes 1572868
  250.2 6.7 copy-start.87
  278.3 6.6 copy-start.87
  306.4 117.0 %copy-start.148 = (pred[2]{0:T(512)(128)(4,1)}, pred[2]{0:T(512)(128)(4,1)S(1)}, u32[]{:S(2)}) copy-start(pred[2]{0:T(512)(128)(4,1)S(1)} %get-tuple-element.2950) | copy-start | bytes 10
  306.4 116.3 %copy-start.140 = (pred[16]{0:T(512)(128)(4,1)S(1)}, pred[16]{0:T(512)(128)(4,1)}, u32[]{:S(2)}) copy-start(pred[16]{0:T(512)(128)(4,1)} %compare_bitcast_fusion.5) | copy-start | bytes 52
  306.4 116.3 %copy-start.142 = (f32[16,1]{0,1:T(1,128)S(1)}, f32[16,1]{0,1:T(1,128)}, u32[]{:S(2)}) copy-start(f32[16,1]{0,1:T(1,128)} %copy-done.141) | copy-start | bytes 196
  306.4 116.7 %copy-start.135 = (pred[8]{0:T(512)(128)(4,1)S(1)}, pred[8]{0:T(512)(128)(4,1)}, u32[]{:S(2)}) copy-start(pred[8]{0:T(512)(128)(4,1)} %compare_bitcast_fusion.3) | copy-start | bytes 28
  306.4 116.7 %copy-start.139 = (f32[8,1]{0,1:T(1,128)S(1)}, f32[8,1]{0,1:T(1,128)}, u32[]{:S(2)}) copy-start(f32[8,1]{0,1:T(1,128)} %copy-done.138) | copy-start | bytes 100
  306.5 117.0 %copy-start.132 = (pred[4]{0:T(512)(128)(4,1)S(1)}, pred[4]{0:T(512)(128)(4,1)}, u32[]{:S(2)}) copy-start(pred[4]{0:T(512)(128)(4,1)} %compare_bitcast_fusion.1) | copy-start | bytes 16
  306.5 117.0 %copy-start.137 = (f32[4,1]{0,1:T(1,128)S(1)}, f32[4,1]{0,1:T(1,128)}, u32[]{:S(2)}) copy-start(f32[4,1]{0,1:T(1,128)} %copy-done.136) | copy-start | bytes 52
  345.4 78.2 %copy-start.69 = (f32[32768]{0:T(1024)}, f32[32768]{0:T(1024)S(1)}, u32[]{:S(2)}) copy-start(f32[32768]{0:T(1024)S(1)} %all-gather.1) | copy-start | bytes 393220
  345.4 78.4 %copy-start.131 = (pred[2]{0:T(512)(128)(4,1)S(1)}, pred[2]{0:T(512)(128)(4,1)}, u32[]{:S(2)}) copy-start(pred[2]{0:T(512)(128)(4,1)} %compare_bitcast_fusion) | copy-start | bytes 10
  345.5 78.4 %copy-start.134 = (f32[2,1]{0,1:T(1,128)S(1)}, f32[2,1]{0,1:T(1,128)}, u32[]{:S(2)}) copy-start(f32[2,1]{0,1:T(1,128)} %copy-done.133) | copy-start | bytes 28
  383.2 43.6 %copy-start.70 = (f32[32768]{0:T(1024)}, f32[32768]{0:T(1024)S(1)}, u32[]{:S(2)}) copy-start(f32[32768]{0:T(1024)S(1)} %all-gather.2) | copy-start | bytes 393220
  383.2 43.7 %copy-start.126 = (pred[3]{0:T(512)(128)(4,1)S(1)}, pred[3]{0:T(512)(128)(4,1)}, u32[]{:S(2)}) copy-start(pred[3]{0:T(512)(128)(4,1)} %compare_bitcast_fusion.2) | copy-start | bytes 13
  383.2 43.7 %copy-start.130 = (f32[3,1]{0,1:T(1,128)S(1)}, f32[3,1]{0,1:T(1,128)}, u32[]{:S(2)}) copy-start(f32[3,1]{0,1:T(1,128)} %slice.709) | copy-start | bytes 40
  427.4 10.0 copy-start.11
  427.4 10.0 copy-start.20
  437.4 112.4 %copy-start.79 = (f32[1,1024]{1,0:T(1,128)}, f32[1,1024]{1,0:T(1,128)S(1)}, u32[]{:S(2)}) copy-start(f32[1,1024]{1,0:T(1,128)S(1)} %get-tuple-element.2181) | copy-start | bytes 12292
  437.4 112.4 %copy-start.81 = (f32[1,1024]{1,0:T(1,128)}, f32[1,1024]{1,0:T(1,128)S(1)}, u32[]{:S(2)}) copy-start(f32[1,1024]{1,0:T(1,128)S(1)} %get-tuple-element.2182) | copy-start | bytes 12292
  437.4 5.9 copy-start.17
  444.7 12.1 copy-start.92
  444.7 12.1 copy-start.102
  444.7 12.1 copy-start.103
  444.7 12.1 copy-start.109
  444.7 12.1 copy-start.110
  444.7 12.1 collective-permute-start.1
  457.5 9.8 copy-start.57
  459.9 9.4 copy-start.47
  459.9 7.4 copy-start.43
  459.9 7.4 copy-start.74
  459.9 7.4 copy-start.124
  469.3 7.5 copy-start.72
  469.3 11.6 copy-start.64
  483.4 56.8 %collective-permute-start.2 = (f32[1,1024]{1,0:T(1,128)S(1)}, f32[1,1024]{1,0:T(1,128)S(1)}, u32[]{:S(2)}, u32[]{:S(2)}) collective-permute-start(f32[1,1024]{1,0:T(1,128)S(1)} %slice.921), channel_id=1, source_target_pairs={{1,0},{2,1},{3,2},{4,3},{5,4},{6,5},{7,6},{8,7},{9,8},{10,9},{11,1... | collective-permute-start | bytes 12296 | tf_op jit(solution)/shard_map/ppermute | solution.py:29
  553.2 78.7 %copy-start.76 = (f32[16,1024]{1,0:T(8,128)S(1)}, f32[16,1024]{1,0:T(8,128)}, u32[]{:S(2)}) copy-start(f32[16,1024]{1,0:T(8,128)} %slice.782) | copy-start | bytes 196612
  637.3 42.0 %copy-start.2 = (f32[2,128,1024]{2,1,0:T(8,128)S(1)}, f32[2,128,1024]{2,1,0:T(8,128)}, u32[]{:S(2)}) copy-start(f32[2,128,1024]{2,1,0:T(8,128)} %get-tuple-element.2975) | copy-start | bytes 3145732
  637.3 42.0 %copy-start.5 = (f32[2,128,1024]{2,1,0:T(8,128)S(1)}, f32[2,128,1024]{2,1,0:T(8,128)}, u32[]{:S(2)}) copy-start(f32[2,128,1024]{2,1,0:T(8,128)} %get-tuple-element.2966) | copy-start | bytes 3145732
  732.8 8.2 copy-start.48
  732.8 8.2 copy-start.73
  749.2 20.1 %copy-start.114 = (s32[416]{0:T(512)S(1)}, s32[416]{0:T(512)}, u32[]{:S(2)}) copy-start(s32[416]{0:T(512)} %copy-done.113) | copy-start | bytes 4996
  879.2 3.2 collective-permute-start.3
  882.5 40.0 %copy-start.78 = (f32[11,1024]{1,0:T(8,128)S(1)}, f32[11,1024]{1,0:T(8,128)}, u32[]{:S(2)}) copy-start(f32[11,1024]{1,0:T(8,128)} %param.24) | copy-start | bytes 135172
  882.5 40.0 %copy-start.83 = (f32[11,1024]{1,0:T(8,128)S(1)}, f32[11,1024]{1,0:T(8,128)}, u32[]{:S(2)}) copy-start(f32[11,1024]{1,0:T(8,128)} %param.26) | copy-start | bytes 135172
  882.5 40.0 %copy-start.84 = (f32[11,1024]{1,0:T(8,128)S(1)}, f32[11,1024]{1,0:T(8,128)}, u32[]{:S(2)}) copy-start(f32[11,1024]{1,0:T(8,128)} %param.25) | copy-start | bytes 135172
  882.5 40.0 %copy-start.143 = (f32[11]{0:T(128)S(1)}, f32[11]{0:T(128)}, u32[]{:S(2)}) copy-start(f32[11]{0:T(128)} %constant.304.clone) | copy-start | bytes 136
  882.5 40.7 %copy-start.25 = (f32[256,1024]{1,0:T(8,128)S(1)}, f32[256,1024]{1,0:T(8,128)}, u32[]{:S(2)}) copy-start(f32[256,1024]{1,0:T(8,128)} %copy-done.23) | copy-start | bytes 3145732
  (121 other events, 304.9 us)
Sparse Core Ops, SparseCore 0:
  11.5 188.8 all-gather.7
  872.0 510.1 reduce-scatter.3
where the time goes:
time: 1410 us; the launch traced here: 1400 us
  waiting for transfers between devices  584 us (41%)
  local copies, waits for them, and re-layouts  310 us (22%)
  blocking collectives  310 us (22%)
  other arithmetic  86 us (6%)
  matrix products  79 us (6%)
  between operations  18.8 us (1%)
    unnamed x3, waiting for transfers between devices  456 us
    all_gather x1, waiting for transfers between devices, body(): lax.all_gather(owned_rows, 'seq', axis=0, tiled=True)  126 us
    scatter x1, local copies, waits for them, and re-layouts, body(): slot_grad = jnp.zeros((slot_total, BLOCK_ROWS, EMBED_SIZE), jnp.float32)....  103 us
    unnamed x1, blocking collectives  43.2 us
    all_gather x1, blocking collectives, body(): lax.all_gather(multiplier[None], 'seq', axis=0, tiled=True)  39.2 us
    all_gather x1, blocking collectives, body(): lax.all_gather(sum_num[None], 'seq', axis=0, tiled=True)  38.9 us
    all_gather x1, blocking collectives, body(): lax.all_gather(sum_max[None], 'seq', axis=0, tiled=True)  38.7 us
    all_gather x1, blocking collectives, body(): lax.all_gather(direct_num[None], 'seq', axis=0, tiled=True)  38.3 us
  transfers between devices with their start and end apart: 6, of which 3 were waited for; matrix products, arithmetic and copies ran while one was open for 4% of the time, Pallas kernels for 0%

commit v1 on v0

--- a/solution.py
+++ b/solution.py
@@ -1,8 +1,11 @@
+import functools
 import math
 
 import jax
 import jax.numpy as jnp
 from jax import lax
+from jax.experimental import pallas as pl
+from jax.experimental.pallas import tpu as pltpu
 from jax.sharding import PartitionSpec as P
 
 EMBED_SIZE = 1024
@@ -11,6 +14,482 @@
 ROWS_ALL = 13312
 BLOCKS = 416
 STEP = 10
+GRID_DEVICES = 32
+MESH = pl.DeviceIdType.MESH
+
+def grid_place():
+    me = lax.axis_index("seq")
+    return me, lax.rem(me, 2), lax.rem(me // 2, 2), lax.rem(me // 4, 2), me // 8
+
+def spans(slots):
+    third = -(-slots // 3)
+    cuts = [0, third, min(2 * third, slots), slots]
+    return [(cuts[i], cuts[i + 1] - cuts[i]) for i in range(3)]
+
+def gather_kernel(slots, own_ref, out_ref, *scratch):
+    send_sem, recv_sem, sib_send, sib_recv, own_sem = scratch
+    me, core, x, y, z = grid_place()
+    sib = me + 1 - 2 * core
+    x_peer = me + 2 - 4 * x
+    y_peer = me + 4 - 8 * y
+    up = me + 8
+    down = me - 8
+    bar = pltpu.get_barrier_semaphore()
+    pl.semaphore_signal(bar, inc=1, device_id=(sib,), device_id_type=MESH)
+    pl.semaphore_signal(bar, inc=1, device_id=(x_peer,), device_id_type=MESH)
+    pl.semaphore_signal(bar, inc=1, device_id=(y_peer,), device_id_type=MESH)
+    @pl.when(z < 3)
+    def _():
+        pl.semaphore_signal(bar, inc=1, device_id=(up,), device_id_type=MESH)
+    @pl.when(z > 0)
+    def _():
+        pl.semaphore_signal(bar, inc=1, device_id=(down,), device_id_type=MESH)
+    pl.semaphore_wait(bar, 4 + jnp.where((z > 0) & (z < 3), 1, 0))
+    span = spans(slots)
+    targets = (x_peer, y_peer, up, down)
+
+    def chip(cx, cy, cz):
+        return (cz * 2 + cy) * 2 + cx
+
+    def view(cx, cy, cz, color, c=None):
+        dev = chip(cx, cy, cz) * 2 + (core if c is None else c)
+        lo, n = span[color]
+        return out_ref.at[dev, pl.ds(lo, n)]
+
+    def send(cx, cy, cz, color, way, own=False):
+        lo, n = span[color]
+        src = own_ref.at[pl.ds(lo, n)] if own else view(cx, cy, cz, color)
+        idx = chip(cx, cy, cz)
+        return pltpu.make_async_remote_copy(src_ref=src, dst_ref=view(cx, cy, cz, color),
+            send_sem=send_sem.at[idx, color, way], recv_sem=recv_sem.at[idx, color],
+            device_id=(targets[way],), device_id_type=MESH)
+
+    def send_sib(cx, cy, cz, color, own=False):
+        lo, n = span[color]
+        src = own_ref.at[pl.ds(lo, n)] if own else view(cx, cy, cz, color)
+        idx = chip(cx, cy, cz)
+        return pltpu.make_async_remote_copy(src_ref=src, dst_ref=view(cx, cy, cz, color),
+            send_sem=sib_send.at[idx, color], recv_sem=sib_recv.at[idx, color],
+            device_id=(sib,), device_id_type=MESH)
+
+    x2, y2 = 1 - x, 1 - y
+    pending = []
+
+    def go(copy, cond=None):
+        if cond is None:
+            copy.start()
+        else:
+            @pl.when(cond)
+            def _():
+                copy.start()
+        pending.append((copy, cond))
+
+    zup, zdown = z < 3, z > 0
+    own_copies = []
+    for color in range(3):
+        lo, n = span[color]
+        cp = pltpu.make_async_copy(own_ref.at[pl.ds(lo, n)], view(x, y, z, color), own_sem.at[color])
+        cp.start()
+        own_copies.append(cp)
+    order = {0: (0, 2, 1), 1: (1, 2, 0)}
+    for color in (0, 1, 2):
+        go(send(x, y, z, color, 2, True), zup)
+        go(send(x, y, z, color, 3, True), zdown)
+    for color, way in ((0, 0), (1, 1), (2, 0), (2, 1), (0, 1), (1, 0)):
+        go(send(x, y, z, color, way, True))
+    for color in range(3):
+        go(send_sib(x, y, z, color, True))
+
+    def arrive(cx, cy, cz, color):
+        send(cx, cy, cz, color, 0).wait_recv()
+
+    def sibling(cx, cy, cz, color):
+        go(send_sib(cx, cy, cz, color))
+
+    is0, is1 = core == 0, core == 1
+    px = jnp.where(is0, x2, x)
+    py = jnp.where(is0, y, y2)
+    qx = jnp.where(is0, x, x2)
+    qy = jnp.where(is0, y2, y)
+    first = lambda cx, cy, cz: (go(send(cx, cy, cz, 2, 0), is0), go(send(cx, cy, cz, 2, 1), is1))
+    last = lambda cx, cy, cz: (go(send(cx, cy, cz, 2, 1), is0), go(send(cx, cy, cz, 2, 0), is1))
+
+    arrive(x2, y, z, 0)
+    go(send(x2, y, z, 0, 2), zup)
+    go(send(x2, y, z, 0, 3), zdown)
+    go(send(x2, y, z, 0, 1))
+    sibling(x2, y, z, 0)
+    arrive(x, y2, z, 1)
+    go(send(x, y2, z, 1, 2), zup)
+    go(send(x, y2, z, 1, 3), zdown)
+    go(send(x, y2, z, 1, 0))
+    sibling(x, y2, z, 1)
+    arrive(px, py, z, 2)
+    last(px, py, z)
+    sibling(px, py, z, 2)
+
+    for dist in (1, 2, 3):
+        sides = []
+        for sign, fwd, guard_f in ((1, 3, zdown), (-1, 2, zup)):
+            q = z + sign * dist
+            have = (q >= 0) & (q < 4)
+            sides.append((q, fwd, have, guard_f))
+        for which in ("c", "a", "b", "a2", "b2"):
+            for q, fwd, have, gf in sides:
+                @pl.when(have)
+                def _(q=q, fwd=fwd, gf=gf, which=which):
+                    if which == "c":
+                        arrive(x, y, q, 2)
+                        cp = send(x, y, q, 2, fwd)
+                        pl.when(gf)(lambda: cp.start())
+                        for w in (0, 1):
+                            send(x, y, q, 2, w).start()
+                        send_sib(x, y, q, 2).start()
+                    else:
+                        color = 0 if which[0] == "a" else 1
+                        cx, cy = {"a": (x, y), "b": (x, y), "a2": (x2, y), "b2": (x, y2)}[which]
+                        arrive(cx, cy, q, color)
+                        cp = send(cx, cy, q, color, fwd)
+                        pl.when(gf)(lambda: cp.start())
+                        send(cx, cy, q, color, 1 if color == 0 else 0).start()
+                        send_sib(cx, cy, q, color).start()
+        for q, fwd, have, gf in sides:
+            @pl.when(have)
+            def _(q=q):
+                arrive(px, py, q, 2)
+                pl.when(is0)(lambda: send(px, py, q, 2, 1).start())
+                pl.when(is1)(lambda: send(px, py, q, 2, 0).start())
+                send_sib(px, py, q, 2).start()
+        if dist == 1:
+            tail_list = [(z, None)]
+        else:
+            tail_list = []
+        def terminal(q):
+            for cx, cy, color in ((x, y2, 0), (x2, y2, 0), (x2, y, 1), (x2, y2, 1), (qx, qy, 2), (x2, y2, 2)):
+                arrive(cx, cy, q, color)
+                send_sib(cx, cy, q, color).start()
+        if dist == 1:
+            terminal(z)
+        else:
+            for sign in (1, -1):
+                q = z + sign * (dist - 1)
+                pl.when((q >= 0) & (q < 4))(lambda q=q: terminal(q))
+        if dist == 3:
+            for sign in (1, -1):
+                q = z + sign * 3
+                pl.when((q >= 0) & (q < 4))(lambda q=q: terminal(q))
+    for cp in own_copies:
+        cp.wait()
+    for color in range(3):
+        pl.when(zup)(lambda color=color: send(x, y, z, color, 2).wait_send())
+        pl.when(zdown)(lambda color=color: send(x, y, z, color, 3).wait_send())
+        for w in (0, 1):
+            send(x, y, z, color, w).wait_send()
+    for cx, cy, color, w in ((x2, y, 0, 1), (x, y2, 1, 0)):
+        pl.when(zup)(lambda: send(cx, cy, z, color, 2).wait_send())
+        pl.when(zdown)(lambda: send(cx, cy, z, color, 3).wait_send())
+        send(cx, cy, z, color, w).wait_send()
+    pl.when(is0)(lambda: send(px, py, z, 2, 1).wait_send())
+    pl.when(is1)(lambda: send(px, py, z, 2, 0).wait_send())
+    for dist in (1, 2, 3):
+        for sign, fwd, gf in ((1, 3, zdown), (-1, 2, zup)):
+            q = z + sign * dist
+            @pl.when((q >= 0) & (q < 4))
+            def _(q=q, fwd=fwd, gf=gf):
+                for cx, cy, color in ((x, y, 2), (x, y, 0), (x, y, 1), (x2, y, 0), (x, y2, 1)):
+                    pl.when(gf)(lambda: send(cx, cy, q, color, fwd).wait_send())
+                    ways = (0, 1) if color == 2 else ((1,) if color == 0 else (0,))
+                    for w in ways:
+                        send(cx, cy, q, color, w).wait_send()
+                pl.when(is0)(lambda: send(px, py, q, 2, 1).wait_send())
+                pl.when(is1)(lambda: send(px, py, q, 2, 0).wait_send())
+    for cz in range(4):
+        for cy in range(2):
+            for cx in range(2):
+                for color in range(3):
+                    cp = send_sib(cx, cy, cz, color)
+                    cp.wait_send()
+                    cp.wait_recv()
+
+def gather_blocks(owned, cid=1):
+    slots = owned.shape[0]
+    return pl.pallas_call(
+        functools.partial(gather_kernel, slots),
+        out_shape=jax.ShapeDtypeStruct((32,) + owned.shape, owned.dtype),
+        in_specs=[pl.BlockSpec(memory_space=pl.ANY)],
+        out_specs=pl.BlockSpec(memory_space=pl.ANY),
+        scratch_shapes=[
+            pltpu.SemaphoreType.DMA((16, 3, 4)),
+            pltpu.SemaphoreType.DMA((16, 3)),
+            pltpu.SemaphoreType.DMA((16, 3)),
+            pltpu.SemaphoreType.DMA((16, 3)),
+            pltpu.SemaphoreType.DMA((3,)),
+        ],
+        compiler_params=pltpu.CompilerParams(collective_id=cid, has_side_effects=True),
+        name="gather_blocks",
+    )(owned)
+
+def scatter_kernel(slots, part_ref, out_ref, acc, sib, xin, yin, zin, load_sem, sib_send, sib_recv, send_sem, xsem, ysem, zsem):
+    me, core, x, y, z = grid_place()
+    sibling = me + 1 - 2 * core
+    x_peer = me + 2 - 4 * x
+    y_peer = me + 4 - 8 * y
+    up, down = me + 8, me - 8
+    zup, zdown = z < 3, z > 0
+    bar = pltpu.get_barrier_semaphore()
+    for peer in (sibling, x_peer, y_peer):
+        pl.semaphore_signal(bar, inc=1, device_id=(peer,), device_id_type=MESH)
+    @pl.when(zup)
+    def _():
+        pl.semaphore_signal(bar, inc=1, device_id=(up,), device_id_type=MESH)
+    @pl.when(zdown)
+    def _():
+        pl.semaphore_signal(bar, inc=1, device_id=(down,), device_id_type=MESH)
+    span = spans(slots)
+    x2, y2 = 1 - x, 1 - y
+    is0, is1 = core == 0, core == 1
+    px, py = jnp.where(is0, x2, x), jnp.where(is0, y, y2)
+    qx, qy = jnp.where(is0, x, x2), jnp.where(is0, y2, y)
+
+    def load(chip):
+        return pltpu.make_async_copy(part_ref.at[2 * chip + core], acc.at[chip], load_sem.at[chip])
+
+    def give(chip):
+        return pltpu.make_async_remote_copy(src_ref=part_ref.at[2 * chip + 1 - core], dst_ref=sib.at[chip],
+            send_sem=sib_send.at[chip], recv_sem=sib_recv.at[chip], device_id=(sibling,), device_id_type=MESH)
+
+    levels = []
+    for dist in (3, 2, 1):
+        for sign in (1, -1):
+            q = z + sign * dist
+            levels.append((dist, sign, q, (q >= 0) & (q < 4)))
+    for _, _, q, have in levels:
+        @pl.when(have)
+        def _(q=q):
+            for i in range(4):
+                load(4 * q + i).start()
+    for i in range(4):
+        load(4 * z + i).start()
+    pl.semaphore_wait(bar, 4 + jnp.where(zup & zdown, 1, 0))
+    for _, _, q, have in levels:
+        @pl.when(have)
+        def _(q=q):
+            for i in range(4):
+                give(4 * q + i).start()
+    for i in range(4):
+        give(4 * z + i).start()
+
+    def ready(q):
+        for i in range(4):
+            chip = 4 * q + i
+            load(chip).wait()
+            give(chip).wait_recv()
+            def step(s, _, chip=chip):
+                total = acc[chip, s].astype(jnp.float32) + sib[chip, s].astype(jnp.float32)
+                acc[chip, s] = total.astype(acc.dtype)
+                return 0
+            lax.fori_loop(0, slots, step, 0)
+
+    def chip_of(cx, cy, cz):
+        return (cz * 2 + cy) * 2 + cx
+
+    def out_copy(cx, cy, cz, color, target, buf, index, sem):
+        lo, n = span[color]
+        chip = chip_of(cx, cy, cz)
+        return pltpu.make_async_remote_copy(src_ref=acc.at[chip, pl.ds(lo, n)], dst_ref=buf.at[index, pl.ds(0, n)],
+            send_sem=send_sem.at[chip, color], recv_sem=sem.at[index], device_id=(target,), device_id_type=MESH)
+
+    def arrived(buf, index, sem, color):
+        lo, n = span[color]
+        pltpu.make_async_remote_copy(src_ref=acc.at[0, pl.ds(lo, n)], dst_ref=buf.at[index, pl.ds(0, n)],
+            send_sem=send_sem.at[0, color], recv_sem=sem.at[index], device_id=(sibling,), device_id_type=MESH).wait_recv()
+
+    def add(cx, cy, cz, color, pieces):
+        lo, n = span[color]
+        chip = chip_of(cx, cy, cz)
+        for buf, index, sem in pieces:
+            arrived(buf, index, sem, color)
+        def step(s, _):
+            total = acc[chip, lo + s].astype(jnp.float32)
+            for buf, index, _sem in pieces:
+                total = total + buf[index, s].astype(jnp.float32)
+            acc[chip, lo + s] = total.astype(acc.dtype)
+            return 0
+        lax.fori_loop(0, n, step, 0)
+
+    def X(i): return (xin, i, xsem)
+    def Y(i): return (yin, i, ysem)
+    def Z(i): return (zin, i, zsem)
+
+    def terminal(q):
+        for i, cx in enumerate((x, x2)):
+            out_copy(cx, y2, q, 0, y_peer, yin, 2 * q + i, ysem).start()
+        for i, cy in enumerate((y, y2)):
+            out_copy(x2, cy, q, 1, x_peer, xin, 2 * q + i, xsem).start()
+        @pl.when(is0)
+        def _():
+            for i, cx in enumerate((x, x2)):
+                out_copy(cx, y2, q, 2, y_peer, yin, 8 + 2 * q + i, ysem).start()
+        @pl.when(is1)
+        def _():
+            for i, cy in enumerate((y, y2)):
+                out_copy(x2, cy, q, 2, x_peer, xin, 8 + 2 * q + i, xsem).start()
+
+    def plane_two(q):
+        @pl.when(is0)
+        def _():
+            add(x2, y, q, 2, [Y(8 + 2 * q + 1)])
+            out_copy(x2, y, q, 2, x_peer, xin, 8 + 2 * q, xsem).start()
+        @pl.when(is1)
+        def _():
+            add(x, y2, q, 2, [X(8 + 2 * q + 1)])
+            out_copy(x, y2, q, 2, y_peer, yin, 8 + 2 * q, ysem).start()
+
+    def column(q, sign, dist):
+        target = up if sign == 1 else down
+        more = zdown if sign == 1 else zup
+        at_target = dist == 1
+        base_out = (20 if (at_target and sign == 1) else 5 * q)
+        kinds = (
+            (0, x, y, 2, [X(8 + 2 * q), Y(8 + 2 * q)]),
+            (1, x, y, 0, [Y(2 * q)]),
+            (2, x, y, 1, [X(2 * q)]),
+            (3, x2, y, 0, [Y(2 * q + 1)]),
+            (4, x, y2, 1, [X(2 * q + 1)]),
+        )
+        for k, cx, cy, color, pieces in (kinds[1], kinds[2], kinds[3], kinds[4], kinds[0]):
+            @pl.when(more)
+            def _():
+                add(cx, cy, q, color, pieces + [Z(5 * q + k)])
+            @pl.when(jnp.logical_not(more))
+            def _():
+                add(cx, cy, q, color, pieces)
+            out_copy(cx, cy, q, color, target, zin, base_out + k, zsem).start()
+
+    def run(dist, work):
+        for d, sign, q, have in levels:
+            if d == dist:
+                pl.when(have)(functools.partial(work, q, sign, dist))
+
+    def begin(q, sign, dist):
+        ready(q)
+        terminal(q)
+
+    def middle(q, sign, dist):
+        plane_two(q)
+    run(3, begin)
+    run(3, middle)
+    run(2, begin)
+    run(3, column)
+    run(2, middle)
+    run(1, begin)
+    run(2, column)
+    run(1, middle)
+    ready(z)
+    terminal(z)
+    run(1, column)
+    plane_two(z)
+
+    def own(k, cx, cy, color, pieces):
+        @pl.when(zup & zdown)
+        def _():
+            add(cx, cy, z, color, pieces + [Z(5 * z + k), Z(20 + k)])
+        @pl.when(zup & jnp.logical_not(zdown))
+        def _():
+            add(cx, cy, z, color, pieces + [Z(5 * z + k)])
+        @pl.when(zdown & jnp.logical_not(zup))
+        def _():
+            add(cx, cy, z, color, pieces + [Z(20 + k)])
+    own(3, x2, y, 0, [Y(2 * z + 1)])
+    out_copy(x2, y, z, 0, x_peer, xin, 16, xsem).start()
+    own(4, x, y2, 1, [X(2 * z + 1)])
+    out_copy(x, y2, z, 1, y_peer, yin, 16, ysem).start()
+    own(0, x, y, 2, [X(8 + 2 * z), Y(8 + 2 * z)])
+    own(1, x, y, 0, [Y(2 * z), X(16)])
+    own(2, x, y, 1, [X(2 * z), Y(16)])
+    pltpu.sync_copy(acc.at[chip_of(x, y, z)], out_ref)
+    for chip in range(16):
+        give(chip).wait_send()
+        for color in range(3):
+            @pl.when(chip != chip_of(x, y, z))
+            def _():
+                lo, n = span[color]
+                pltpu.make_async_remote_copy(src_ref=acc.at[chip, pl.ds(lo, n)], dst_ref=xin.at[0, pl.ds(0, n)],
+                    send_sem=send_sem.at[chip, color], recv_sem=xsem.at[0], device_id=(sibling,), device_id_type=MESH).wait_send()
+
+def scatter_blocks(part, cid=2):
+    _, slots, rows, feats = part.shape
+    most = max(n for _, n in spans(slots))
+    chunk = (most, rows, feats)
+    dt = part.dtype
+    return pl.pallas_call(
+        functools.partial(scatter_kernel, slots),
+        out_shape=jax.ShapeDtypeStruct(part.shape[1:], dt),
+        in_specs=[pl.BlockSpec(memory_space=pl.ANY)],
+        out_specs=pl.BlockSpec(memory_space=pl.ANY),
+        scratch_shapes=[
+            pltpu.VMEM((16, slots, rows, feats), dt),
+            pltpu.VMEM((16, slots, rows, feats), dt),
+            pltpu.VMEM((17,) + chunk, dt),
+            pltpu.VMEM((17,) + chunk, dt),
+            pltpu.VMEM((25,) + chunk, dt),
+            pltpu.SemaphoreType.DMA((16,)),
+            pltpu.SemaphoreType.DMA((16,)),
+            pltpu.SemaphoreType.DMA((16,)),
+            pltpu.SemaphoreType.DMA((16, 3)),
+            pltpu.SemaphoreType.DMA((17,)),
+            pltpu.SemaphoreType.DMA((17,)),
+            pltpu.SemaphoreType.DMA((25,)),
+        ],
+        compiler_params=pltpu.CompilerParams(collective_id=cid, has_side_effects=True, vmem_limit_bytes=58 * 2**20),
+        name="scatter_blocks",
+    )(part)
+
+
+def exchange_kernel(devices, own_ref, out_ref, send_sem, recv_sem, own_sem):
+    me = lax.axis_index("seq")
+    bar = pltpu.get_barrier_semaphore()
+    for o in range(1, devices):
+        pl.semaphore_signal(bar, inc=1, device_id=(lax.rem(me + o, devices),), device_id_type=MESH)
+    pl.semaphore_wait(bar, devices - 1)
+    keep = pltpu.make_async_copy(own_ref, out_ref.at[me], own_sem)
+    keep.start()
+
+    def copy(o, place, peer):
+        return pltpu.make_async_remote_copy(
+            src_ref=own_ref,
+            dst_ref=out_ref.at[place],
+            send_sem=send_sem.at[o],
+            recv_sem=recv_sem.at[o],
+            device_id=(peer,),
+            device_id_type=MESH,
+        )
+
+    for o in range(1, devices):
+        copy(o, me, lax.rem(me + o, devices)).start()
+    for o in range(1, devices):
+        peer = lax.rem(me - o + devices, devices)
+        copy(o, peer, peer).wait()
+    keep.wait()
+
+
+def exchange_rows(rows, cid):
+    devices = lax.axis_size("seq")
+    if devices != GRID_DEVICES:
+        return lax.all_gather(rows[None], "seq", axis=0, tiled=True)
+    return pl.pallas_call(
+        functools.partial(exchange_kernel, devices),
+        out_shape=jax.ShapeDtypeStruct((devices,) + rows.shape, rows.dtype),
+        in_specs=[pl.BlockSpec(memory_space=pltpu.VMEM)],
+        out_specs=pl.BlockSpec(memory_space=pltpu.VMEM),
+        scratch_shapes=[
+            pltpu.SemaphoreType.DMA((devices,)),
+            pltpu.SemaphoreType.DMA((devices,)),
+            pltpu.SemaphoreType.DMA,
+        ],
+        compiler_params=pltpu.CompilerParams(collective_id=cid, has_side_effects=True),
+        name="exchange_rows",
+    )(rows)
 
 
 NEGATIVE = -1e30
@@ -192,7 +671,11 @@
     carried_dev = (jnp.cumsum(starts) == 0.0)[:, None]
     zeros_row = jnp.zeros((features,), jnp.float32)
     owned_rows = masters.astype(jnp.bfloat16)
-    forward_rows = split_rows(lax.all_gather(owned_rows, "seq", axis=0, tiled=True), block_slot)
+    if devices == GRID_DEVICES:
+        gathered = gather_blocks(owned_rows).reshape(-1, BLOCK_ROWS, EMBED_SIZE)
+    else:
+        gathered = lax.all_gather(owned_rows, "seq", axis=0, tiled=True)
+    forward_rows = split_rows(gathered, block_slot)
     key_w, value_w, recept_w, output_w, chan_recept_w, chan_key_w, chan_value_w = forward_rows
     inputs = tokens_in.astype(jnp.float32)
     normed, unit_one, inverse_one = norm_forward(inputs, vectors[0], vectors[1])
@@ -243,12 +726,17 @@
             jnp.maximum(early_reset, later_reset),
         )
 
+    all_rows = exchange_rows(jnp.stack([sum_num, sum_den, sum_max]), 3)
+    offset_rows = offsets // tokens
+    has_start = jnp.sum(
+        (offset_rows[None, :] == jnp.arange(devices)[:, None]).astype(jnp.float32), axis=1
+    )
     summaries = (
-        lax.all_gather(sum_num[None], "seq", axis=0, tiled=True),
-        lax.all_gather(sum_den[None], "seq", axis=0, tiled=True),
-        lax.all_gather(sum_max[None], "seq", axis=0, tiled=True),
-        lax.all_gather(count_row[None], "seq", axis=0, tiled=True),
-        lax.all_gather(reset_flag[None], "seq", axis=0, tiled=True),
+        all_rows[:, 0],
+        all_rows[:, 1],
+        all_rows[:, 2],
+        jnp.full((devices, 1), float(tokens), jnp.float32),
+        jnp.minimum(has_start, 1.0)[:, None],
     )
     running = lax.associative_scan(merge_state, summaries)
     below_index = jnp.maximum(device_place - 1, 0)
@@ -289,7 +777,6 @@
     chan_value = product(squared, chan_value_w)
     gate_two = jax.nn.sigmoid(product(chan_in_recept, chan_recept_w))
     layer_out = (resid + gate_two * chan_value).astype(jnp.bfloat16)
-    backward_rows = split_rows(lax.all_gather(owned_rows, "seq", axis=0, tiled=True), block_slot)
     (
         key_back,
         value_back,
@@ -298,7 +785,7 @@
         chan_recept_back,
         chan_key_back,
         chan_value_back,
-    ) = backward_rows
+    ) = forward_rows
     out_grad = cotangent.astype(jnp.float32) * pad_mask.astype(jnp.float32)[:, None]
     grad_chan_value = (out_grad * gate_two).astype(jnp.bfloat16)
     grad_chan_gate = (out_grad * chan_value * gate_two * (1.0 - gate_two)).astype(jnp.bfloat16)
@@ -340,11 +827,8 @@
     def merge_grad(early, later):
         return (later[0] + later[2] * early[0], later[1] + later[2] * early[1], later[2] * early[2])
 
-    terms_back = (
-        lax.all_gather(direct_num[None], "seq", axis=0, tiled=True),
-        lax.all_gather(direct_den[None], "seq", axis=0, tiled=True),
-        lax.all_gather(multiplier[None], "seq", axis=0, tiled=True),
-    )
+    back_rows = exchange_rows(jnp.stack([direct_num, direct_den, multiplier]), 4)
+    terms_back = (back_rows[:, 0], back_rows[:, 1], back_rows[:, 2])
     running_back = lax.associative_scan(merge_grad, tuple((column[::-1] for column in terms_back)))
     above_index = jnp.maximum(devices - 2 - device_place, 0)
     onward = tuple(
@@ -409,12 +893,21 @@
         axis=0,
     )
     slot_total = masters.shape[0] * devices
-    slot_grad = (
-        jnp.zeros((slot_total, BLOCK_ROWS, EMBED_SIZE), jnp.float32)
+    slot_block = (
+        jnp.full((slot_total,), BLOCKS, jnp.int32)
         .at[block_slot]
-        .set(row_grad.reshape(BLOCKS, BLOCK_ROWS, EMBED_SIZE))
-    )
-    owner_grad = lax.psum_scatter(slot_grad, "seq", scatter_dimension=0, tiled=True)
+        .set(jnp.arange(BLOCKS, dtype=jnp.int32))
+    )
+    named = (slot_block < BLOCKS)[:, None, None]
+    low_grad = row_grad.astype(jnp.bfloat16).reshape(BLOCKS, BLOCK_ROWS, EMBED_SIZE)
+    slot_grad = jnp.where(named, low_grad[jnp.minimum(slot_block, BLOCKS - 1)], 0.0)
+    if devices == GRID_DEVICES:
+        owner_grad = scatter_blocks(slot_grad.reshape((devices,) + masters.shape))
+        owner_grad = owner_grad.astype(jnp.float32)
+    else:
+        owner_grad = lax.psum_scatter(
+            slot_grad.astype(jnp.float32), "seq", scatter_dimension=0, tiled=True
+        )
     stacked = jnp.stack(
         [
             grad_gain_one,

time: 1410 us -> 702 us (0.50)
  waiting for transfers between devices: 584 us -> 0.77 us
  Pallas kernels: 0 us -> 313 us
  blocking collectives: 310 us -> 41.4 us
  local copies, waits for them, and re-layouts: 310 us -> 146 us
  other arithmetic: 86 us -> 110 us
    unnamed x3 -> x0, waiting for transfers between devices: 456 us -> none
    pallas_call x0 -> x4, Pallas kernels: none -> 313 us  [the longest x1 148 us: scatter_blocks(): pl.pallas_call(functools.partial(scatter_kernel, slots), out_shape=jax.Sh...]
    all_gather x6 -> x0, blocking collectives: 229 us -> none  [the longest x1 39.2 us: body(): lax.all_gather(multiplier[None], 'seq', axis=0, tiled=True)]
    all_gather x1 -> x0, waiting for transfers between devices: 126 us -> none  [body(): lax.all_gather(owned_rows, 'seq', axis=0, tiled=True)]
    scatter x1, local copies, waits for them, and re-layouts: 103 us -> 3.13 us  [body(): slot_block = jnp.full((slot_total,), BLOCKS, jnp.int32).at[block_slot].se...]
    unnamed x1 -> x0, blocking collectives: 43.2 us -> none
    slice x48 -> x47, local copies, waits for them, and re-layouts: 32.1 us -> 3.21 us  [body(): lax.associative_scan(merge_grad, tuple((column[::-1] for column in terms_...]
    gather x0 -> x1, local copies, waits for them, and re-layouts: none -> 24.3 us  [body(): low_grad[jnp.minimum(slot_block, BLOCKS - 1)]]
  transfers between devices with their start and end apart: 6 -> 4, of which waited for: 3 -> 1; matrix products, arithmetic and copies ran while one was open for 4% -> 20% of each run, Pallas kernels for 0% -> 40%
where the time goes in v1:
time: 702 us; the launch traced here: 697 us
  Pallas kernels  313 us (45%)
  local copies, waits for them, and re-layouts  146 us (21%)
  other arithmetic  110 us (16%)
  matrix products  68.9 us (10%)
  blocking collectives  41.4 us (6%)
  starting transfers between devices  7.61 us (1%)
    pallas_call x1, Pallas kernels, scatter_blocks(): pl.pallas_call(functools.partial(scatter_kernel, slots), out_shape=jax.Sh...  148 us
    pallas_call x1, Pallas kernels, gather_blocks(): pl.pallas_call(functools.partial(gather_kernel, slots), out_shape=jax.Sha...  129 us
    psum x1, blocking collectives, body(): vector_grad = lax.psum(stacked, 'seq')  41.4 us
    pallas_call x2, Pallas kernels, exchange_rows(): pl.pallas_call(functools.partial(exchange_kernel, devices), out_shape=jax...  36.8 us
    gather x1, local copies, waits for them, and re-layouts, body(): low_grad[jnp.minimum(slot_block, BLOCKS - 1)]  24.3 us
    gather x1, local copies, waits for them, and re-layouts, split_rows(): weight_rows = gathered[block_slot].reshape(ROWS_ALL, EMBED_SIZE)  24 us
    dot_general x7, matrix products, product_left(): lax.dot_general(left_side, right_side, (((0,), (0,)), ((), ())), preferre...  23.4 us
    dot_general x7, matrix products, product_back(): lax.dot_general(left_side, right_side, (((1,), (1,)), ((), ())), preferre...  22 us
  transfers between devices with their start and end apart: 4, of which 1 were waited for; matrix products, arithmetic and copies ran while one was open for 20% of the time, Pallas kernels for 40%

profile of v1, /device:TPU:0, one launch (start us, length us, event | category | flops | bytes accessed | tf_op | source)
XLA Modules:
  0.0 696.7 jit_solution(10799257768669636473)
XLA Ops:
  2.9 1.3 fusion.113
  4.3 1.3 fusion.107
  5.6 2.4 collective-permute-start
  9.1 129.0 %gather_blocks.1 = bf16[32,15,32,1024]{3,2,1,0:T(8,128)(2,1)} custom-call(bf16[15,32,1024]{2,1,0:T(8,128)(2,1)} %convert_element_type.123.own_ref), custom_call_target="tpu_custom_call" | custom-call | tf_op jit(solution)/shard_map/gather_blocks/pallas_call | solution.py:216
  138.2 3.1 scatter_custom_fusion
  141.9 24.0 %gather_fusion = bf16[416,32,1024]{2,1,0:T(8,128)(2,1)} fusion(bf16[480,32,1024]{2,1,0:T(8,128)(2,1)} %bitcast.661, s32[1024]{0:T(1024)S(1)} %get-tuple-element.2194), kind=kCustom, calls=%fused_computation | custom fusion | bytes 54527616 | tf_op jit(solution)/shard_map/gather | solution.py:546
  165.9 12.4 %fusion.190 = (bf16[128,32,1024]{2,1,0:T(8,128)(2,1)}, bf16[128,32,1024]{2,1,0:T(8,128)(2,1)}) fusion(bf16[416,32,1024]{2,1,0:T(8,128)(2,1)} %gather_fusion), kind=kLoop, calls=%fused_computation.527 | loop fusion | bytes 33554432 | tf_op jit(solution)/shard_map/slice | solution.py:553
  178.2 7.6 %fusion.191 = (bf16[32,32,1024]{2,1,0:T(8,128)(2,1)}, bf16[32,32,1024]{2,1,0:T(8,128)(2,1)}, bf16[32,32,1024]{2,1,0:T(8,128)(2,1)}, bf16[32,32,1024]{2,1,0:T(8,128)(2,1)}, bf16[32,32,1024]{2,1,0:T(8,128)(2,1)}) fusion(bf16[416,32,1024]{2,1,0:T(8,128)(2,1)} %gather_fusion), kind=kLoop, calls=%fused_computation.528 | loop fusion | bytes 20971520 | tf_op jit(solution)/shard_map/slice | solution.py:552
  188.9 1.3 fusion.197
  219.6 46.0 %while.107 = (s32[]{:T(128)}, f32[1024]{0:T(1024)}, f32[1024]{0:T(1024)}, f32[1024]{0:T(1024)}, f32[2,128,1024]{2,1,0:T(8,128)}, /*index=5*/f32[2,128,1024]{2,1,...) while((s32[]{:T(128)}, f32[1024]{0:T(1024)}, ...), condition=%wide.region_10.11_spmd.clone.clone.clone.clone, body=%wide.region_4.10_spmd.clone.clone.clone.clone.sunk | while | flops 412256768 | bytes 67647752 | solution.py:617
  222.0 1.2 convert_reduce_fusion.6
  227.8 1.7 bitcast_dynamic-update-slice_fusion.9
  230.8 2.4 multiply_dynamic-update-slice_fusion.2
  237.1 1.3 select_dynamic-update-slice_fusion.5
  244.3 1.2 convert_reduce_fusion.6
  247.7 1.3 multiply_add_fusion.20
  249.0 1.3 multiply_add_fusion.21
  251.4 1.7 bitcast_dynamic-update-slice_fusion.9
  254.4 2.4 multiply_dynamic-update-slice_fusion.2
  260.7 1.3 select_dynamic-update-slice_fusion.5
  265.6 1.3 pad_maximum_fusion.10.own_ref
  266.9 15.1 %exchange_rows.2 = f32[32,3,1024]{2,1,0:T(4,128)} custom-call(f32[3,1024]{1,0:T(4,128)} %pad_maximum_fusion.10.own_ref), custom_call_target="tpu_custom_call" | custom-call | tf_op jit(solution)/shard_map/exchange_rows/pallas_call | solution.py:480
  282.0 1.9 fusion.194
  287.1 1.4 slice_bitcast_fusion.2
  293.2 1.3 pad.192
  299.0 1.3 pad.191
  304.9 6.0 multiply_convert_fusion.4
  312.4 2.0 collective-permute-start.1
  315.9 6.5 convolution_maximum_fusion
  322.4 2.4 fusion.120
  325.6 1.9 multiply_convert_fusion.2
  327.5 7.6 %fusion.92 = bf16[256,4096]{1,0:T(8,128)(2,1)} fusion(f32[256,4096]{1,0:T(8,128)S(1)} %convolution_maximum_fusion, bf16[256,1024]{1,0:T(8,128)(2,1)S(1)} %get-tuple-element.2093, bf16[4096,1024]{1,0:T(8,128)(2,1)} %bitcast.685), kind=kOutput, calls=%fused_computation.194 | convolution fusion | flops 2150629376 | bytes 15204352 | tf_op jit(solution)/shard_map/dot_general | solution.py:516
  335.1 4.0 fusion.201
  339.1 2.6 multiply_reduce_fusion.3
  341.7 1.5 collective-permute-start.2
  344.0 1.9 copy.202
  353.6 2.7 multiply_add_fusion.5
  356.4 3.3 multiply_reduce_fusion.6
  360.4 21.7 %exchange_rows.3 = f32[32,3,1024]{2,1,0:T(4,128)} custom-call(f32[3,1024]{1,0:T(4,128)} %pad_maximum_fusion.14.own_ref), custom_call_target="tpu_custom_call" | custom-call | tf_op jit(solution)/shard_map/exchange_rows/pallas_call | solution.py:480
  382.1 1.9 fusion.193
  389.1 27.0 %while.106 = (s32[]{:T(128)}, f32[1024]{0:T(1024)S(1)}, f32[1024]{0:T(1024)S(1)}, f32[1024]{0:T(1024)S(1)}, f32[1024]{0:T(1024)S(1)}, /*index=5*/f32[1024]{0:T(1...) while((s32[]{:T(128)}, f32[1024]{0:T(1024)S(1)}, ...), condition=%wide.region_31.32_spmd.clone, body=%wide.region_21.31_spmd.clone.sunk | while | flops 410812672 | bytes 67400216 | solution.py:617
  390.5 4.0 fusion.257
  394.5 2.4 fusion.258
  400.6 1.2 bitcast_dynamic-update-slice_fusion.8
  404.0 4.0 fusion.257
  408.1 2.4 fusion.258
  416.2 3.4 convert_dynamic-update-slice_fusion.7
  419.6 2.0 fusion.202
  422.5 1.3 copy-done.44
  424.0 1.9 add_multiply_fusion.2
  426.0 1.8 collective-permute-start.3
  427.8 2.1 convert_dynamic-update-slice_fusion.6
  430.0 2.4 convert_dynamic-update-slice_fusion.5
  432.4 2.0 convert_dynamic-update-slice_fusion.4
  434.4 2.1 convert_dynamic-update-slice_fusion.3
  436.5 5.7 convert_dynamic-update-slice_fusion.2
  442.2 5.7 convert_dynamic-update-slice_fusion.1
  447.9 24.3 %gather_fusion.1 = bf16[480,32,1024]{2,1,0:T(8,128)(2,1)} fusion(bf16[416,32,1024]{2,1,0:T(8,128)(2,1)} %bitcast.70, s32[1024]{0:T(1024)S(1)} %copy-done.157), kind=kCustom, calls=%fused_computation.1 | custom fusion | bytes 62916480 | tf_op jit(solution)/shard_map/gather | solution.py:903
  472.3 21.4 %broadcast_select_fusion.3.part_ref = bf16[32,15,32,1024]{3,2,1,0:T(8,128)(2,1)} fusion(bf16[32,15,32,1024]{3,2,1,0:T(8,128)(2,1)} %bitcast.660, pred[32,15]{1,0:T(8,128)(4,1)S(1)} %copy-done.150), kind=kLoop, calls=%fused_computation.188 | loop fusion | flops 15728640 | bytes 62915040 | tf_op jit(solution)/shard_map/jit(_where)/select_n | solution.py:903
  493.6 147.6 %scatter_blocks.1 = bf16[15,32,1024]{2,1,0:T(8,128)(2,1)} custom-call(bf16[32,15,32,1024]{3,2,1,0:T(8,128)(2,1)} %broadcast_select_fusion.3.part_ref), custom_call_target="tpu_custom_call" | custom-call | tf_op jit(solution)/shard_map/scatter_blocks/pallas_call | solution.py:425
  641.2 6.3 multiply_subtract_fusion.1
  649.2 2.2 fusion.112
  651.5 41.4 %psum.7 = f32[11,1024]{1,0:T(8,128)S(1)} all-reduce(f32[11,1024]{1,0:T(8,128)S(1)} %stack.70), channel_id=1, replica_groups=mesh['seq'=32] {'seq'}, use_global_device_ids=true, to_apply=%region_45.46 | all-reduce | flops 11264 | bytes 90112 | tf_op jit(solution)/shard_map/psum | solution.py:926
  692.9 2.6 fusion.111
  (872 shorter events, 111.4 us)
Async XLA Ops:
  0.6 7.4 %copy-start.46 = (f32[15,32,1024]{2,1,0:T(8,128)S(1)}, f32[15,32,1024]{2,1,0:T(8,128)}, u32[]{:S(2)}) copy-start(f32[15,32,1024]{2,1,0:T(8,128)} %param.20) | copy-start | bytes 5898244
  1.7 197.8 %copy-start.83 = (f32[1,1024]{1,0:T(1,128)}, f32[1,1024]{1,0:T(1,128)S(1)}, u32[]{:S(2)}) copy-start(f32[1,1024]{1,0:T(1,128)S(1)} %get-tuple-element.2141) | copy-start | bytes 12292
  1.7 197.8 %copy-start.85 = (f32[1,1024]{1,0:T(1,128)}, f32[1,1024]{1,0:T(1,128)S(1)}, u32[]{:S(2)}) copy-start(f32[1,1024]{1,0:T(1,128)S(1)} %get-tuple-element.2140) | copy-start | bytes 12292
  1.7 197.8 %copy-start.118 = (f32[1,1024]{1,0:T(1,128)}, f32[1,1024]{1,0:T(1,128)S(1)}, u32[]{:S(2)}) copy-start(f32[1,1024]{1,0:T(1,128)S(1)} %get-tuple-element.2137) | copy-start | bytes 12292
  1.7 197.8 %copy-start.120 = (f32[1,1024]{1,0:T(1,128)}, f32[1,1024]{1,0:T(1,128)S(1)}, u32[]{:S(2)}) copy-start(f32[1,1024]{1,0:T(1,128)S(1)} %get-tuple-element.2139) | copy-start | bytes 12292
  1.7 197.8 %copy-start.122 = (f32[1,1024]{1,0:T(1,128)}, f32[1,1024]{1,0:T(1,128)S(1)}, u32[]{:S(2)}) copy-start(f32[1,1024]{1,0:T(1,128)S(1)} %get-tuple-element.2135) | copy-start | bytes 12292
  1.7 197.8 %copy-start.124 = (f32[1,1024]{1,0:T(1,128)}, f32[1,1024]{1,0:T(1,128)S(1)}, u32[]{:S(2)}) copy-start(f32[1,1024]{1,0:T(1,128)S(1)} %get-tuple-element.2136) | copy-start | bytes 12292
  2.9 196.6 %copy-start.116 = (f32[256]{0:T(256)}, f32[256]{0:T(256)S(1)}, u32[]{:S(2)}) copy-start(f32[256]{0:T(256)S(1)} %broadcast_multiply_fusion.10) | copy-start | bytes 3076
  4.3 195.3 %copy-start.139 = (f32[256]{0:T(256)}, f32[256]{0:T(256)S(1)}, u32[]{:S(2)}) copy-start(f32[256]{0:T(256)S(1)} %add_rsqrt_fusion.1) | copy-start | bytes 3076
  5.6 193.9 %copy-start.32 = (f32[256,1024]{1,0:T(8,128)}, f32[256,1024]{1,0:T(8,128)S(1)}, u32[]{:S(2)}) copy-start(f32[256,1024]{1,0:T(8,128)S(1)} %fusion.107) | copy-start | bytes 3145732
  5.6 193.8 %collective-permute-start = (f32[1,1024]{1,0:T(1,128)S(1)}, f32[1,1024]{1,0:T(1,128)S(1)}, u32[]{:S(2)}, u32[]{:S(2)}) collective-permute-start(f32[1,1024]{1,0:T(1,128)S(1)} %slice.849), channel_id=1, source_target_pairs={{0,1},{1,2},{2,3},{3,4},{4,5},{5,6},{6,7},{7,8},{8,9},{9,10},{10,1... | collective-permute-start | bytes 12296 | tf_op jit(solution)/shard_map/ppermute | solution.py:508
  9.1 129.0 %copy-start.161 = (s32[416]{0:T(512)S(1)}, s32[416]{0:T(512)}, u32[]{:S(2)}) copy-start(s32[416]{0:T(512)} %param.23) | copy-start | bytes 4996
  141.3 24.6 %copy-start.141 = (s32[480]{0:T(512)}, s32[480]{0:T(512)S(1)}, u32[]{:S(2)}) copy-start(s32[480]{0:T(512)S(1)} %scatter_custom_fusion) | copy-start | bytes 5764
  178.2 7.6 %copy-start.166 = (s32[7]{0:T(128)S(1)}, s32[7]{0:T(128)}, u32[]{:S(2)}) copy-start(s32[7]{0:T(128)} %param.19) | copy-start | bytes 88
  178.2 21.3 %copy-start.10 = (bf16[256,1024]{1,0:T(8,128)(2,1)S(1)}, bf16[256,1024]{1,0:T(8,128)(2,1)}, u32[]{:S(2)}) copy-start(bf16[256,1024]{1,0:T(8,128)(2,1)} %param.16) | copy-start | bytes 1572868
  190.2 11.6 %copy-start.136 = (f32[256]{0:T(256)}, f32[256]{0:T(256)S(1)}, u32[]{:S(2)}) copy-start(f32[256]{0:T(256)S(1)} %get-tuple-element.2186) | copy-start | bytes 3076
  230.7 9.4 %copy-start.92 = (f32[2,1024]{1,0:T(2,128)S(1)}, f32[2,1024]{1,0:T(2,128)}, u32[]{:S(2)}) copy-start(f32[2,1024]{1,0:T(2,128)} %get-tuple-element.2890) | copy-start | bytes 24580 | tf_op jit(solution)/shard_map/jvp()/while
  230.7 9.5 %copy-start.95 = (f32[2,1024]{1,0:T(2,128)S(1)}, f32[2,1024]{1,0:T(2,128)}, u32[]{:S(2)}) copy-start(f32[2,1024]{1,0:T(2,128)} %get-tuple-element.2891) | copy-start | bytes 24580 | tf_op jit(solution)/shard_map/jvp()/while
  230.7 9.6 %copy-start.98 = (f32[2,1024]{1,0:T(2,128)S(1)}, f32[2,1024]{1,0:T(2,128)}, u32[]{:S(2)}) copy-start(f32[2,1024]{1,0:T(2,128)} %get-tuple-element.2892) | copy-start | bytes 24580 | tf_op jit(solution)/shard_map/jvp()/while
  230.7 9.6 %copy-start.101 = (f32[2,1024]{1,0:T(2,128)S(1)}, f32[2,1024]{1,0:T(2,128)}, u32[]{:S(2)}) copy-start(f32[2,1024]{1,0:T(2,128)} %get-tuple-element.2893) | copy-start | bytes 24580 | tf_op jit(solution)/shard_map/jvp()/while
  230.8 9.7 %copy-start.156 = (f32[128]{0:T(128)S(1)}, f32[128]{0:T(128)}, u32[]{:S(2)}) copy-start(f32[128]{0:T(128)} %get-tuple-element.2819) | copy-start | bytes 1540 | tf_op jit(solution)/shard_map/jvp()/while
  230.8 10.3 %copy-start.104 = (f32[2,1024]{1,0:T(2,128)S(1)}, f32[2,1024]{1,0:T(2,128)}, u32[]{:S(2)}) copy-start(f32[2,1024]{1,0:T(2,128)} %get-tuple-element.2896) | copy-start | bytes 24580 | tf_op jit(solution)/shard_map/jvp()/while
  230.8 10.3 %copy-start.107 = (f32[2,1024]{1,0:T(2,128)S(1)}, f32[2,1024]{1,0:T(2,128)}, u32[]{:S(2)}) copy-start(f32[2,1024]{1,0:T(2,128)} %get-tuple-element.2897) | copy-start | bytes 24580 | tf_op jit(solution)/shard_map/jvp()/while
  230.8 10.4 %copy-start.110 = (f32[2,1024]{1,0:T(2,128)S(1)}, f32[2,1024]{1,0:T(2,128)}, u32[]{:S(2)}) copy-start(f32[2,1024]{1,0:T(2,128)} %get-tuple-element.2898) | copy-start | bytes 24580 | tf_op jit(solution)/shard_map/jvp()/while
  230.8 10.4 %copy-start.113 = (f32[2,1024]{1,0:T(2,128)S(1)}, f32[2,1024]{1,0:T(2,128)}, u32[]{:S(2)}) copy-start(f32[2,1024]{1,0:T(2,128)} %get-tuple-element.2899) | copy-start | bytes 24580 | tf_op jit(solution)/shard_map/jvp()/while
  234.2 7.1 %copy-start.1 = (f32[2,128,1024]{2,1,0:T(8,128)}, f32[2,128,1024]{2,1,0:T(8,128)S(1)}, u32[]{:S(2)}) copy-start(f32[2,128,1024]{2,1,0:T(8,128)S(1)} %get-tuple-element.2920) | copy-start | bytes 3145732 | tf_op jit(solution)/shard_map/jvp()/while
  243.7 7.6 %copy-start.82 = (f32[128]{0:T(128)S(1)}, f32[128]{0:T(128)}, u32[]{:S(2)}) copy-start(f32[128]{0:T(128)} %get-tuple-element.2952) | copy-start | bytes 1540 | tf_op jit(solution)/shard_map/jvp()/while
  254.4 9.5 %copy-start.92 = (f32[2,1024]{1,0:T(2,128)S(1)}, f32[2,1024]{1,0:T(2,128)}, u32[]{:S(2)}) copy-start(f32[2,1024]{1,0:T(2,128)} %get-tuple-element.2890) | copy-start | bytes 24580 | tf_op jit(solution)/shard_map/jvp()/while
  254.4 9.5 %copy-start.95 = (f32[2,1024]{1,0:T(2,128)S(1)}, f32[2,1024]{1,0:T(2,128)}, u32[]{:S(2)}) copy-start(f32[2,1024]{1,0:T(2,128)} %get-tuple-element.2891) | copy-start | bytes 24580 | tf_op jit(solution)/shard_map/jvp()/while
  254.4 9.6 %copy-start.98 = (f32[2,1024]{1,0:T(2,128)S(1)}, f32[2,1024]{1,0:T(2,128)}, u32[]{:S(2)}) copy-start(f32[2,1024]{1,0:T(2,128)} %get-tuple-element.2892) | copy-start | bytes 24580 | tf_op jit(solution)/shard_map/jvp()/while
  254.4 9.7 %copy-start.101 = (f32[2,1024]{1,0:T(2,128)S(1)}, f32[2,1024]{1,0:T(2,128)}, u32[]{:S(2)}) copy-start(f32[2,1024]{1,0:T(2,128)} %get-tuple-element.2893) | copy-start | bytes 24580 | tf_op jit(solution)/shard_map/jvp()/while
  254.4 9.8 %copy-start.156 = (f32[128]{0:T(128)S(1)}, f32[128]{0:T(128)}, u32[]{:S(2)}) copy-start(f32[128]{0:T(128)} %get-tuple-element.2819) | copy-start | bytes 1540 | tf_op jit(solution)/shard_map/jvp()/while
  254.4 10.3 %copy-start.104 = (f32[2,1024]{1,0:T(2,128)S(1)}, f32[2,1024]{1,0:T(2,128)}, u32[]{:S(2)}) copy-start(f32[2,1024]{1,0:T(2,128)} %get-tuple-element.2896) | copy-start | bytes 24580 | tf_op jit(solution)/shard_map/jvp()/while
  254.4 10.4 %copy-start.107 = (f32[2,1024]{1,0:T(2,128)S(1)}, f32[2,1024]{1,0:T(2,128)}, u32[]{:S(2)}) copy-start(f32[2,1024]{1,0:T(2,128)} %get-tuple-element.2897) | copy-start | bytes 24580 | tf_op jit(solution)/shard_map/jvp()/while
  254.4 10.4 %copy-start.110 = (f32[2,1024]{1,0:T(2,128)S(1)}, f32[2,1024]{1,0:T(2,128)}, u32[]{:S(2)}) copy-start(f32[2,1024]{1,0:T(2,128)} %get-tuple-element.2898) | copy-start | bytes 24580 | tf_op jit(solution)/shard_map/jvp()/while
  254.4 10.5 %copy-start.113 = (f32[2,1024]{1,0:T(2,128)S(1)}, f32[2,1024]{1,0:T(2,128)}, u32[]{:S(2)}) copy-start(f32[2,1024]{1,0:T(2,128)} %get-tuple-element.2899) | copy-start | bytes 24580 | tf_op jit(solution)/shard_map/jvp()/while
  257.9 7.2 %copy-start.1 = (f32[2,128,1024]{2,1,0:T(8,128)}, f32[2,128,1024]{2,1,0:T(8,128)S(1)}, u32[]{:S(2)}) copy-start(f32[2,128,1024]{2,1,0:T(8,128)S(1)} %get-tuple-element.2920) | copy-start | bytes 3145732 | tf_op jit(solution)/shard_map/jvp()/while
  265.6 18.7 %copy-start.129 = (f32[1024]{0:T(1024)S(1)}, f32[1024]{0:T(1024)}, u32[]{:S(2)}) copy-start(f32[1024]{0:T(1024)} %get-tuple-element.2183) | copy-start | bytes 12292
  265.6 18.7 %copy-start.168 = (pred[16]{0:T(512)(128)(4,1)S(1)}, pred[16]{0:T(512)(128)(4,1)}, u32[]{:S(2)}) copy-start(pred[16]{0:T(512)(128)(4,1)} %compare_bitcast_fusion.5) | copy-start | bytes 52
  265.6 18.9 %copy-start.130 = (f32[1024]{0:T(1024)S(1)}, f32[1024]{0:T(1024)}, u32[]{:S(2)}) copy-start(f32[1024]{0:T(1024)} %get-tuple-element.2182) | copy-start | bytes 12292
  265.6 18.9 %copy-start.164 = (pred[8]{0:T(512)(128)(4,1)S(1)}, pred[8]{0:T(512)(128)(4,1)}, u32[]{:S(2)}) copy-start(pred[8]{0:T(512)(128)(4,1)} %compare_bitcast_fusion.3) | copy-start | bytes 28
  284.1 7.4 %copy-start.160 = (pred[3]{0:T(512)(128)(4,1)S(1)}, pred[3]{0:T(512)(128)(4,1)}, u32[]{:S(2)}) copy-start(pred[3]{0:T(512)(128)(4,1)} %compare_bitcast_fusion.2) | copy-start | bytes 13
  284.2 8.8 %copy-start.159 = (pred[7]{0:T(512)(128)(4,1)S(1)}, pred[7]{0:T(512)(128)(4,1)}, u32[]{:S(2)}) copy-start(pred[7]{0:T(512)(128)(4,1)} %compare_bitcast_fusion.4) | copy-start | bytes 25
  287.1 9.0 %copy-start.81 = (f32[7,1024]{1,0:T(8,128)S(1)}, f32[7,1024]{1,0:T(8,128)}, u32[]{:S(2)}) copy-start(f32[7,1024]{1,0:T(8,128)} %slice.724) | copy-start | bytes 86020
  293.2 11.7 %copy-start.11 = (bf16[256,1024]{1,0:T(8,128)(2,1)S(1)}, bf16[256,1024]{1,0:T(8,128)(2,1)}, u32[]{:S(2)}) copy-start(bf16[256,1024]{1,0:T(8,128)(2,1)} %param.16) | copy-start | bytes 1572868
  293.2 11.7 %copy-start.33 = (f32[256,1024]{1,0:T(8,128)S(1)}, f32[256,1024]{1,0:T(8,128)}, u32[]{:S(2)}) copy-start(f32[256,1024]{1,0:T(8,128)} %copy-done.32) | copy-start | bytes 3145732
  293.2 11.7 %copy-start.84 = (f32[1,1024]{1,0:T(1,128)S(1)}, f32[1,1024]{1,0:T(1,128)}, u32[]{:S(2)}) copy-start(f32[1,1024]{1,0:T(1,128)} %copy-done.83) | copy-start | bytes 12292
  293.2 11.7 %copy-start.86 = (f32[1,1024]{1,0:T(1,128)S(1)}, f32[1,1024]{1,0:T(1,128)}, u32[]{:S(2)}) copy-start(f32[1,1024]{1,0:T(1,128)} %copy-done.85) | copy-start | bytes 12292
  312.4 2.8 collective-permute-start.1
  315.2 7.1 %slice-start.2 = ((s8[8388608]{0:T(1024)(128)(4,1)}), s8[4194304]{0:T(1024)(128)(4,1)S(1)}, s32[]{:S(2)}) async-start(s8[8388608]{0:T(1024)(128)(4,1)} %bitcast.686), calls=%async_computation.2 | async-start | bytes 8388608
  315.9 8.9 %copy-start.68 = (bf16[256,1024]{1,0:T(8,128)(2,1)}, bf16[256,1024]{1,0:T(8,128)(2,1)S(1)}, u32[]{:S(2)}) copy-start(bf16[256,1024]{1,0:T(8,128)(2,1)S(1)} %get-tuple-element.2086) | copy-start | bytes 1572868
  325.6 9.5 %slice-start = ((s8[8388608]{0:T(1024)(128)(4,1)}), s8[4194304]{0:T(1024)(128)(4,1)S(1)}, s32[]{:S(2)}) async-start(s8[8388608]{0:T(1024)(128)(4,1)} %bitcast.682), calls=%async_computation | async-start | bytes 8388608
  327.5 7.6 %copy-start.70 = (bf16[256,1024]{1,0:T(8,128)(2,1)}, bf16[256,1024]{1,0:T(8,128)(2,1)S(1)}, u32[]{:S(2)}) copy-start(bf16[256,1024]{1,0:T(8,128)(2,1)S(1)} %get-tuple-element.2093) | copy-start | bytes 1572868
  327.5 11.6 %copy-start.74 = (bf16[256,1024]{1,0:T(8,128)(2,1)}, bf16[256,1024]{1,0:T(8,128)(2,1)S(1)}, u32[]{:S(2)}) copy-start(bf16[256,1024]{1,0:T(8,128)(2,1)S(1)} %get-tuple-element.2089) | copy-start | bytes 1572868
  327.5 7.6 %slice-start.1 = ((s8[8388608]{0:T(1024)(128)(4,1)}), s8[4194304]{0:T(1024)(128)(4,1)S(1)}, s32[]{:S(2)}) async-start(s8[8388608]{0:T(1024)(128)(4,1)} %bitcast.682), calls=%async_computation.1 | async-start | bytes 8388608
  341.7 5.0 collective-permute-start.2
  426.0 221.8 %collective-permute-start.3 = (f32[1,1024]{1,0:T(1,128)S(1)}, f32[1,1024]{1,0:T(1,128)S(1)}, u32[]{:S(2)}, u32[]{:S(2)}) collective-permute-start(f32[1,1024]{1,0:T(1,128)S(1)} %slice.936), channel_id=1, source_target_pairs={{1,0},{2,1},{3,2},{4,3},{5,4},{6,5},{7,6},{8,7},{9,8},{10,9},{11,1... | collective-permute-start | bytes 12296 | tf_op jit(solution)/shard_map/ppermute | solution.py:508
  447.9 24.3 %copy-start.150 = (pred[32,15]{1,0:T(8,128)(4,1)S(1)}, pred[32,15]{1,0:T(8,128)(4,1)}, u32[]{:S(2)}) copy-start(pred[32,15]{1,0:T(8,128)(4,1)} %broadcast_in_dim.465) | copy-start | bytes 1444
  493.6 147.6 %copy-start.47 = (f32[15,32,1024]{2,1,0:T(8,128)S(1)}, f32[15,32,1024]{2,1,0:T(8,128)}, u32[]{:S(2)}) copy-start(f32[15,32,1024]{2,1,0:T(8,128)} %param.20) | copy-start | bytes 5898244
  641.2 6.6 copy-start.50
  651.4 44.1 %copy-start.77 = (f32[11,1024]{1,0:T(8,128)S(1)}, f32[11,1024]{1,0:T(8,128)}, u32[]{:S(2)}) copy-start(f32[11,1024]{1,0:T(8,128)} %param.24) | copy-start | bytes 135172
  651.4 44.1 %copy-start.87 = (f32[11,1024]{1,0:T(8,128)S(1)}, f32[11,1024]{1,0:T(8,128)}, u32[]{:S(2)}) copy-start(f32[11,1024]{1,0:T(8,128)} %param.26) | copy-start | bytes 135172
  651.4 44.1 %copy-start.88 = (f32[11,1024]{1,0:T(8,128)S(1)}, f32[11,1024]{1,0:T(8,128)}, u32[]{:S(2)}) copy-start(f32[11,1024]{1,0:T(8,128)} %param.25) | copy-start | bytes 135172
  651.4 44.2 %copy-start.167 = (f32[11]{0:T(128)S(1)}, f32[11]{0:T(128)}, u32[]{:S(2)}) copy-start(f32[11]{0:T(128)} %constant.336.clone) | copy-start | bytes 136
  (168 other events, 419.6 us)

commit v2 on v1

v2 whole, which is shorter than its diff:
```python
import functools

import jax
import jax.numpy as jnp
from jax import lax
from jax.experimental import pallas as pl
from jax.experimental.pallas import tpu as pltpu
from jax.sharding import PartitionSpec as P

EMBED_SIZE = 1024
FF = 4096
BLOCK_ROWS = 32
ROWS_ALL = 13312
BLOCKS = 416
STEP = 10
GRID_DEVICES = 32
MESH = pl.DeviceIdType.MESH


NEGATIVE = -1e30
NORM_EPS = 1e-05
BETA_ONE = 0.9
BETA_TWO = 0.999
ADAM_EPS = 1e-08
MATRIX_RATE = 0.05
WEIGHT_DECAY = 0.01
VECTOR_RATE = (0.25, 0.25, 0.25, 0.25, 0.25, 2.0, 0.25, 0.25, 0.25, 0.25, 0.25)


def shifted(block, axis, distance):
    devices = range(lax.axis_size(axis))
    route = [(i - distance, i) for i in devices if i - distance in devices]
    return lax.ppermute(block, axis, route)


def product_back(left_side, right_side):
    return lax.dot_general(
        left_side, right_side, (((1,), (1,)), ((), ())), preferred_element_type=jnp.float32
    )


def product_left(left_side, right_side):
    return lax.dot_general(
        left_side, right_side, (((0,), (0,)), ((), ())), preferred_element_type=jnp.float32
    )


def adam_update(weight, first_moment, second_moment, gradient, step_rate, feature_fade_speed):
    first_moment = BETA_ONE * first_moment + (1.0 - BETA_ONE) * gradient
    second_moment = BETA_TWO * second_moment + (1.0 - BETA_TWO) * gradient * gradient
    first_fixed = first_moment / (1.0 - BETA_ONE**STEP)
    second_fixed = second_moment / (1.0 - BETA_TWO**STEP)
    weight = weight - step_rate * (
        first_fixed / (jnp.sqrt(second_fixed) + ADAM_EPS) + feature_fade_speed * weight
    )
    return (first_moment, second_moment, weight)


def grid_place():
    me = lax.axis_index("seq")
    return me, lax.rem(me, 2), lax.rem(me // 2, 2), lax.rem(me // 4, 2), me // 8

def spans(slots):
    side = 4 * slots // 15
    cuts = [0, side, 2 * side, slots]
    return [(cuts[i], cuts[i + 1] - cuts[i]) for i in range(3)]

def gather_kernel(slots, own_ref, x_ref, grad_ref, out_ref, after_ref, after_grad_ref, before_ref, *scratch):
    send_sem, recv_sem, sib_send, sib_recv, own_sem, halo_send, halo_recv = scratch
    me, core, x, y, z = grid_place()
    sib = me + 1 - 2 * core
    x_peer = me + 2 - 4 * x
    y_peer = me + 4 - 8 * y
    up = me + 8
    down = me - 8
    bar = pltpu.get_barrier_semaphore()
    pl.semaphore_signal(bar, inc=1, device_id=(sib,), device_id_type=MESH)
    pl.semaphore_signal(bar, inc=1, device_id=(x_peer,), device_id_type=MESH)
    pl.semaphore_signal(bar, inc=1, device_id=(y_peer,), device_id_type=MESH)
    @pl.when(z < 3)
    def _():
        pl.semaphore_signal(bar, inc=1, device_id=(up,), device_id_type=MESH)
    @pl.when(z > 0)
    def _():
        pl.semaphore_signal(bar, inc=1, device_id=(down,), device_id_type=MESH)
    more, less = me < GRID_DEVICES - 1, me > 0

    @pl.when(more)
    def _():
        pl.semaphore_signal(bar, inc=1, device_id=(me + 1,), device_id_type=MESH)

    @pl.when(less)
    def _():
        pl.semaphore_signal(bar, inc=1, device_id=(me - 1,), device_id_type=MESH)

    halos = jnp.where(more, 1, 0) + jnp.where(less, 1, 0)
    pl.semaphore_wait(bar, 4 + jnp.where((z > 0) & (z < 3), 1, 0) + halos)
    tokens = x_ref.shape[0]

    def halo_copy(k):
        src, dst, peer = (
            (x_ref.at[pl.ds(0, 16)], after_ref, me - 1),
            (grad_ref.at[pl.ds(0, 16)], after_grad_ref, me - 1),
            (x_ref.at[pl.ds(tokens - 16, 16)], before_ref, me + 1),
        )[k]
        return pltpu.make_async_remote_copy(src_ref=src, dst_ref=dst, send_sem=halo_send.at[k],
            recv_sem=halo_recv.at[k], device_id=(peer,), device_id_type=MESH)
    span = spans(slots)
    targets = (x_peer, y_peer, up, down)

    def chip(cx, cy, cz):
        return (cz * 2 + cy) * 2 + cx

    def view(cx, cy, cz, color, c=None):
        dev = chip(cx, cy, cz) * 2 + (core if c is None else c)
        lo, n = span[color]
        return out_ref.at[dev, pl.ds(lo, n)]

    def send(cx, cy, cz, color, way, own=False):
        lo, n = span[color]
        src = own_ref.at[pl.ds(lo, n)] if own else view(cx, cy, cz, color)
        idx = chip(cx, cy, cz)
        return pltpu.make_async_remote_copy(src_ref=src, dst_ref=view(cx, cy, cz, color),
            send_sem=send_sem.at[idx, color, way], recv_sem=recv_sem.at[idx, color],
            device_id=(targets[way],), device_id_type=MESH)

    def send_sib(cx, cy, cz, color, own=False):
        lo, n = span[color]
        src = own_ref.at[pl.ds(lo, n)] if own else view(cx, cy, cz, color)
        idx = chip(cx, cy, cz)
        return pltpu.make_async_remote_copy(src_ref=src, dst_ref=view(cx, cy, cz, color),
            send_sem=sib_send.at[idx, color], recv_sem=sib_recv.at[idx, color],
            device_id=(sib,), device_id_type=MESH)

    x2, y2 = 1 - x, 1 - y
    pending = []

    def go(copy, cond=None):
        if cond is None:
            copy.start()
        else:
            @pl.when(cond)
            def _():
                copy.start()
        pending.append((copy, cond))

    zup, zdown = z < 3, z > 0
    own_copies = []
    for color in range(3):
        lo, n = span[color]
        cp = pltpu.make_async_copy(own_ref.at[pl.ds(lo, n)], view(x, y, z, color), own_sem.at[color])
        cp.start()
        own_copies.append(cp)
    order = {0: (0, 2, 1), 1: (1, 2, 0)}
    for color in (0, 1, 2):
        go(send(x, y, z, color, 2, True), zup)
        go(send(x, y, z, color, 3, True), zdown)
    for color, way in ((0, 0), (1, 1), (2, 0), (2, 1), (0, 1), (1, 0)):
        go(send(x, y, z, color, way, True))
    for color in range(3):
        go(send_sib(x, y, z, color, True))

    def arrive(cx, cy, cz, color):
        send(cx, cy, cz, color, 0).wait_recv()

    def sibling(cx, cy, cz, color):
        go(send_sib(cx, cy, cz, color))

    is0, is1 = core == 0, core == 1
    px = jnp.where(is0, x2, x)
    py = jnp.where(is0, y, y2)
    qx = jnp.where(is0, x, x2)
    qy = jnp.where(is0, y2, y)
    first = lambda cx, cy, cz: (go(send(cx, cy, cz, 2, 0), is0), go(send(cx, cy, cz, 2, 1), is1))
    last = lambda cx, cy, cz: (go(send(cx, cy, cz, 2, 1), is0), go(send(cx, cy, cz, 2, 0), is1))

    arrive(x2, y, z, 0)
    go(send(x2, y, z, 0, 2), zup)
    go(send(x2, y, z, 0, 3), zdown)
    go(send(x2, y, z, 0, 1))
    sibling(x2, y, z, 0)
    arrive(x, y2, z, 1)
    go(send(x, y2, z, 1, 2), zup)
    go(send(x, y2, z, 1, 3), zdown)
    go(send(x, y2, z, 1, 0))
    sibling(x, y2, z, 1)
    arrive(px, py, z, 2)
    last(px, py, z)
    sibling(px, py, z, 2)

    for dist in (1, 2, 3):
        sides = []
        for sign, fwd, guard_f in ((1, 3, zdown), (-1, 2, zup)):
            q = z + sign * dist
            have = (q >= 0) & (q < 4)
            sides.append((q, fwd, have, guard_f))
        for which in ("c", "a", "b", "a2", "b2"):
            for q, fwd, have, gf in sides:
                @pl.when(have)
                def _(q=q, fwd=fwd, gf=gf, which=which):
                    if which == "c":
                        arrive(x, y, q, 2)
                        cp = send(x, y, q, 2, fwd)
                        pl.when(gf)(lambda: cp.start())
                        for w in (0, 1):
                            send(x, y, q, 2, w).start()
                        send_sib(x, y, q, 2).start()
                    else:
                        color = 0 if which[0] == "a" else 1
                        cx, cy = {"a": (x, y), "b": (x, y), "a2": (x2, y), "b2": (x, y2)}[which]
                        arrive(cx, cy, q, color)
                        cp = send(cx, cy, q, color, fwd)
                        pl.when(gf)(lambda: cp.start())
                        send(cx, cy, q, color, 1 if color == 0 else 0).start()
                        send_sib(cx, cy, q, color).start()
        for q, fwd, have, gf in sides:
            @pl.when(have)
            def _(q=q):
                arrive(px, py, q, 2)
                pl.when(is0)(lambda: send(px, py, q, 2, 1).start())
                pl.when(is1)(lambda: send(px, py, q, 2, 0).start())
                send_sib(px, py, q, 2).start()
        if dist == 1:
            tail_list = [(z, None)]
        else:
            tail_list = []
        def terminal(q):
            for cx, cy, color in ((x, y2, 0), (x2, y2, 0), (x2, y, 1), (x2, y2, 1), (qx, qy, 2), (x2, y2, 2)):
                arrive(cx, cy, q, color)
                send_sib(cx, cy, q, color).start()
        if dist == 1:
            terminal(z)
        else:
            for sign in (1, -1):
                q = z + sign * (dist - 1)
                pl.when((q >= 0) & (q < 4))(lambda q=q: terminal(q))
        if dist == 3:
            for sign in (1, -1):
                q = z + sign * 3
                pl.when((q >= 0) & (q < 4))(lambda q=q: terminal(q))
    @pl.when(less)
    def _():
        for k in (0, 1):
            halo_copy(k).start()

    @pl.when(more)
    def _():
        halo_copy(2).start()

    @pl.when(less)
    def _():
        for k in (0, 1):
            halo_copy(k).wait_send()
        halo_copy(2).wait_recv()

    @pl.when(more)
    def _():
        halo_copy(2).wait_send()
        for k in (0, 1):
            halo_copy(k).wait_recv()

    for cp in own_copies:
        cp.wait()
    for color in range(3):
        pl.when(zup)(lambda color=color: send(x, y, z, color, 2).wait_send())
        pl.when(zdown)(lambda color=color: send(x, y, z, color, 3).wait_send())
        for w in (0, 1):
            send(x, y, z, color, w).wait_send()
    for cx, cy, color, w in ((x2, y, 0, 1), (x, y2, 1, 0)):
        pl.when(zup)(lambda: send(cx, cy, z, color, 2).wait_send())
        pl.when(zdown)(lambda: send(cx, cy, z, color, 3).wait_send())
        send(cx, cy, z, color, w).wait_send()
    pl.when(is0)(lambda: send(px, py, z, 2, 1).wait_send())
    pl.when(is1)(lambda: send(px, py, z, 2, 0).wait_send())
    for dist in (1, 2, 3):
        for sign, fwd, gf in ((1, 3, zdown), (-1, 2, zup)):
            q = z + sign * dist
            @pl.when((q >= 0) & (q < 4))
            def _(q=q, fwd=fwd, gf=gf):
                for cx, cy, color in ((x, y, 2), (x, y, 0), (x, y, 1), (x2, y, 0), (x, y2, 1)):
                    pl.when(gf)(lambda: send(cx, cy, q, color, fwd).wait_send())
                    ways = (0, 1) if color == 2 else ((1,) if color == 0 else (0,))
                    for w in ways:
                        send(cx, cy, q, color, w).wait_send()
                pl.when(is0)(lambda: send(px, py, q, 2, 1).wait_send())
                pl.when(is1)(lambda: send(px, py, q, 2, 0).wait_send())
    for cz in range(4):
        for cy in range(2):
            for cx in range(2):
                for color in range(3):
                    cp = send_sib(cx, cy, cz, color)
                    cp.wait_send()
                    cp.wait_recv()

def gather_blocks(owned, tokens_in, out_grad, cid=1):
    slots = owned.shape[0]
    anywhere = pl.BlockSpec(memory_space=pl.ANY)
    halo = jax.ShapeDtypeStruct((16,) + tokens_in.shape[1:], tokens_in.dtype)
    return pl.pallas_call(
        functools.partial(gather_kernel, slots),
        out_shape=(jax.ShapeDtypeStruct((GRID_DEVICES,) + owned.shape, owned.dtype), halo, halo, halo),
        in_specs=[anywhere] * 3,
        out_specs=(anywhere,) * 4,
        scratch_shapes=[
            pltpu.SemaphoreType.DMA((16, 3, 4)),
            pltpu.SemaphoreType.DMA((16, 3)),
            pltpu.SemaphoreType.DMA((16, 3)),
            pltpu.SemaphoreType.DMA((16, 3)),
            pltpu.SemaphoreType.DMA((3,)),
            pltpu.SemaphoreType.DMA((3,)),
            pltpu.SemaphoreType.DMA((3,)),
        ],
        compiler_params=pltpu.CompilerParams(collective_id=cid, has_side_effects=True),
        name="gather_blocks",
    )(owned, tokens_in, out_grad)


def scatter_kernel(
    slots, part_ref, rows_ref, out_ref, total_ref, acc, sib, xin, yin, zin, sums,
    load_sem, sib_send, sib_recv, send_sem, xsem, ysem, zsem, row_send, row_recv,
):
    me, core, x, y, z = grid_place()
    sibling = me + 1 - 2 * core
    x_peer = me + 2 - 4 * x
    y_peer = me + 4 - 8 * y
    up, down = me + 8, me - 8
    zup, zdown = z < 3, z > 0
    bar = pltpu.get_barrier_semaphore()
    for peer in (sibling, x_peer, y_peer):
        pl.semaphore_signal(bar, inc=1, device_id=(peer,), device_id_type=MESH)
    @pl.when(zup)
    def _():
        pl.semaphore_signal(bar, inc=1, device_id=(up,), device_id_type=MESH)
    @pl.when(zdown)
    def _():
        pl.semaphore_signal(bar, inc=1, device_id=(down,), device_id_type=MESH)
    far = me + 16 - 32 * (z // 2)
    pl.semaphore_signal(bar, inc=1, device_id=(far,), device_id_type=MESH)
    row_peers = (sibling, x_peer, y_peer, me + 8 - 16 * lax.rem(z, 2), far)
    sums[0] = rows_ref[...]
    span = spans(slots)
    x2, y2 = 1 - x, 1 - y
    is0, is1 = core == 0, core == 1

    def row_copy(k):
        return pltpu.make_async_remote_copy(src_ref=sums.at[2 * k], dst_ref=sums.at[2 * k + 1],
            send_sem=row_send.at[k], recv_sem=row_recv.at[k], device_id=(row_peers[k],), device_id_type=MESH)

    def row_step(k):
        row_copy(k).wait()
        sums[2 * k + 2] = sums[2 * k] + sums[2 * k + 1]
        if k < 4:
            row_copy(k + 1).start()

    def load(chip):
        return pltpu.make_async_copy(part_ref.at[2 * chip + core], acc.at[chip], load_sem.at[chip])

    def give(chip):
        return pltpu.make_async_remote_copy(src_ref=part_ref.at[2 * chip + 1 - core], dst_ref=sib.at[chip],
            send_sem=sib_send.at[chip], recv_sem=sib_recv.at[chip], device_id=(sibling,), device_id_type=MESH)

    levels = []
    for dist in (3, 2, 1):
        for sign in (1, -1):
            q = z + sign * dist
            levels.append((dist, sign, q, (q >= 0) & (q < 4)))

    def run(dist, work):
        for d, sign, q, have in levels:
            if d == dist:
                pl.when(have)(functools.partial(work, q))

    def run_signed(dist, work):
        for d, sign, q, have in levels:
            if d == dist:
                pl.when(have)(functools.partial(work, q, sign, dist))

    def begin_loads(q):
        for i in plane_order():
            load(4 * q + i).start()

    def begin_gives(q):
        for i in plane_order():
            give(4 * q + i).start()

    def plane_order():
        return (2 * y2 + x2, 2 * y + x2, 2 * y2 + x, 2 * y + x)

    run(3, begin_loads)
    run(2, begin_loads)
    run(1, begin_loads)
    begin_loads(z)
    pl.semaphore_wait(bar, 5 + jnp.where(zup & zdown, 1, 0))
    row_copy(0).start()
    run(3, begin_gives)
    run(2, begin_gives)

    def ready(cx, cy, q):
        chip = chip_of(cx, cy, q)
        load(chip).wait()
        give(chip).wait_recv()

        def step(s, _):
            total = acc[chip, s].astype(jnp.float32) + sib[chip, s].astype(jnp.float32)
            acc[chip, s] = total.astype(acc.dtype)
            return 0

        lax.fori_loop(0, slots, step, 0)

    def chip_of(cx, cy, cz):
        return (cz * 2 + cy) * 2 + cx

    def out_copy(cx, cy, cz, color, target, buf, index, sem):
        lo, n = span[color]
        chip = chip_of(cx, cy, cz)
        return pltpu.make_async_remote_copy(src_ref=acc.at[chip, pl.ds(lo, n)], dst_ref=buf.at[index, pl.ds(0, n)],
            send_sem=send_sem.at[chip, color], recv_sem=sem.at[index], device_id=(target,), device_id_type=MESH)

    def arrived(buf, index, sem, color):
        lo, n = span[color]
        pltpu.make_async_remote_copy(src_ref=acc.at[0, pl.ds(lo, n)], dst_ref=buf.at[index, pl.ds(0, n)],
            send_sem=send_sem.at[0, color], recv_sem=sem.at[index], device_id=(sibling,), device_id_type=MESH).wait_recv()

    def add(cx, cy, cz, color, pieces):
        lo, n = span[color]
        chip = chip_of(cx, cy, cz)
        for buf, index, sem in pieces:
            arrived(buf, index, sem, color)
        def step(s, _):
            total = acc[chip, lo + s].astype(jnp.float32)
            for buf, index, _sem in pieces:
                total = total + buf[index, s].astype(jnp.float32)
            acc[chip, lo + s] = total.astype(acc.dtype)
            return 0
        lax.fori_loop(0, n, step, 0)

    def X(i): return (xin, i, xsem)
    def Y(i): return (yin, i, ysem)
    def Z(i): return (zin, i, zsem)

    def term_x(q, color, i):
        cy = (y, y2)[i]
        out_copy(x2, cy, q, color, x_peer, xin, (8 if color == 2 else 0) + 2 * q + i, xsem).start()

    def term_y(q, color, i):
        cx = (x, x2)[i]
        out_copy(cx, y2, q, color, y_peer, yin, (8 if color == 2 else 0) + 2 * q + i, ysem).start()

    def term_a(q):
        ready(x2, y2, q)
        term_x(q, 1, 1)
        term_y(q, 0, 1)

    def term_c(q):

        @pl.when(is0)
        def _():
            term_y(q, 2, 1)
            term_y(q, 2, 0)

        @pl.when(is1)
        def _():
            term_x(q, 2, 1)
            term_x(q, 2, 0)

        ready(x, y, q)

    def term_b(q):
        ready(x2, y, q)
        term_x(q, 1, 0)
        ready(x, y2, q)
        term_y(q, 0, 0)

    def plane_two(q):
        @pl.when(is0)
        def _():
            add(x2, y, q, 2, [Y(8 + 2 * q + 1)])
            out_copy(x2, y, q, 2, x_peer, xin, 8 + 2 * q, xsem).start()
        @pl.when(is1)
        def _():
            add(x, y2, q, 2, [X(8 + 2 * q + 1)])
            out_copy(x, y2, q, 2, y_peer, yin, 8 + 2 * q, ysem).start()

    def column(part, q, sign, dist):
        target = up if sign == 1 else down
        more = zdown if sign == 1 else zup
        at_target = dist == 1
        base_out = (20 if (at_target and sign == 1) else 5 * q)
        kinds = (
            (0, x, y, 2, [X(8 + 2 * q), Y(8 + 2 * q)]),
            (1, x, y, 0, [Y(2 * q)]),
            (2, x, y, 1, [X(2 * q)]),
            (3, x2, y, 0, [Y(2 * q + 1)]),
            (4, x, y2, 1, [X(2 * q + 1)]),
        )
        for k, cx, cy, color, pieces in ((kinds[4], kinds[3], kinds[2], kinds[1]), (kinds[0],))[part]:
            @pl.when(more)
            def _():
                add(cx, cy, q, color, pieces + [Z(5 * q + k)])
            @pl.when(jnp.logical_not(more))
            def _():
                add(cx, cy, q, color, pieces)
            out_copy(cx, cy, q, color, target, zin, base_out + k, zsem).start()

    planes = functools.partial(column, 0)
    last = functools.partial(column, 1)
    run(3, term_a)
    run(3, term_b)
    run(3, term_c)
    row_step(0)
    run_signed(3, planes)
    run(2, term_a)
    run(2, term_b)
    run(2, term_c)
    run(3, plane_two)
    run(1, begin_gives)
    run_signed(3, last)
    run(1, term_a)
    run(1, term_b)
    run(1, term_c)
    row_step(1)
    run_signed(2, planes)
    begin_gives(z)
    run(2, plane_two)
    term_a(z)
    term_b(z)
    term_c(z)
    run_signed(2, last)
    row_step(2)
    run_signed(1, planes)
    run(1, plane_two)
    run_signed(1, last)
    row_step(3)
    plane_two(z)
    row_step(4)
    total_ref[...] = sums[10]

    def own(k, cx, cy, color, pieces):
        @pl.when(zup & zdown)
        def _():
            add(cx, cy, z, color, pieces + [Z(5 * z + k), Z(20 + k)])
        @pl.when(zup & jnp.logical_not(zdown))
        def _():
            add(cx, cy, z, color, pieces + [Z(5 * z + k)])
        @pl.when(zdown & jnp.logical_not(zup))
        def _():
            add(cx, cy, z, color, pieces + [Z(20 + k)])
    own(3, x2, y, 0, [Y(2 * z + 1)])
    out_copy(x2, y, z, 0, x_peer, xin, 16, xsem).start()
    own(4, x, y2, 1, [X(2 * z + 1)])
    out_copy(x, y2, z, 1, y_peer, yin, 16, ysem).start()
    own(0, x, y, 2, [X(8 + 2 * z), Y(8 + 2 * z)])
    own(1, x, y, 0, [Y(2 * z), X(16)])
    own(2, x, y, 1, [X(2 * z), Y(16)])
    pltpu.sync_copy(acc.at[chip_of(x, y, z)], out_ref)
    for chip in range(16):
        give(chip).wait_send()
        for color in range(3):
            @pl.when(chip != chip_of(x, y, z))
            def _():
                lo, n = span[color]
                pltpu.make_async_remote_copy(src_ref=acc.at[chip, pl.ds(lo, n)], dst_ref=xin.at[0, pl.ds(0, n)],
                    send_sem=send_sem.at[chip, color], recv_sem=xsem.at[0], device_id=(sibling,), device_id_type=MESH).wait_send()

def scatter_blocks(part, rows, cid=2):
    _, slots, height, feats = part.shape
    most = max(n for _, n in spans(slots))
    chunk = (most, height, feats)
    dt = part.dtype
    return pl.pallas_call(
        functools.partial(scatter_kernel, slots),
        out_shape=(
            jax.ShapeDtypeStruct(part.shape[1:], dt),
            jax.ShapeDtypeStruct(rows.shape, rows.dtype),
        ),
        in_specs=[pl.BlockSpec(memory_space=pl.ANY), pl.BlockSpec(memory_space=pltpu.VMEM)],
        out_specs=(pl.BlockSpec(memory_space=pl.ANY), pl.BlockSpec(memory_space=pltpu.VMEM)),
        scratch_shapes=[
            pltpu.VMEM((16, slots, height, feats), dt),
            pltpu.VMEM((16, slots, height, feats), dt),
            pltpu.VMEM((17,) + chunk, dt),
            pltpu.VMEM((17,) + chunk, dt),
            pltpu.VMEM((25,) + chunk, dt),
            pltpu.VMEM((11,) + rows.shape, rows.dtype),
            pltpu.SemaphoreType.DMA((16,)),
            pltpu.SemaphoreType.DMA((16,)),
            pltpu.SemaphoreType.DMA((16,)),
            pltpu.SemaphoreType.DMA((16, 3)),
            pltpu.SemaphoreType.DMA((17,)),
            pltpu.SemaphoreType.DMA((17,)),
            pltpu.SemaphoreType.DMA((25,)),
            pltpu.SemaphoreType.DMA((5,)),
            pltpu.SemaphoreType.DMA((5,)),
        ],
        compiler_params=pltpu.CompilerParams(collective_id=cid, has_side_effects=True, vmem_limit_bytes=58 * 2**20),
        name="scatter_blocks",
    )(part, rows)


ROW_TILE = 16
CHUNKS = 8
LANES = 128
VMEM_BYTES = 60 * 2**20


def rows_at(index, size=ROW_TILE):
    return pl.ds(pl.multiple_of(index * size, size), size)


def fetch_blocks(slot_ref, pool_ref, store_ref, sem, first_block, place, count):
    def step(b, carry):
        pltpu.make_async_copy(
            pool_ref.at[slot_ref[first_block + b]], store_ref.at[place + b], sem
        ).start()
        return carry

    lax.fori_loop(0, count, step, 0)


def await_blocks(pool_ref, store_ref, sem, place, count):
    pltpu.make_async_copy(
        pool_ref.at[pl.ds(0, count)], store_ref.at[pl.ds(place, count)], sem
    ).wait()


def times_weight(left_ref, store_ref, place, count, write, width=256):
    features = store_ref.shape[2]

    def step(n, carry):
        cols = pl.ds(pl.multiple_of(n * width, width), width)
        right = store_ref[place : place + count, :, cols].reshape(count * BLOCK_ROWS, width)
        write(cols, jnp.dot(left_ref[...], right, preferred_element_type=jnp.float32))
        return carry

    lax.fori_loop(0, features // width, step, 0)


def times_weight_back(left_ref, store_ref, place, count, write, width=256):
    blocks = width // BLOCK_ROWS

    def step(n, carry):
        cols = pl.ds(pl.multiple_of(n * width, width), width)
        right = store_ref[pl.ds(place + n * blocks, blocks)].reshape(width, store_ref.shape[2])
        write(cols, product_back(left_ref[...], right))
        return carry

    lax.fori_loop(0, count // blocks, step, 0)


def weight_gradient(left_ref, right_ref, own, slot_ref, grad_ref, stage, sems, first_block, width=256):
    blocks = width // BLOCK_ROWS
    steps = left_ref.shape[1] // width

    def drain(slot):
        pltpu.make_async_copy(stage.at[slot], grad_ref.at[pl.ds(0, blocks)], sems.at[slot]).wait()

    def step(n, carry):
        slot = lax.rem(n, 2)

        @pl.when(n >= 2)
        def _():
            drain(slot)

        cols = pl.ds(pl.multiple_of(n * width, width), width)
        piece = product_left(left_ref[0:own, cols], right_ref[0:own])
        stage[slot] = piece.astype(stage.dtype).reshape(stage.shape[1:])

        def put(b, inner):
            pltpu.make_async_copy(
                stage.at[slot, b],
                grad_ref.at[slot_ref[first_block + n * blocks + b]],
                sems.at[slot],
            ).start()
            return inner

        return lax.fori_loop(0, blocks, put, carry)

    lax.fori_loop(0, steps, step, 0)
    drain(0)
    drain(1)


def unit_norm(values):
    centered = values - jnp.mean(values, axis=1, keepdims=True)
    inverse = lax.rsqrt(jnp.mean(centered * centered, axis=1, keepdims=True) + NORM_EPS)
    return centered * inverse, inverse


def merge(first, second):
    top = jnp.maximum(first[2], second[2])
    one, two = jnp.exp(first[2] - top), jnp.exp(second[2] - top)
    return (one * first[0] + two * second[0], one * first[1] + two * second[1], top)


def aged(state, distance, alive, rate):
    return (state[0], state[1], jnp.where(alive > 0.5, state[2] - distance * rate, NEGATIVE))


def reset(state, start):
    cut = start > 0.5
    return (
        jnp.where(cut, 0.0, state[0]),
        jnp.where(cut, 0.0, state[1]),
        jnp.where(cut, NEGATIVE, state[2]),
    )


def advance(state, key, value, rate):
    older = state[2] - rate
    top = jnp.maximum(older, key)
    old, new = jnp.exp(older - top), jnp.exp(key - top)
    return (old * state[0] + new * value, old * state[1] + new, top)


def shift_in(ext, own):
    ext[0:8] = jnp.concatenate([ext[own + 10 : own + 11], ext[own : own + 7]], axis=0)


def halo_previous(ext, own, features):
    return jnp.concatenate(
        [
            ext[own + 7 : own + 8],
            ext[own + 8 : own + 9],
            ext[own + 11 : own + 12],
            jnp.zeros((ROW_TILE - 3, features), jnp.float32),
        ],
        axis=0,
    )


def normed_pair(ext, marks_ref, j):
    here = ext[pl.ds(pl.multiple_of(j * ROW_TILE + 8, 8), ROW_TILE)]
    before = ext[rows_at(j)] * marks_ref[rows_at(j), 1:2]
    return here, before


def over_tiles(tiles, work, halo):
    def step(j, carry):
        work(j)
        return carry

    lax.fori_loop(0, tiles - 1, step, 0)
    halo(tiles - 1)


def take_step(wide, first, length):
    at = pl.ds(first, CHUNKS, stride=length)
    return jnp.concatenate([wide[k, at] for k in range(wide.shape[0])], axis=1)


def put_step(wide, first, length, tile):
    at = pl.ds(first, CHUNKS, stride=length)
    lanes = wide.shape[2]
    for k in range(wide.shape[0]):
        wide[k, at] = tile[:, k * lanes : (k + 1) * lanes]


def take_rows(wide, at):
    return jnp.concatenate([wide[k, at] for k in range(wide.shape[0])], axis=1)


def put_rows(wide, at, tile):
    lanes = wide.shape[2]
    for k in range(wide.shape[0]):
        wide[k, at] = tile[:, k * lanes : (k + 1) * lanes]


def none_between(offsets, low, high):
    hit = None
    for offset in offsets:
        inside = (low <= offset) & (offset <= high)
        hit = inside if hit is None else hit | inside
    return jnp.where(hit, 0.0, 1.0)


def write_marks(doc_ref, marks_ref, chunk_ref, link_ref, flag_ref, own, devices):
    rows = marks_ref.shape[0]
    length = own // CHUNKS
    total = own * devices
    me = lax.axis_index("seq")
    first = me * own
    offsets = [jnp.int32(0)]
    for k in range(doc_ref.shape[0] - 1):
        offsets.append(offsets[-1] + doc_ref[k])
    row = lax.broadcasted_iota(jnp.int32, (rows, 1), 0)
    chunk, step = lax.rem(row, CHUNKS), row // CHUNKS
    extra = jnp.where(row < own + 2, row, own - 1 - (row - (own + 2)) - own)
    place = first + jnp.where(row < own, chunk * length + step, extra)
    inside = (place >= 0) & (place < total)
    keep = jnp.where(inside, none_between(offsets, place, place), 0.0)
    begin = first + chunk * length
    marks_ref[:, 0:1] = 1.0 - keep
    marks_ref[:, 1:2] = keep
    marks_ref[:, 2:3] = jnp.where(row < own, none_between(offsets, begin, place), 1.0)
    marks_ref[:, 3:4] = jnp.where(row < own, none_between(offsets, place + 1, begin + length - 1), 1.0)
    chunk = lax.broadcasted_iota(jnp.int32, (CHUNKS, 1), 0)
    begin = first + chunk * length
    end = begin + length - 1
    chunk_ref[:, 0:1] = none_between(offsets, begin, end)
    chunk_ref[:, 1:2] = jnp.where(first > 0, none_between(offsets, first - 1, begin - 1), 0.0)
    chunk_ref[:, 2:3] = none_between(offsets, begin, end - 1)
    chunk_ref[:, 3:4] = (1 + chunk * length).astype(jnp.float32)
    chunk_ref[:, 4:5] = jnp.where(first + own < total, none_between(offsets, end + 1, first + own), 0.0)
    chunk_ref[:, 5:6] = (1 + (CHUNKS - 1 - chunk) * length).astype(jnp.float32)
    count = link_ref.shape[0]
    group = devices // count
    span = own * group
    here = me // group
    other = lax.broadcasted_iota(jnp.int32, (count, 1), 0)
    link_ref[:, 0:1] = jnp.where(other < here, none_between(offsets, span * (other + 1) - 1, span * here - 2), 0.0)
    link_ref[:, 1:2] = (span * (here - 1 - other)).astype(jnp.float32)
    link_ref[:, 2:3] = jnp.where(other > here, none_between(offsets, span * (here + 1) + 1, span * other), 0.0)
    link_ref[:, 3:4] = (span * (other - here - 1)).astype(jnp.float32)
    pair = span * here + jnp.zeros((1, 1), jnp.int32)
    flag_ref[:, 0:1] = none_between(offsets, pair + own - 1, pair + 2 * own - 2)
    flag_ref[:, 1:2] = none_between(offsets, pair - 1, pair + own - 2)
    flag_ref[:, 2:3] = none_between(offsets, pair + 1, pair + own)
    flag_ref[:, 3:4] = none_between(offsets, pair + own + 1, pair + 2 * own)


def open_kernel(
    devices,
    slot_ref, doc_ref, tokens_ref, grads_ref, after_ref, after_grad_ref, before_ref, vec_ref, pool_ref,
    x_ref, grad_ref, marks_ref, chunk_ref, link_ref, flag_ref,
    key_ref, value_ref, recept_ref, num_ref, den_ref, max_ref, in_key, in_value, in_recept, prefix_ref, summary_ref,
    ext, wide, wide_grad, store, sem,
):
    rows, features = x_ref.shape
    own = rows - ROW_TILE
    tiles = rows // ROW_TILE
    length = own // CHUNKS
    per = EMBED_SIZE // BLOCK_ROWS
    for m in range(3):
        fetch_blocks(slot_ref, pool_ref, store, sem.at[m], m * per, m * per, per)
    write_marks(doc_ref, marks_ref, chunk_ref, link_ref, flag_ref, own, devices)
    me = lax.axis_index("seq")

    def widen(j, carry):
        put_rows(wide, rows_at(j), tokens_ref[rows_at(j)].astype(jnp.float32))
        put_rows(wide_grad, rows_at(j), grads_ref[rows_at(j)].astype(jnp.float32))
        return carry

    lax.fori_loop(0, tiles - 1, widen, 0)

    def norm(j, tile):
        x_ref[rows_at(j)] = tile.astype(jnp.bfloat16)
        unit, _ = unit_norm(tile)
        ext[pl.ds(pl.multiple_of(j * ROW_TILE + 8, 8), ROW_TILE)] = unit * vec_ref[0:1] + vec_ref[1:2]

    def arrange(j, carry):
        norm(j, jnp.concatenate([take_step(wide, 2 * j + k, length) for k in range(2)], axis=0))
        pair = [take_step(wide_grad, 2 * j + k, length) for k in range(2)]
        grad_ref[rows_at(j)] = jnp.concatenate(pair, axis=0).astype(jnp.bfloat16)
        return carry

    lax.fori_loop(0, tiles - 1, arrange, 0)
    more, less = me < devices - 1, me > 0
    later = jnp.where(more, after_ref[...].astype(jnp.float32), 0.0)[0:2]
    earlier = jnp.where(less, before_ref[...].astype(jnp.float32), 0.0)
    blank_rows = jnp.zeros((ROW_TILE - 4, features), jnp.float32)
    norm(
        tiles - 1,
        jnp.concatenate([later, earlier[ROW_TILE - 1 :], earlier[ROW_TILE - 2 : ROW_TILE - 1], blank_rows], axis=0),
    )
    later_grad = jnp.where(more, after_grad_ref[...].astype(jnp.float32), 0.0)[0:2]
    grad_ref[own:rows] = jnp.concatenate([later_grad, blank_rows, blank_rows[:2]], axis=0).astype(jnp.bfloat16)
    shift_in(ext, own)

    def mix(j, here, before):
        for row, ref in ((2, in_key), (3, in_value), (4, in_recept)):
            weight = vec_ref[row : row + 1]
            ref[rows_at(j)] = (weight * here + (1.0 - weight) * before).astype(jnp.bfloat16)

    def halo(j):
        here = ext[own + 8 : own + 8 + ROW_TILE]
        before = halo_previous(ext, own, features) * marks_ref[own:rows, 1:2]
        mix(j, here, before)

    over_tiles(tiles, lambda j: mix(j, *normed_pair(ext, marks_ref, j)), halo)
    for m, (left, out) in enumerate(((in_key, key_ref), (in_value, value_ref), (in_recept, recept_ref))):
        await_blocks(pool_ref, store, sem.at[m], m * per, per)

        def write(cols, piece, out=out):
            out[:, cols] = piece

        times_weight(left, store, m * per, per, write)
    rate = jnp.exp(vec_ref[5:6])

    def token(i, state, key, value):
        state = reset(state, marks_ref[rows_at(i, CHUNKS), 0:1])
        num_ref[rows_at(i, CHUNKS)], den_ref[rows_at(i, CHUNKS)], max_ref[rows_at(i, CHUNKS)] = state
        return advance(state, key, value, rate)

    def step(i, state):
        return token(i, state, key_ref[rows_at(i, CHUNKS)], value_ref[rows_at(i, CHUNKS)])

    blank = jnp.zeros((CHUNKS, features), jnp.float32)
    state = lax.fori_loop(0, length - 1, step, (blank, blank, blank + NEGATIVE))
    late = tuple(item[CHUNKS - 1 :] for item in state)
    ends = step(length - 1, state)
    prior = (value_ref[own + 2 : own + 3], jnp.ones((1, features), jnp.float32), key_ref[own + 2 : own + 3])
    for c in range(CHUNKS):
        for k in range(3):
            prefix_ref[k, c : c + 1] = prior[k]
        if c < CHUNKS - 1:
            old = aged(prior, float(length), chunk_ref[c : c + 1, 0:1], rate)
            prior = merge(tuple(item[c : c + 1] for item in ends), old)
    last = merge(late, aged(prior, float(length - 1), chunk_ref[CHUNKS - 1 :, 2:3], rate))
    summary_ref[...] = jnp.concatenate(last, axis=0)


def open_pass(devices, slots, doc_lengths, tokens_in, out_grad, halo, vectors, pool):
    own, features = tokens_in.shape
    rows = own + ROW_TILE
    count = devices // 2 if devices == GRID_DEVICES else devices
    full = jax.ShapeDtypeStruct((rows, features), jnp.float32)
    part = jax.ShapeDtypeStruct((own, features), jnp.float32)
    low = jax.ShapeDtypeStruct((rows, features), jnp.bfloat16)
    small = lambda *shape: jax.ShapeDtypeStruct(shape, jnp.float32)
    vmem = pl.BlockSpec(memory_space=pltpu.VMEM)
    smem = pl.BlockSpec(memory_space=pltpu.SMEM)
    return pl.pallas_call(
        functools.partial(open_kernel, devices),
        out_shape=(
            low, low, small(rows, 4), small(CHUNKS, 6), small(count, 4), small(1, 4),
            full, full, full, part, part, part, low, low, low, small(3, CHUNKS, features), small(3, features),
        ),
        in_specs=[smem] * 2 + [vmem] * 6 + [pl.BlockSpec(memory_space=pl.ANY)],
        out_specs=(vmem,) * 17,
        scratch_shapes=[
            pltpu.VMEM((rows + 8, features), jnp.float32),
            pltpu.VMEM((features // LANES, own, LANES), jnp.float32),
            pltpu.VMEM((features // LANES, own, LANES), jnp.float32),
            pltpu.VMEM((3 * EMBED_SIZE // BLOCK_ROWS, BLOCK_ROWS, features), jnp.bfloat16),
            pltpu.SemaphoreType.DMA((3,)),
        ],
        compiler_params=pltpu.CompilerParams(vmem_limit_bytes=VMEM_BYTES),
        name="open_pass",
    )(slots, doc_lengths, tokens_in, out_grad, *halo, vectors, pool)


def middle_kernel(
    slot_ref, x_ref, grad_ref, vec_ref, marks_ref, chunk_ref, incoming_ref, prefix_ref,
    key_ref, value_ref, recept_ref, num_ref, den_ref, max_ref, pool_ref,
    layer_ref, resid_grad, wkv, gw, full_num, full_den, full_max, own_share, back_num, back_den, back_max,
    recept_grad, suffix_ref, summary_ref, sums_ref, slot_grad,
    mixed, ext, unit, inverse, low_key, low_recept, hidden, squared, value_acc, gate, gcv, gcg, hidden_grad,
    attn_grad, top_log, wide, store, stage, sem, stage_sem,
):
    rows, features = x_ref.shape
    own = rows - ROW_TILE
    tiles = rows // ROW_TILE
    length = own // CHUNKS
    per = EMBED_SIZE // BLOCK_ROWS
    ff = FF // BLOCK_ROWS
    at_out, at_recept, at_key, at_value = 0, per, 2 * per, 2 * per + ff
    fetch_blocks(slot_ref, pool_ref, store, sem.at[0], 3 * per, at_out, per)
    fetch_blocks(slot_ref, pool_ref, store, sem.at[1], 5 * per, at_key, ff)
    fetch_blocks(slot_ref, pool_ref, store, sem.at[2], 5 * per + ff, at_value, ff)
    fetch_blocks(slot_ref, pool_ref, store, sem.at[3], 4 * per, at_recept, per)
    rate = jnp.exp(vec_ref[5:6])
    bonus = vec_ref[6:7]
    incoming = tuple(incoming_ref[k : k + 1] for k in range(3))
    carry = merge(
        tuple(prefix_ref[k] for k in range(3)),
        aged(tuple(jnp.broadcast_to(v, (CHUNKS, features)) for v in incoming), chunk_ref[:, 3:4], chunk_ref[:, 1:2], rate),
    )

    def attend(j, size, state, key, value, recept):
        own_log = bonus + key
        top = jnp.maximum(state[2], own_log)
        old, new = jnp.exp(state[2] - top), jnp.exp(own_log - top)
        scale = 1.0 / (old * state[1] + new)
        out = (old * state[0] + new * value) * scale
        wkv[rows_at(j, size)] = out
        own_share[rows_at(j, size)] = new * scale
        top_log[rows_at(j, size)] = top
        value_acc[rows_at(j, size)] = scale
        ext[rows_at(j, size)] = jax.nn.sigmoid(recept) * out

    def attend_step(i, state_carry):
        at = rows_at(i, CHUNKS)
        alive = marks_ref[at, 2:3]
        distance = jnp.float32(i) if isinstance(i, int) else i.astype(jnp.float32)
        state = merge((num_ref[at], den_ref[at], max_ref[at]), aged(carry, distance, alive, rate))
        full_num[at], full_den[at], full_max[at] = state
        attend(i, CHUNKS, state, key_ref[at], value_ref[at], recept_ref[at])
        return state_carry

    lax.fori_loop(0, length, attend_step, 0)

    def row(ref, r):
        return ref[r : r + 1]

    end = advance(
        (row(full_num, own - 1), row(full_den, own - 1), row(full_max, own - 1)),
        row(key_ref, own - 1), row(value_ref, own - 1), rate,
    )
    halo_one = reset(end, marks_ref[own : own + 1, 0:1])
    halo_two = reset(
        advance(halo_one, row(key_ref, own), row(value_ref, own), rate), marks_ref[own + 1 : own + 2, 0:1]
    )
    halo_zero = reset(incoming, marks_ref[own + 2 : own + 3, 0:1])
    rest = jnp.zeros((ROW_TILE - 3, features), jnp.float32)
    halo_state = tuple(
        jnp.concatenate([halo_one[k], halo_two[k], halo_zero[k], rest + (NEGATIVE if k == 2 else 0.0)], axis=0)
        for k in range(3)
    )
    attend(tiles - 1, ROW_TILE, halo_state, key_ref[own:rows], value_ref[own:rows], recept_ref[own:rows])

    def pack(j, c):
        mixed[rows_at(j)] = ext[rows_at(j)].astype(jnp.bfloat16)
        back_num[rows_at(j)] = value_acc[rows_at(j)]
        return c

    lax.fori_loop(0, tiles, pack, 0)
    await_blocks(pool_ref, store, sem.at[0], at_out, per)

    def write_resid(cols, piece):
        unit[:, cols] = x_ref[:, cols].astype(jnp.float32) + piece

    times_weight(mixed, store, at_out, per, write_resid)

    def norm(j, c):
        resid = unit[rows_at(j)]
        resid_grad[rows_at(j)] = resid
        out, inv = unit_norm(resid)
        unit[rows_at(j)] = out
        inverse[rows_at(j)] = inv
        ext[pl.ds(pl.multiple_of(j * ROW_TILE + 8, 8), ROW_TILE)] = out * vec_ref[7:8] + vec_ref[8:9]
        return c

    lax.fori_loop(0, tiles, norm, 0)
    shift_in(ext, own)

    def mix(j, here, before):
        for r, ref in ((9, low_key), (10, low_recept)):
            weight = vec_ref[r : r + 1]
            ref[rows_at(j)] = (weight * here + (1.0 - weight) * before).astype(jnp.bfloat16)

    def halo_pair():
        here = ext[own + 8 : own + 8 + ROW_TILE]
        return here, halo_previous(ext, own, features) * marks_ref[own:rows, 1:2]

    over_tiles(tiles, lambda j: mix(j, *normed_pair(ext, marks_ref, j)), lambda j: mix(j, *halo_pair()))

    await_blocks(pool_ref, store, sem.at[1], at_key, ff)

    def write_hidden(cols, piece):
        up = jnp.maximum(piece, 0.0)
        hidden[:, cols] = up
        squared[:, cols] = (up * up).astype(jnp.bfloat16)

    times_weight_back(low_key, store, at_key, ff, write_hidden)
    await_blocks(pool_ref, store, sem.at[2], at_value, ff)

    def write_value(cols, piece):
        value_acc[:, cols] = piece

    times_weight(squared, store, at_value, ff, write_value)
    await_blocks(pool_ref, store, sem.at[3], at_recept, per)

    def write_gate(cols, piece):
        gate[:, cols] = piece

    times_weight(low_recept, store, at_recept, per, write_gate)

    def finish(j, c):
        at = rows_at(j)
        opened = jax.nn.sigmoid(gate[at])
        value = value_acc[at]
        out = resid_grad[at] + opened * value

        @pl.when(j < tiles - 1)
        def _():
            for k in range(2):
                put_step(wide, 2 * j + k, length, out[8 * k : 8 * k + 8])

        grad = grad_ref[at].astype(jnp.float32) * opened
        gcv[at] = grad.astype(jnp.bfloat16)
        gcg[at] = (grad * value * (1.0 - opened)).astype(jnp.bfloat16)
        return c

    lax.fori_loop(0, tiles, finish, 0)

    def emit(j, c):
        layer_ref[rows_at(j)] = take_rows(wide, rows_at(j)).astype(jnp.bfloat16)
        return c

    lax.fori_loop(0, tiles - 1, emit, 0)

    def write_hidden_grad(cols, piece):
        hidden_grad[:, cols] = (piece * (2.0 * hidden[:, cols])).astype(jnp.bfloat16)

    times_weight_back(gcv, store, at_value, ff, write_hidden_grad)
    weight_gradient(squared, gcv, own, slot_ref, slot_grad, stage, stage_sem, 5 * per + ff)
    weight_gradient(hidden_grad, low_key, own, slot_ref, slot_grad, stage, stage_sem, 5 * per)
    weight_gradient(low_recept, gcg, own, slot_ref, slot_grad, stage, stage_sem, 4 * per)
    times_weight(hidden_grad, store, at_key, ff, write_value)
    times_weight_back(gcg, store, at_recept, per, write_gate)
    carried = hidden.at[:, 0:features]
    mix_key, mix_recept = vec_ref[9:10], vec_ref[10:11]

    def carry_over(j, c):
        at = rows_at(j)
        carried[at] = marks_ref[at, 1:2] * ((1.0 - mix_key) * value_acc[at] + (1.0 - mix_recept) * gate[at])
        return c

    lax.fori_loop(0, tiles, carry_over, 0)
    halo_next = jnp.concatenate(
        [carried[own + 1 : own + 2], jnp.zeros((ROW_TILE - 1, features), jnp.float32)], axis=0
    )
    carried[own : own + 8] = jnp.concatenate([carried[1:8], carried[own : own + 1]], axis=0)

    def norm_back(j, following):
        at = rows_at(j)
        grad = mix_key * value_acc[at] + mix_recept * gate[at] + following
        scaled = grad * vec_ref[7:8]
        inner = (
            scaled
            - jnp.mean(scaled, axis=1, keepdims=True)
            - unit[at] * jnp.mean(scaled * unit[at], axis=1, keepdims=True)
        )
        total = grad_ref[at].astype(jnp.float32) + inner * inverse[at]
        resid_grad[at] = total
        attn_grad[at] = total.astype(jnp.bfloat16)
        return grad

    def fold(piece):
        return piece[:8] + piece[8:]

    def back_step(j, sums):
        at = rows_at(j)
        grad = norm_back(j, carried[pl.ds(pl.multiple_of(j * ROW_TILE + 8, 8), ROW_TILE)])
        here, before = normed_pair(ext, marks_ref, j)
        spread = here - before
        return (
            sums[0] + fold(grad * unit[at]),
            sums[1] + fold(grad),
            sums[2] + fold(value_acc[at] * spread),
            sums[3] + fold(gate[at] * spread),
        )

    blank = jnp.zeros((CHUNKS, features), jnp.float32)
    sums = lax.fori_loop(0, tiles - 1, back_step, (blank,) * 4)
    for k in range(4):
        sums_ref[k : k + 1] = jnp.sum(sums[k], axis=0, keepdims=True)
    norm_back(tiles - 1, halo_next)

    weight_gradient(mixed, attn_grad, own, slot_ref, slot_grad, stage, stage_sem, 3 * per)
    times_weight_back(attn_grad, store, at_out, per, write_gate)

    def gate_back(j, c):
        at = rows_at(j)
        opened = jax.nn.sigmoid(recept_ref[at])
        grad = gate[at] * opened
        gw[at] = grad
        recept_grad[at] = (grad * wkv[at] * (1.0 - opened)).astype(jnp.bfloat16)
        ext[at] = grad * back_num[at]
        return c

    lax.fori_loop(0, tiles, gate_back, 0)

    def back_token(state, share, out, top, start):
        older = state[2] - rate
        high = jnp.maximum(older, -top)
        old, new = jnp.exp(older - high), jnp.exp(-top - high)
        return reset((old * state[0] + new * share, old * state[1] - new * share * out, high), start)

    def back_scan(n, state):
        i = length - 1 - n
        at = rows_at(i, CHUNKS)
        back_num[at], back_den[at], back_max[at] = state
        return back_token(state, ext[at], wkv[at], top_log[at], marks_ref[at, 0:1])

    heads = lax.fori_loop(0, length, back_scan, (blank, blank, blank + NEGATIVE))
    for ref in (back_num, back_den, back_max):
        ref[own:rows] = jnp.zeros((ROW_TILE, features), jnp.float32)
    nothing = jnp.zeros((1, features), jnp.float32)
    after = back_token(
        (nothing, nothing, nothing + NEGATIVE),
        row(ext, own), row(wkv, own), row(top_log, own), marks_ref[own : own + 1, 0:1],
    )
    for c in range(CHUNKS - 1, -1, -1):
        for k in range(3):
            suffix_ref[k, c : c + 1] = after[k]
        if c > 0:
            old = aged(after, float(length), chunk_ref[c : c + 1, 0:1], rate)
            after = merge(tuple(item[c : c + 1] for item in heads), old)
    first = (row(back_num, 0), row(back_den, 0), row(back_max, 0))
    last = merge(first, aged(after, float(length - 1), marks_ref[0:1, 3:4], rate))
    summary_ref[...] = jnp.concatenate(last, axis=0)


def middle_pass(slots, x_rows, grad_rows, vectors, marks, chunk_marks, incoming, opened, pool):
    key, value, recept, num, den, top, prefix = opened
    rows, features = x_rows.shape
    own = rows - ROW_TILE
    full = jax.ShapeDtypeStruct((rows, features), jnp.float32)
    part = jax.ShapeDtypeStruct((own, features), jnp.float32)
    low = jax.ShapeDtypeStruct((rows, features), jnp.bfloat16)
    vmem = pl.BlockSpec(memory_space=pltpu.VMEM)
    anywhere = pl.BlockSpec(memory_space=pl.ANY)
    f32 = lambda *shape: pltpu.VMEM(shape, jnp.float32)
    b16 = lambda *shape: pltpu.VMEM(shape, jnp.bfloat16)
    return pl.pallas_call(
        middle_kernel,
        out_shape=(
            jax.ShapeDtypeStruct((own, features), jnp.bfloat16),
            full, full, full, part, part, part, full, full, full, full, low,
            jax.ShapeDtypeStruct((3, CHUNKS, features), jnp.float32),
            jax.ShapeDtypeStruct((3, features), jnp.float32),
            jax.ShapeDtypeStruct((4, features), jnp.float32),
            jax.ShapeDtypeStruct(pool.shape, jnp.bfloat16),
        ),
        in_specs=[pl.BlockSpec(memory_space=pltpu.SMEM)] + [vmem] * 13 + [anywhere],
        out_specs=(vmem,) * 15 + (anywhere,),
        scratch_shapes=[
            b16(rows, features),
            f32(rows + 8, features),
            f32(rows, features),
            f32(rows, 1),
            b16(rows, features),
            b16(rows, features),
            f32(rows, FF),
            b16(rows, FF),
            f32(rows, features),
            f32(rows, features),
            b16(rows, features),
            b16(rows, features),
            b16(rows, FF),
            b16(rows, features),
            f32(rows, features),
            f32(features // LANES, own, LANES),
            b16((2 * EMBED_SIZE + 2 * FF) // BLOCK_ROWS, BLOCK_ROWS, features),
            b16(2, 256 // BLOCK_ROWS, BLOCK_ROWS, features),
            pltpu.SemaphoreType.DMA((4,)),
            pltpu.SemaphoreType.DMA((2,)),
        ],
        compiler_params=pltpu.CompilerParams(vmem_limit_bytes=VMEM_BYTES),
        name="middle_pass",
    )(slots, x_rows, grad_rows, vectors, marks, chunk_marks, incoming, prefix, key, value, recept, num, den, top, pool)


def close_kernel(
    slot_ref, x_ref, vec_ref, marks_ref, chunk_ref, incoming_ref, suffix_ref, key_ref, value_ref,
    in_key, in_value, in_recept, resid_grad, wkv, gw, full_num, full_den, full_max, own_share,
    back_num, back_den, back_max, recept_grad, sums_two_ref, pool_ref, grads_in,
    input_ref, sums_ref, slot_grad,
    ext, unit, inverse, key_wide, value_wide, key_grad, value_grad, grad_key_in, grad_value_in, grad_recept_in,
    carried, wide, store, stage, sem, stage_sem,
):
    rows, features = x_ref.shape
    own = rows - ROW_TILE
    tiles = rows // ROW_TILE
    length = own // CHUNKS
    per = EMBED_SIZE // BLOCK_ROWS
    for m in range(3):
        fetch_blocks(slot_ref, pool_ref, store, sem.at[m], m * per, m * per, per)
    rate = jnp.exp(vec_ref[5:6])
    incoming = tuple(incoming_ref[k : k + 1] for k in range(3))
    carry = merge(
        tuple(suffix_ref[k] for k in range(3)),
        aged(tuple(jnp.broadcast_to(v, (CHUNKS, features)) for v in incoming), chunk_ref[:, 5:6], chunk_ref[:, 4:5], rate),
    )

    def spread_back(state, key, value, share, grad, out):
        direct = share * grad
        bonus_grad = direct * (value - out)
        lift = jnp.exp(key + state[2])
        return bonus_grad + lift * (state[0] * value + state[1]), direct + lift * state[0], bonus_grad

    def token(i, sums):
        at = rows_at(i, CHUNKS)
        distance = (length - 1 - i).astype(jnp.float32)
        state = merge((back_num[at], back_den[at], back_max[at]), aged(carry, distance, marks_ref[at, 3:4], rate))
        key_g, value_g, bonus_grad = spread_back(state, key_ref[at], value_ref[at], own_share[at], gw[at], wkv[at])
        key_wide[at] = key_g
        value_wide[at] = value_g
        fade = jnp.exp(state[2] + full_max[at] - rate) * (state[0] * full_num[at] + state[1] * full_den[at])
        return sums[0] + fade, sums[1] + bonus_grad

    blank = jnp.zeros((CHUNKS, features), jnp.float32)
    fade, bonus_sum = lax.fori_loop(0, length, token, (blank, blank))
    sums_ref[5:6] = -rate * jnp.sum(fade, axis=0, keepdims=True)
    sums_ref[6:7] = jnp.sum(bonus_sum, axis=0, keepdims=True)
    halo = tuple(
        jnp.concatenate([incoming[k], jnp.zeros((ROW_TILE - 1, features), jnp.float32) + (NEGATIVE if k == 2 else 0.0)], axis=0)
        for k in range(3)
    )
    key_g, value_g, _ = spread_back(
        halo, key_ref[own:rows], value_ref[own:rows], own_share[own:rows], gw[own:rows], wkv[own:rows]
    )
    key_wide[own:rows] = key_g
    value_wide[own:rows] = value_g

    def pack(j, c):
        at = rows_at(j)
        key_grad[at] = key_wide[at].astype(jnp.bfloat16)
        value_grad[at] = value_wide[at].astype(jnp.bfloat16)
        return c

    lax.fori_loop(0, tiles, pack, 0)
    weight_gradient(in_recept, recept_grad, own, slot_ref, slot_grad, stage, stage_sem, 2 * per)
    weight_gradient(in_key, key_grad, own, slot_ref, slot_grad, stage, stage_sem, 0)
    weight_gradient(in_value, value_grad, own, slot_ref, slot_grad, stage, stage_sem, per)
    for m, (left, out) in enumerate(((key_grad, grad_key_in), (value_grad, grad_value_in), (recept_grad, grad_recept_in))):
        await_blocks(pool_ref, store, sem.at[m], m * per, per)

        def write(cols, piece, out=out):
            out[:, cols] = piece

        times_weight_back(left, store, m * per, per, write)

    def norm(j, c):
        out, inv = unit_norm(x_ref[rows_at(j)].astype(jnp.float32))
        unit[rows_at(j)] = out
        inverse[rows_at(j)] = inv
        ext[pl.ds(pl.multiple_of(j * ROW_TILE + 8, 8), ROW_TILE)] = out * vec_ref[0:1] + vec_ref[1:2]
        return c

    lax.fori_loop(0, tiles, norm, 0)
    shift_in(ext, own)
    mixes = tuple(vec_ref[k : k + 1] for k in (2, 3, 4))

    def carry_over(j, c):
        at = rows_at(j)
        total = (1.0 - mixes[0]) * grad_key_in[at] + (1.0 - mixes[1]) * grad_value_in[at] + (1.0 - mixes[2]) * grad_recept_in[at]
        carried[at] = marks_ref[at, 1:2] * total
        return c

    lax.fori_loop(0, tiles, carry_over, 0)
    carried[own : own + 8] = jnp.concatenate([carried[1:8], carried[own : own + 1]], axis=0)

    def fold(piece):
        return piece[:8] + piece[8:]

    def back_step(j, sums):
        at = rows_at(j)
        grads = (grad_key_in[at], grad_value_in[at], grad_recept_in[at])
        grad = carried[pl.ds(pl.multiple_of(j * ROW_TILE + 8, 8), ROW_TILE)]
        for weight, piece in zip(mixes, grads):
            grad = grad + weight * piece
        scaled = grad * vec_ref[0:1]
        inner = (
            scaled
            - jnp.mean(scaled, axis=1, keepdims=True)
            - unit[at] * jnp.mean(scaled * unit[at], axis=1, keepdims=True)
        )
        out = resid_grad[at] + inner * inverse[at]
        for k in range(2):
            put_step(wide, 2 * j + k, length, out[8 * k : 8 * k + 8])
        here, before = normed_pair(ext, marks_ref, j)
        spread = here - before
        return (sums[0] + fold(grad * unit[at]), sums[1] + fold(grad)) + tuple(
            s + fold(piece * spread) for s, piece in zip(sums[2:], grads)
        )

    sums = lax.fori_loop(0, tiles - 1, back_step, (blank,) * 5)
    for k in range(5):
        sums_ref[k : k + 1] = jnp.sum(sums[k], axis=0, keepdims=True)
    sums_ref[7:] = sums_two_ref[...]

    def emit(j, c):
        input_ref[rows_at(j)] = take_rows(wide, rows_at(j))
        return c

    lax.fori_loop(0, tiles - 1, emit, 0)


def close_pass(slots, x_rows, vectors, marks, chunk_marks, incoming, suffix, key, value, lows, kept, pool, slot_grad):
    rows, features = x_rows.shape
    own = rows - ROW_TILE
    vmem = pl.BlockSpec(memory_space=pltpu.VMEM)
    anywhere = pl.BlockSpec(memory_space=pl.ANY)
    f32 = lambda *shape: pltpu.VMEM(shape, jnp.float32)
    b16 = lambda *shape: pltpu.VMEM(shape, jnp.bfloat16)
    operands = (slots, x_rows, vectors, marks, chunk_marks, incoming, suffix, key, value) + lows + kept + (pool, slot_grad)
    return pl.pallas_call(
        close_kernel,
        out_shape=(
            jax.ShapeDtypeStruct((own, features), jnp.float32),
            jax.ShapeDtypeStruct(vectors.shape, jnp.float32),
            jax.ShapeDtypeStruct(pool.shape, jnp.bfloat16),
        ),
        in_specs=[pl.BlockSpec(memory_space=pltpu.SMEM)] + [vmem] * (len(operands) - 3) + [anywhere] * 2,
        out_specs=(vmem, vmem, anywhere),
        input_output_aliases={len(operands) - 1: 2},
        scratch_shapes=[
            f32(rows + 8, features),
            f32(rows, features),
            f32(rows, 1),
            f32(rows, features),
            f32(rows, features),
            b16(rows, features),
            b16(rows, features),
            f32(rows, features),
            f32(rows, features),
            f32(rows, features),
            f32(rows, features),
            f32(features // LANES, own, LANES),
            b16(3 * EMBED_SIZE // BLOCK_ROWS, BLOCK_ROWS, features),
            b16(2, 256 // BLOCK_ROWS, BLOCK_ROWS, features),
            pltpu.SemaphoreType.DMA((3,)),
            pltpu.SemaphoreType.DMA((2,)),
        ],
        compiler_params=pltpu.CompilerParams(vmem_limit_bytes=VMEM_BYTES),
        name="close_pass",
    )(*operands)


def chain_kernel(forward, tokens, own_ref, vec_ref, link_ref, flag_ref, out_ref, near, chips, joint, send_sem, recv_sem):
    me, core, _, _, _ = grid_place()
    chip = me // 2
    count = GRID_DEVICES // 2
    sign = 1 if forward else -1
    before = chip if forward else count - 1 - chip
    sibling = me + 1 - 2 * core
    chips[...] = jnp.zeros_like(chips)
    bar = pltpu.get_barrier_semaphore()
    pl.semaphore_signal(bar, inc=1, device_id=(sibling,), device_id_type=MESH)
    for o in range(1, count):
        @pl.when(o <= before)
        def _():
            pl.semaphore_signal(bar, inc=1, device_id=(me - 2 * sign * o,), device_id_type=MESH)
    pl.semaphore_wait(bar, count - before)
    swap = pltpu.make_async_remote_copy(
        src_ref=own_ref, dst_ref=near, send_sem=send_sem.at[0], recv_sem=recv_sem.at[0],
        device_id=(sibling,), device_id_type=MESH,
    )
    swap.start()
    rate = jnp.exp(vec_ref[5:6])
    at = 0 if forward else 2
    swap.wait()
    mine = tuple(own_ref[k : k + 1] for k in range(3))
    other = tuple(near[k : k + 1] for k in range(3))
    second = (core == 1) if forward else (core == 0)
    one = tuple(jnp.where(second, b, a) for a, b in zip(mine, other))
    two = tuple(jnp.where(second, a, b) for a, b in zip(mine, other))
    joint[...] = jnp.concatenate(merge(two, aged(one, float(tokens), flag_ref[0:1, at : at + 1], rate)), axis=0)

    def copy(o, place, peer):
        return pltpu.make_async_remote_copy(
            src_ref=joint, dst_ref=chips.at[place], send_sem=send_sem.at[o], recv_sem=recv_sem.at[o],
            device_id=(peer,), device_id_type=MESH,
        )

    for o in range(1, count):
        @pl.when(o < count - before)
        def _():
            copy(o, chip, me + 2 * sign * o).start()
    for o in range(1, count):
        @pl.when(o <= before)
        def _():
            copy(o, chip - sign * o, sibling).wait_recv()
    logs = jnp.where(link_ref[:, at : at + 1] > 0.5, chips[:, 2] - link_ref[:, at + 1 : at + 2] * rate, NEGATIVE)
    top = jnp.max(logs, axis=0, keepdims=True)
    weight = jnp.exp(logs - top)
    prior = (
        jnp.sum(weight * chips[:, 0], axis=0, keepdims=True),
        jnp.sum(weight * chips[:, 1], axis=0, keepdims=True),
        top,
    )
    beside = merge(one, aged(prior, float(tokens), flag_ref[0:1, at + 1 : at + 2], rate))
    out_ref[...] = jnp.concatenate([jnp.where(second, b, a) for a, b in zip(prior, beside)], axis=0)
    for o in range(1, count):
        @pl.when(o < count - before)
        def _():
            copy(o, chip, me + 2 * sign * o).wait_send()


def chain_state(rows, vectors, links, flags, forward, tokens, cid):
    devices = lax.axis_size("seq")
    if devices != GRID_DEVICES:
        every = lax.all_gather(rows[None], "seq", axis=0, tiled=True)
        at = 0 if forward else 2
        aged_logs = every[:, 2] - links[:, at + 1 : at + 2] * jnp.exp(vectors[5])
        logs = jnp.where(links[:, at : at + 1] > 0.5, aged_logs, NEGATIVE)
        top = jnp.max(logs, axis=0)
        weight = jnp.exp(logs - top)
        return jnp.stack([jnp.sum(weight * every[:, 0], axis=0), jnp.sum(weight * every[:, 1], axis=0), top])
    count = devices // 2
    vmem = pl.BlockSpec(memory_space=pltpu.VMEM)
    return pl.pallas_call(
        functools.partial(chain_kernel, forward, tokens),
        out_shape=jax.ShapeDtypeStruct(rows.shape, jnp.float32),
        in_specs=[vmem] * 4,
        out_specs=vmem,
        scratch_shapes=[
            pltpu.VMEM(rows.shape, jnp.float32),
            pltpu.VMEM((count,) + rows.shape, jnp.float32),
            pltpu.VMEM(rows.shape, jnp.float32),
            pltpu.SemaphoreType.DMA((count,)),
            pltpu.SemaphoreType.DMA((count,)),
        ],
        compiler_params=pltpu.CompilerParams(collective_id=cid, has_side_effects=True),
        name="chain_forward" if forward else "chain_backward",
    )(rows, vectors, links, flags)


def body(
    tokens_in,
    cotangent,
    pad_mask,
    doc_lengths,
    masters,
    moment_one,
    moment_two,
    block_slot,
    vectors,
    vector_one,
    vector_two,
):
    tokens, features = tokens_in.shape
    devices = lax.axis_size("seq")
    device_place = lax.axis_index("seq")
    owned_rows = masters.astype(jnp.bfloat16)
    out_grad = cotangent * pad_mask.astype(cotangent.dtype)[:, None]
    if devices == GRID_DEVICES:
        gathered, *halo = gather_blocks(owned_rows, tokens_in, out_grad)
        gathered = gathered.reshape(-1, BLOCK_ROWS, features)
    else:
        gathered = lax.all_gather(owned_rows, "seq", axis=0, tiled=True)
        halo = [
            shifted(tokens_in[:ROW_TILE], "seq", -1),
            shifted(out_grad[:ROW_TILE], "seq", -1),
            shifted(tokens_in[tokens - ROW_TILE :], "seq", 1),
        ]
    (
        x_rows, grad_rows, marks, chunk_marks, links, flags,
        key, value, recept, num, den, top, in_key, in_value, in_recept, prefix, summary,
    ) = open_pass(devices, block_slot, doc_lengths, tokens_in, out_grad, halo, vectors, gathered)
    incoming = chain_state(summary, vectors, links, flags, True, tokens, 3)
    (
        layer_out, resid_grad, wkv, gw, full_num, full_den, full_max, own_share, back_num, back_den, back_max,
        recept_grad, suffix, back_summary, sums_two, slot_grad,
    ) = middle_pass(
        block_slot, x_rows, grad_rows, vectors, marks, chunk_marks, incoming,
        (key, value, recept, num, den, top, prefix), gathered,
    )
    back_incoming = chain_state(back_summary, vectors, links, flags, False, tokens, 4)
    input_grad, stacked, slot_grad = close_pass(
        block_slot, x_rows, vectors, marks, chunk_marks, back_incoming, suffix, key, value,
        (in_key, in_value, in_recept),
        (resid_grad, wkv, gw, full_num, full_den, full_max, own_share, back_num, back_den, back_max, recept_grad, sums_two),
        gathered, slot_grad,
    )
    own_slots = device_place * masters.shape[0] + jnp.arange(masters.shape[0], dtype=jnp.int32)
    named = jnp.any(own_slots[:, None] == block_slot[None, :], axis=1)
    if devices == GRID_DEVICES:
        owner_grad, vector_grad = scatter_blocks(slot_grad.reshape((devices,) + masters.shape), stacked)
        owner_grad = owner_grad.astype(jnp.float32)
    else:
        owner_grad = lax.psum_scatter(
            slot_grad.astype(jnp.float32), "seq", scatter_dimension=0, tiled=True
        )
        vector_grad = lax.psum(stacked, "seq")
    owner_grad = jnp.where(named[:, None, None], owner_grad, 0.0)
    new_one, new_two, new_master = adam_update(
        masters, moment_one, moment_two, owner_grad, MATRIX_RATE, WEIGHT_DECAY
    )
    vector_rates = jnp.array(VECTOR_RATE, jnp.float32)[:, None]
    vector_first, vector_second, vector_next = adam_update(
        vectors, vector_one, vector_two, vector_grad, vector_rates, 0.0
    )
    return (
        layer_out,
        input_grad,
        new_one,
        new_two,
        new_master,
        vector_first,
        vector_second,
        vector_next,
    )


def solution(mesh):
    placed = (
        P("seq", None),
        P("seq", None),
        P("seq"),
        P(),
        P("seq", None, None),
        P("seq", None, None),
        P("seq", None, None),
        P(),
        P(),
        P(),
        P(),
    )
    return jax.shard_map(
        body,
        mesh=mesh,
        in_specs=placed,
        out_specs=(
            P("seq", None),
            P("seq", None),
            P("seq", None, None),
            P("seq", None, None),
            P("seq", None, None),
            P(),
            P(),
            P(),
        ),
        check_vma=False,
    )
```

time: 702 us -> 417 us (0.59)
  local copies, waits for them, and re-layouts: 146 us -> 0.04 us
  other arithmetic: 110 us -> 12.5 us
  Pallas kernels: 313 us -> 403 us
  matrix products: 68.9 us -> 0 us
  blocking collectives: 41.4 us -> 0 us
  starting transfers between devices: 7.61 us -> 0 us
    pallas_call x4 -> x7, Pallas kernels: 313 us -> 403 us  [the longest x1 129 us: scatter_blocks(): pl.pallas_call(functools.partial(scatter_kernel, slots), out_shape=(jax.S...]
    dot_general x25 -> x0, matrix products: 68.9 us -> none  [the longest x7 23.4 us: product_left(): lax.dot_general(left_side, right_side, (((0,), (0,)), ((), ())), preferre...]
    gather x2 -> x0, local copies, waits for them, and re-layouts: 48.3 us -> none  [the longest x1 24.3 us: body(): low_grad[jnp.minimum(slot_block, BLOCKS - 1)]]
    psum x1 -> x0, blocking collectives: 41.4 us -> none  [body(): vector_grad = lax.psum(stacked, 'seq')]
    slice x116 -> x0, local copies, waits for them, and re-layouts: 36 us -> none  [the longest x1 12.4 us: split_rows(): weight_rows[5 * EMBED_SIZE:5 * EMBED_SIZE + FF]]
    select_n x25 -> x0, other arithmetic: 29.1 us -> none  [the longest x1 21.4 us: body(): jnp.where(named, low_grad[jnp.minimum(slot_block, BLOCKS - 1)], 0.0)]
    reduce_sum x18 -> x0, other arithmetic: 19.6 us -> none  [the longest x2 7.99 us: block_step(): carry_weight * den_state]
    another operation x21 -> x0, local copies, waits for them, and re-layouts: 18.4 us -> none
  transfers between devices with their start and end apart: 4 -> 0, of which waited for: 1 -> 0; matrix products, arithmetic and copies ran while one was open for 20% -> 0% of each run, Pallas kernels for 40% -> 0%
where the time goes in v2:
time: 417 us; the launch traced here: 416 us
  Pallas kernels  403 us (97%)
  other arithmetic  12.5 us (3%)
    pallas_call x1, Pallas kernels, scatter_blocks(): pl.pallas_call(functools.partial(scatter_kernel, slots), out_shape=(jax.S...  129 us
    pallas_call x1, Pallas kernels, gather_blocks(): pl.pallas_call(functools.partial(gather_kernel, slots), out_shape=(jax.Sh...  121 us
    pallas_call x1, Pallas kernels, middle_pass(): pl.pallas_call(middle_kernel, out_shape=(jax.ShapeDtypeStruct((own, featu...  73.9 us
    pallas_call x1, Pallas kernels, close_pass(): pl.pallas_call(close_kernel, out_shape=(jax.ShapeDtypeStruct((own, featur...  31.3 us
    pallas_call x2, Pallas kernels, chain_state(): pl.pallas_call(functools.partial(chain_kernel, forward, tokens), out_shap...  29.1 us
    pallas_call x1, Pallas kernels, open_pass(): pl.pallas_call(functools.partial(open_kernel, devices), out_shape=(low, l...  18.9 us

profile of v2, /device:TPU:0, one launch (start us, length us, event | category | flops | bytes accessed | tf_op | source)
XLA Modules:
  0.0 416.1 jit_solution(12478439770424067189)
XLA Ops:
  0.6 0.7 convert_element_type.9
  1.3 1.9 broadcast_multiply_fusion.grad_ref.grads_ref
  3.3 2.6 convert_element_type.10.own_ref
  5.9 120.6 %gather_blocks.1 = (bf16[32,15,32,1024]{3,2,1,0:T(8,128)(2,1)}, bf16[16,1024]{1,0:T(8,128)(2,1)}, bf16[16,1024]{1,0:T(8,128)(2,1)}, bf16[16,1024]{1,0:T(8,128)(2,1)}) custom-call(bf16[15,32,1024]{2,1,0:T(8,128)(2,1)} %convert_element_type.10.own_ref, bf16[256,1024]{1,0:T(8,128)(2,1)} %tokens_ref.1, bf16[256,1024]{1,0:T(8,128)(2,1)} %broadcast_multiply_fusion.grad_ref.grads_ref), custom_call_target="tpu_custom_call" | custom-call | tf_op jit(solution)/shard_map/gather_blocks/pallas_call | solution.py:299
  126.5 18.9 %open_pass.1 = (bf16[272,1024]{1,0:T(8,128)(2,1)}, bf16[272,1024]{1,0:T(8,128)(2,1)}, f32[272,4]{1,0:T(8,128)}, f32[8,6]{1,0:T(8,128)}, f32[16,4]{1,0:T(8,128)},...) custom-call(s32[416]{0:T(512)} %slot_ref.5, ...), custom_call_target="tpu_custom_call" | custom-call | tf_op jit(solution)/shard_map/open_pass/pallas_call | solution.py:922
  145.4 13.6 %chain_forward.1.incoming_ref = f32[3,1024]{1,0:T(4,128)} custom-call(f32[3,1024]{1,0:T(4,128)} %get-tuple-element.58.own_ref, f32[11,1024]{1,0:T(8,128)} %vec_ref.9, f32[16,4]{1,0:T(8,128)} %get-tuple-element.59.link_ref, f32[1,4]{1,0:T(1,128)} %get-tuple-element.60.flag_ref), custom_call_target="tpu_custom_call" | custom-call | tf_op jit(solution)/shard_map/chain_forward/pallas_call | solution.py:1484
  159.1 73.9 %middle_pass.1 = (bf16[256,1024]{1,0:T(8,128)(2,1)}, f32[272,1024]{1,0:T(8,128)}, f32[272,1024]{1,0:T(8,128)}, f32[272,1024]{1,0:T(8,128)}, f32[256,1024]{1,0:T(...) custom-call(s32[416]{0:T(512)} %slot_ref.5, ...), custom_call_target="tpu_custom_call" | custom-call | tf_op jit(solution)/shard_map/middle_pass/pallas_call | solution.py:1206
  233.0 15.5 %chain_backward.1.incoming_ref = f32[3,1024]{1,0:T(4,128)} custom-call(f32[3,1024]{1,0:T(4,128)} %get-tuple-element.69.own_ref, f32[11,1024]{1,0:T(8,128)} %vec_ref.9, f32[16,4]{1,0:T(8,128)} %get-tuple-element.59.link_ref, f32[1,4]{1,0:T(1,128)} %get-tuple-element.60.flag_ref), custom_call_target="tpu_custom_call" | custom-call | tf_op jit(solution)/shard_map/chain_backward/pallas_call | solution.py:1484
  248.4 31.3 %close_pass.1 = (f32[256,1024]{1,0:T(8,128)}, f32[11,1024]{1,0:T(8,128)}, bf16[480,32,1024]{2,1,0:T(8,128)(2,1)}) custom-call(s32[416]{0:T(512)} %slot_ref.5, bf16[272,1024]{1,0:T(8,128)(2,1)} %get-tuple-element.54.x_ref, f32[11,1024]{1,0:T(8,128)} %vec_ref.9, f32[272,4]{1,0:T(8,128)} %get-tuple-element.56.marks_ref, ...), custom_call_target="tpu_custom_call", output_to_operand_aliasing={{2}: (25, {})} | custom-call | tf_op jit(solution)/shard_map/close_pass/pallas_call | solution.py:1379
  279.8 0.0 copy-start.5
  279.8 0.0 copy-start
  279.8 128.9 %scatter_blocks.1 = (bf16[15,32,1024]{2,1,0:T(8,128)(2,1)}, f32[11,1024]{1,0:T(8,128)}) custom-call(bf16[32,15,32,1024]{3,2,1,0:T(8,128)(2,1)} %bitcast.5, f32[11,1024]{1,0:T(8,128)} %get-tuple-element.89.rows_ref), custom_call_target="tpu_custom_call" | custom-call | tf_op jit(solution)/shard_map/scatter_blocks/pallas_call | solution.py:570
  408.7 0.0 copy-done.5
  408.7 0.2 compare_reduce_fusion
  408.9 0.0 copy-done
  408.9 0.0 copy-start.1
  408.9 0.0 copy-start.2
  409.0 0.0 copy-start.3
  409.0 0.0 copy-start.4
  409.0 0.0 copy-start.6
  409.0 6.3 %multiply_subtract_fusion = (f32[15,32,1024]{2,1,0:T(8,128)}, f32[15,32,1024]{2,1,0:T(8,128)}, f32[15,32,1024]{2,1,0:T(8,128)}) fusion(f32[15,32,1024]{2,1,0:T(8,128)S(1)} %copy-done, bf16[15,32,1024]{2,1,0:T(8,128)(2,1)} %get-tuple-element.90, pred[15]{0:T(512)(128)(4,1)S(1)} %compare_reduce_fusion, f32[15,32,1024]{2,1,0:T(8,128)} %param.18, ...), kind=kLoop, calls=%fused_computation.2 | loop fusion | flops 8355840 | bytes 12779535 | tf_op jit(solution)/shard_map/sub | solution.py:53
  415.3 0.0 copy-done.1
  415.3 0.0 copy-done.2
  415.3 0.0 copy-done.3
  415.3 0.0 copy-done.4
  415.3 0.0 copy-done.6
  415.3 0.7 multiply_subtract_fusion.1
  (1 shorter events, 0.0 us)
Async XLA Ops:
  279.8 129.0 %copy-start.5 = (s32[416]{0:T(512)S(1)}, s32[416]{0:T(512)}, u32[]{:S(2)}) copy-start(s32[416]{0:T(512)} %slot_ref.5) | copy-start | bytes 4996
  279.8 129.2 %copy-start = (f32[15,32,1024]{2,1,0:T(8,128)S(1)}, f32[15,32,1024]{2,1,0:T(8,128)}, u32[]{:S(2)}) copy-start(f32[15,32,1024]{2,1,0:T(8,128)} %param.16) | copy-start | bytes 5898244
  408.9 6.4 %copy-start.1 = (f32[11,1024]{1,0:T(8,128)S(1)}, f32[11,1024]{1,0:T(8,128)}, u32[]{:S(2)}) copy-start(f32[11,1024]{1,0:T(8,128)} %vec_ref.9) | copy-start | bytes 135172
  408.9 6.4 %copy-start.2 = (f32[11,1024]{1,0:T(8,128)S(1)}, f32[11,1024]{1,0:T(8,128)}, u32[]{:S(2)}) copy-start(f32[11,1024]{1,0:T(8,128)} %param.22) | copy-start | bytes 135172
  409.0 6.4 %copy-start.3 = (f32[11,1024]{1,0:T(8,128)S(1)}, f32[11,1024]{1,0:T(8,128)}, u32[]{:S(2)}) copy-start(f32[11,1024]{1,0:T(8,128)} %param.21) | copy-start | bytes 135172
  409.0 6.4 %copy-start.4 = (f32[11,1024]{1,0:T(8,128)S(1)}, f32[11,1024]{1,0:T(8,128)}, u32[]{:S(2)}) copy-start(f32[11,1024]{1,0:T(8,128)} %get-tuple-element.91) | copy-start | bytes 135172
  409.0 6.4 %copy-start.6 = (f32[11]{0:T(128)S(1)}, f32[11]{0:T(128)}, u32[]{:S(2)}) copy-start(f32[11]{0:T(128)} %constant.10.clone) | copy-start | bytes 136

commit v3 on v2

--- a/solution.py
+++ b/solution.py
@@ -598,6 +598,7 @@
 
 
 ROW_TILE = 16
+BIG_TILE = 64
 CHUNKS = 8
 LANES = 128
 VMEM_BYTES = 60 * 2**20
@@ -609,12 +610,13 @@
 
 def fetch_blocks(slot_ref, pool_ref, store_ref, sem, first_block, place, count):
     def step(b, carry):
-        pltpu.make_async_copy(
-            pool_ref.at[slot_ref[first_block + b]], store_ref.at[place + b], sem
-        ).start()
+        for k in range(4):
+            pltpu.make_async_copy(
+                pool_ref.at[slot_ref[first_block + 4 * b + k]], store_ref.at[place + 4 * b + k], sem
+            ).start()
         return carry
 
-    lax.fori_loop(0, count, step, 0)
+    lax.fori_loop(0, count // 4, step, 0)
 
 
 def await_blocks(pool_ref, store_ref, sem, place, count):
@@ -623,7 +625,7 @@
     ).wait()
 
 
-def times_weight(left_ref, store_ref, place, count, write, width=256):
+def times_weight(left_ref, store_ref, place, count, write, width=512):
     features = store_ref.shape[2]
 
     def step(n, carry):
@@ -635,7 +637,7 @@
     lax.fori_loop(0, features // width, step, 0)
 
 
-def times_weight_back(left_ref, store_ref, place, count, write, width=256):
+def times_weight_back(left_ref, store_ref, place, count, write, width=1024):
     blocks = width // BLOCK_ROWS
 
     def step(n, carry):
@@ -647,37 +649,49 @@
     lax.fori_loop(0, count // blocks, step, 0)
 
 
-def weight_gradient(left_ref, right_ref, own, slot_ref, grad_ref, stage, sems, first_block, width=256):
+def weight_gradient(left_ref, right_ref, own, slot_ref, grad_ref, store_ref, sem, first_block, place, width=1024):
     blocks = width // BLOCK_ROWS
     steps = left_ref.shape[1] // width
 
-    def drain(slot):
-        pltpu.make_async_copy(stage.at[slot], grad_ref.at[pl.ds(0, blocks)], sems.at[slot]).wait()
-
     def step(n, carry):
-        slot = lax.rem(n, 2)
-
-        @pl.when(n >= 2)
-        def _():
-            drain(slot)
-
         cols = pl.ds(pl.multiple_of(n * width, width), width)
         piece = product_left(left_ref[0:own, cols], right_ref[0:own])
-        stage[slot] = piece.astype(stage.dtype).reshape(stage.shape[1:])
+        at = place + n * blocks
+        store_ref[pl.ds(at, blocks)] = piece.astype(store_ref.dtype).reshape(blocks, *store_ref.shape[1:])
 
         def put(b, inner):
-            pltpu.make_async_copy(
-                stage.at[slot, b],
-                grad_ref.at[slot_ref[first_block + n * blocks + b]],
-                sems.at[slot],
-            ).start()
+            for k in range(4):
+                pltpu.make_async_copy(
+                    store_ref.at[at + 4 * b + k],
+                    grad_ref.at[slot_ref[first_block + n * blocks + 4 * b + k]],
+                    sem,
+                ).start()
             return inner
 
-        return lax.fori_loop(0, blocks, put, carry)
+        return lax.fori_loop(0, blocks // 4, put, carry)
 
     lax.fori_loop(0, steps, step, 0)
-    drain(0)
-    drain(1)
+
+
+def await_gradient(store_ref, grad_ref, sem, place, count):
+    pltpu.make_async_copy(
+        store_ref.at[pl.ds(place, count)], grad_ref.at[pl.ds(0, count)], sem
+    ).wait()
+
+
+def for_rows(rows, work, sums=()):
+    own = rows - ROW_TILE
+
+    def step(j, carry):
+        out = work(pl.multiple_of(j * BIG_TILE, BIG_TILE), BIG_TILE, *carry)
+        return carry if out is None else out
+
+    sums = lax.fori_loop(0, own // BIG_TILE, step, sums)
+    return sums
+
+
+def fold(piece):
+    return jnp.sum(piece.reshape(-1, CHUNKS, piece.shape[1]), axis=0)
 
 
 def unit_norm(values):
@@ -728,19 +742,10 @@
     )
 
 
-def normed_pair(ext, marks_ref, j):
-    here = ext[pl.ds(pl.multiple_of(j * ROW_TILE + 8, 8), ROW_TILE)]
-    before = ext[rows_at(j)] * marks_ref[rows_at(j), 1:2]
+def normed_pair(ext, marks_ref, first, size):
+    here = ext[pl.ds(pl.multiple_of(first + 8, 8), size)]
+    before = ext[pl.ds(first, size)] * marks_ref[pl.ds(first, size), 1:2]
     return here, before
-
-
-def over_tiles(tiles, work, halo):
-    def step(j, carry):
-        work(j)
-        return carry
-
-    lax.fori_loop(0, tiles - 1, step, 0)
-    halo(tiles - 1)
 
 
 def take_step(wide, first, length):
@@ -835,48 +840,45 @@
     write_marks(doc_ref, marks_ref, chunk_ref, link_ref, flag_ref, own, devices)
     me = lax.axis_index("seq")
 
-    def widen(j, carry):
-        put_rows(wide, rows_at(j), tokens_ref[rows_at(j)].astype(jnp.float32))
-        put_rows(wide_grad, rows_at(j), grads_ref[rows_at(j)].astype(jnp.float32))
-        return carry
-
-    lax.fori_loop(0, tiles - 1, widen, 0)
-
-    def norm(j, tile):
-        x_ref[rows_at(j)] = tile.astype(jnp.bfloat16)
+    def widen(first, size):
+        at = pl.ds(first, size)
+        put_rows(wide, at, tokens_ref[at].astype(jnp.float32))
+        put_rows(wide_grad, at, grads_ref[at].astype(jnp.float32))
+
+    for_rows(rows, widen)
+
+    def norm(first, size, tile):
+        x_ref[pl.ds(first, size)] = tile.astype(jnp.bfloat16)
         unit, _ = unit_norm(tile)
-        ext[pl.ds(pl.multiple_of(j * ROW_TILE + 8, 8), ROW_TILE)] = unit * vec_ref[0:1] + vec_ref[1:2]
-
-    def arrange(j, carry):
-        norm(j, jnp.concatenate([take_step(wide, 2 * j + k, length) for k in range(2)], axis=0))
-        pair = [take_step(wide_grad, 2 * j + k, length) for k in range(2)]
-        grad_ref[rows_at(j)] = jnp.concatenate(pair, axis=0).astype(jnp.bfloat16)
-        return carry
-
-    lax.fori_loop(0, tiles - 1, arrange, 0)
+        ext[pl.ds(pl.multiple_of(first + 8, 8), size)] = unit * vec_ref[0:1] + vec_ref[1:2]
+
+    def arrange(first, size):
+        steps = [first // CHUNKS + k for k in range(size // CHUNKS)]
+        norm(first, size, jnp.concatenate([take_step(wide, i, length) for i in steps], axis=0))
+        tile = jnp.concatenate([take_step(wide_grad, i, length) for i in steps], axis=0)
+        grad_ref[pl.ds(first, size)] = tile.astype(jnp.bfloat16)
+
+    for_rows(rows, arrange)
     more, less = me < devices - 1, me > 0
     later = jnp.where(more, after_ref[...].astype(jnp.float32), 0.0)[0:2]
     earlier = jnp.where(less, before_ref[...].astype(jnp.float32), 0.0)
     blank_rows = jnp.zeros((ROW_TILE - 4, features), jnp.float32)
     norm(
-        tiles - 1,
+        own,
+        ROW_TILE,
         jnp.concatenate([later, earlier[ROW_TILE - 1 :], earlier[ROW_TILE - 2 : ROW_TILE - 1], blank_rows], axis=0),
     )
     later_grad = jnp.where(more, after_grad_ref[...].astype(jnp.float32), 0.0)[0:2]
     grad_ref[own:rows] = jnp.concatenate([later_grad, blank_rows, blank_rows[:2]], axis=0).astype(jnp.bfloat16)
     shift_in(ext, own)
 
-    def mix(j, here, before):
+    def mix(first, size, here, before):
         for row, ref in ((2, in_key), (3, in_value), (4, in_recept)):
             weight = vec_ref[row : row + 1]
-            ref[rows_at(j)] = (weight * here + (1.0 - weight) * before).astype(jnp.bfloat16)
-
-    def halo(j):
-        here = ext[own + 8 : own + 8 + ROW_TILE]
-        before = halo_previous(ext, own, features) * marks_ref[own:rows, 1:2]
-        mix(j, here, before)
-
-    over_tiles(tiles, lambda j: mix(j, *normed_pair(ext, marks_ref, j)), halo)
+            ref[pl.ds(first, size)] = (weight * here + (1.0 - weight) * before).astype(jnp.bfloat16)
+
+    for_rows(rows, lambda first, size: mix(first, size, *normed_pair(ext, marks_ref, first, size)))
+    mix(own, ROW_TILE, ext[own + 8 : own + 8 + ROW_TILE], halo_previous(ext, own, features) * marks_ref[own:rows, 1:2])
     for m, (left, out) in enumerate(((in_key, key_ref), (in_value, value_ref), (in_recept, recept_ref))):
         await_blocks(pool_ref, store, sem.at[m], m * per, per)
 
@@ -942,10 +944,10 @@
 def middle_kernel(
     slot_ref, x_ref, grad_ref, vec_ref, marks_ref, chunk_ref, incoming_ref, prefix_ref,
     key_ref, value_ref, recept_ref, num_ref, den_ref, max_ref, pool_ref,
-    layer_ref, resid_grad, wkv, gw, full_num, full_den, full_max, own_share, back_num, back_den, back_max,
-    recept_grad, suffix_ref, summary_ref, sums_ref, slot_grad,
-    mixed, ext, unit, inverse, low_key, low_recept, hidden, squared, value_acc, gate, gcv, gcg, hidden_grad,
-    attn_grad, top_log, wide, store, stage, sem, stage_sem,
+    layer_ref, resid_grad, wkv, gw, own_share, recept_grad, suffix_ref, summary_ref, sums_ref,
+    full_out, back_out, slot_grad,
+    full_num, full_den, full_max, mixed, ext, unit, inverse, low_key, low_recept, hidden, squared, value_acc, gate, gcv, gcg, hidden_grad,
+    attn_grad, top_log, wide, store, sem, out_sem, state_sem,
 ):
     rows, features = x_ref.shape
     own = rows - ROW_TILE
@@ -992,6 +994,11 @@
     def row(ref, r):
         return ref[r : r + 1]
 
+    def state_copy(k, target):
+        return pltpu.make_async_copy((full_num, full_den, full_max)[k], target.at[k], state_sem.at[k])
+
+    for k in range(3):
+        state_copy(k, full_out).start()
     end = advance(
         (row(full_num, own - 1), row(full_den, own - 1), row(full_max, own - 1)),
         row(key_ref, own - 1), row(value_ref, own - 1), rate,
@@ -1008,12 +1015,13 @@
     )
     attend(tiles - 1, ROW_TILE, halo_state, key_ref[own:rows], value_ref[own:rows], recept_ref[own:rows])
 
-    def pack(j, c):
-        mixed[rows_at(j)] = ext[rows_at(j)].astype(jnp.bfloat16)
-        back_num[rows_at(j)] = value_acc[rows_at(j)]
-        return c
-
-    lax.fori_loop(0, tiles, pack, 0)
+    def pack(first, size):
+        at = pl.ds(first, size)
+        mixed[at] = ext[at].astype(jnp.bfloat16)
+        gw[at] = value_acc[at]
+
+    for_rows(rows, pack)
+    pack(own, ROW_TILE)
     await_blocks(pool_ref, store, sem.at[0], at_out, per)
 
     def write_resid(cols, piece):
@@ -1021,28 +1029,26 @@
 
     times_weight(mixed, store, at_out, per, write_resid)
 
-    def norm(j, c):
-        resid = unit[rows_at(j)]
-        resid_grad[rows_at(j)] = resid
+    def norm(first, size):
+        at = pl.ds(first, size)
+        resid = unit[at]
+        resid_grad[at] = resid
         out, inv = unit_norm(resid)
-        unit[rows_at(j)] = out
-        inverse[rows_at(j)] = inv
-        ext[pl.ds(pl.multiple_of(j * ROW_TILE + 8, 8), ROW_TILE)] = out * vec_ref[7:8] + vec_ref[8:9]
-        return c
-
-    lax.fori_loop(0, tiles, norm, 0)
+        unit[at] = out
+        inverse[at] = inv
+        ext[pl.ds(pl.multiple_of(first + 8, 8), size)] = out * vec_ref[7:8] + vec_ref[8:9]
+
+    for_rows(rows, norm)
+    norm(own, ROW_TILE)
     shift_in(ext, own)
 
-    def mix(j, here, before):
+    def mix(first, size, here, before):
         for r, ref in ((9, low_key), (10, low_recept)):
             weight = vec_ref[r : r + 1]
-            ref[rows_at(j)] = (weight * here + (1.0 - weight) * before).astype(jnp.bfloat16)
-
-    def halo_pair():
-        here = ext[own + 8 : own + 8 + ROW_TILE]
-        return here, halo_previous(ext, own, features) * marks_ref[own:rows, 1:2]
-
-    over_tiles(tiles, lambda j: mix(j, *normed_pair(ext, marks_ref, j)), lambda j: mix(j, *halo_pair()))
+            ref[pl.ds(first, size)] = (weight * here + (1.0 - weight) * before).astype(jnp.bfloat16)
+
+    for_rows(rows, lambda first, size: mix(first, size, *normed_pair(ext, marks_ref, first, size)))
+    mix(own, ROW_TILE, ext[own + 8 : own + 8 + ROW_TILE], halo_previous(ext, own, features) * marks_ref[own:rows, 1:2])
 
     await_blocks(pool_ref, store, sem.at[1], at_key, ff)
 
@@ -1065,55 +1071,53 @@
 
     times_weight(low_recept, store, at_recept, per, write_gate)
 
-    def finish(j, c):
-        at = rows_at(j)
+    def finish(first, size):
+        at = pl.ds(first, size)
         opened = jax.nn.sigmoid(gate[at])
         value = value_acc[at]
-        out = resid_grad[at] + opened * value
-
-        @pl.when(j < tiles - 1)
-        def _():
-            for k in range(2):
-                put_step(wide, 2 * j + k, length, out[8 * k : 8 * k + 8])
-
         grad = grad_ref[at].astype(jnp.float32) * opened
         gcv[at] = grad.astype(jnp.bfloat16)
         gcg[at] = (grad * value * (1.0 - opened)).astype(jnp.bfloat16)
-        return c
-
-    lax.fori_loop(0, tiles, finish, 0)
-
-    def emit(j, c):
-        layer_ref[rows_at(j)] = take_rows(wide, rows_at(j)).astype(jnp.bfloat16)
-        return c
-
-    lax.fori_loop(0, tiles - 1, emit, 0)
+        return resid_grad[at] + opened * value
+
+    def finish_own(first, size):
+        out = finish(first, size)
+        for k in range(size // CHUNKS):
+            put_step(wide, first // CHUNKS + k, length, out[CHUNKS * k : CHUNKS * (k + 1)])
+
+    for_rows(rows, finish_own)
+    finish(own, ROW_TILE)
+
+    def emit(first, size):
+        layer_ref[pl.ds(first, size)] = take_rows(wide, pl.ds(first, size)).astype(jnp.bfloat16)
+
+    for_rows(rows, emit)
 
     def write_hidden_grad(cols, piece):
         hidden_grad[:, cols] = (piece * (2.0 * hidden[:, cols])).astype(jnp.bfloat16)
 
     times_weight_back(gcv, store, at_value, ff, write_hidden_grad)
-    weight_gradient(squared, gcv, own, slot_ref, slot_grad, stage, stage_sem, 5 * per + ff)
-    weight_gradient(hidden_grad, low_key, own, slot_ref, slot_grad, stage, stage_sem, 5 * per)
-    weight_gradient(low_recept, gcg, own, slot_ref, slot_grad, stage, stage_sem, 4 * per)
+    weight_gradient(squared, gcv, own, slot_ref, slot_grad, store, out_sem.at[2], 5 * per + ff, at_value)
     times_weight(hidden_grad, store, at_key, ff, write_value)
+    weight_gradient(hidden_grad, low_key, own, slot_ref, slot_grad, store, out_sem.at[1], 5 * per, at_key)
     times_weight_back(gcg, store, at_recept, per, write_gate)
+    weight_gradient(low_recept, gcg, own, slot_ref, slot_grad, store, out_sem.at[3], 4 * per, at_recept)
     carried = hidden.at[:, 0:features]
     mix_key, mix_recept = vec_ref[9:10], vec_ref[10:11]
 
-    def carry_over(j, c):
-        at = rows_at(j)
+    def carry_over(first, size):
+        at = pl.ds(first, size)
         carried[at] = marks_ref[at, 1:2] * ((1.0 - mix_key) * value_acc[at] + (1.0 - mix_recept) * gate[at])
-        return c
-
-    lax.fori_loop(0, tiles, carry_over, 0)
+
+    for_rows(rows, carry_over)
+    carry_over(own, ROW_TILE)
     halo_next = jnp.concatenate(
         [carried[own + 1 : own + 2], jnp.zeros((ROW_TILE - 1, features), jnp.float32)], axis=0
     )
     carried[own : own + 8] = jnp.concatenate([carried[1:8], carried[own : own + 1]], axis=0)
 
-    def norm_back(j, following):
-        at = rows_at(j)
+    def norm_back(first, size, following):
+        at = pl.ds(first, size)
         grad = mix_key * value_acc[at] + mix_recept * gate[at] + following
         scaled = grad * vec_ref[7:8]
         inner = (
@@ -1126,13 +1130,10 @@
         attn_grad[at] = total.astype(jnp.bfloat16)
         return grad
 
-    def fold(piece):
-        return piece[:8] + piece[8:]
-
-    def back_step(j, sums):
-        at = rows_at(j)
-        grad = norm_back(j, carried[pl.ds(pl.multiple_of(j * ROW_TILE + 8, 8), ROW_TILE)])
-        here, before = normed_pair(ext, marks_ref, j)
+    def back_step(first, size, *sums):
+        at = pl.ds(first, size)
+        grad = norm_back(first, size, carried[pl.ds(pl.multiple_of(first + 8, 8), size)])
+        here, before = normed_pair(ext, marks_ref, first, size)
         spread = here - before
         return (
             sums[0] + fold(grad * unit[at]),
@@ -1142,24 +1143,24 @@
         )
 
     blank = jnp.zeros((CHUNKS, features), jnp.float32)
-    sums = lax.fori_loop(0, tiles - 1, back_step, (blank,) * 4)
+    sums = for_rows(rows, back_step, (blank,) * 4)
     for k in range(4):
         sums_ref[k : k + 1] = jnp.sum(sums[k], axis=0, keepdims=True)
-    norm_back(tiles - 1, halo_next)
-
-    weight_gradient(mixed, attn_grad, own, slot_ref, slot_grad, stage, stage_sem, 3 * per)
+    norm_back(own, ROW_TILE, halo_next)
+
     times_weight_back(attn_grad, store, at_out, per, write_gate)
-
-    def gate_back(j, c):
-        at = rows_at(j)
+    weight_gradient(mixed, attn_grad, own, slot_ref, slot_grad, store, out_sem.at[0], 3 * per, at_out)
+
+    def gate_back(first, size):
+        at = pl.ds(first, size)
         opened = jax.nn.sigmoid(recept_ref[at])
         grad = gate[at] * opened
+        ext[at] = grad * gw[at]
         gw[at] = grad
         recept_grad[at] = (grad * wkv[at] * (1.0 - opened)).astype(jnp.bfloat16)
-        ext[at] = grad * back_num[at]
-        return c
-
-    lax.fori_loop(0, tiles, gate_back, 0)
+
+    for_rows(rows, gate_back)
+    gate_back(own, ROW_TILE)
 
     def back_token(state, share, out, top, start):
         older = state[2] - rate
@@ -1167,6 +1168,10 @@
         old, new = jnp.exp(older - high), jnp.exp(-top - high)
         return reset((old * state[0] + new * share, old * state[1] - new * share * out, high), start)
 
+    for k in range(3):
+        state_copy(k, full_out).wait()
+    back_num, back_den, back_max = full_num, full_den, full_max
+
     def back_scan(n, state):
         i = length - 1 - n
         at = rows_at(i, CHUNKS)
@@ -1174,8 +1179,8 @@
         return back_token(state, ext[at], wkv[at], top_log[at], marks_ref[at, 0:1])
 
     heads = lax.fori_loop(0, length, back_scan, (blank, blank, blank + NEGATIVE))
-    for ref in (back_num, back_den, back_max):
-        ref[own:rows] = jnp.zeros((ROW_TILE, features), jnp.float32)
+    for k in range(3):
+        state_copy(k, back_out).start()
     nothing = jnp.zeros((1, features), jnp.float32)
     after = back_token(
         (nothing, nothing, nothing + NEGATIVE),
@@ -1190,6 +1195,10 @@
     first = (row(back_num, 0), row(back_den, 0), row(back_max, 0))
     last = merge(first, aged(after, float(length - 1), marks_ref[0:1, 3:4], rate))
     summary_ref[...] = jnp.concatenate(last, axis=0)
+    for k, (place, count) in enumerate(((at_out, per), (at_key, ff), (at_value, ff), (at_recept, per))):
+        await_gradient(store, slot_grad, out_sem.at[k], place, count)
+    for k in range(3):
+        state_copy(k, back_out).wait()
 
 
 def middle_pass(slots, x_rows, grad_rows, vectors, marks, chunk_marks, incoming, opened, pool):
@@ -1207,15 +1216,20 @@
         middle_kernel,
         out_shape=(
             jax.ShapeDtypeStruct((own, features), jnp.bfloat16),
-            full, full, full, part, part, part, full, full, full, full, low,
+            full, full, full, full, low,
             jax.ShapeDtypeStruct((3, CHUNKS, features), jnp.float32),
             jax.ShapeDtypeStruct((3, features), jnp.float32),
             jax.ShapeDtypeStruct((4, features), jnp.float32),
+            jax.ShapeDtypeStruct((3, own, features), jnp.float32),
+            jax.ShapeDtypeStruct((3, own, features), jnp.float32),
             jax.ShapeDtypeStruct(pool.shape, jnp.bfloat16),
         ),
         in_specs=[pl.BlockSpec(memory_space=pltpu.SMEM)] + [vmem] * 13 + [anywhere],
-        out_specs=(vmem,) * 15 + (anywhere,),
+        out_specs=(vmem,) * 9 + (anywhere,) * 3,
         scratch_shapes=[
+            f32(own, features),
+            f32(own, features),
+            f32(own, features),
             b16(rows, features),
             f32(rows + 8, features),
             f32(rows, features),
@@ -1233,9 +1247,9 @@
             f32(rows, features),
             f32(features // LANES, own, LANES),
             b16((2 * EMBED_SIZE + 2 * FF) // BLOCK_ROWS, BLOCK_ROWS, features),
-            b16(2, 256 // BLOCK_ROWS, BLOCK_ROWS, features),
             pltpu.SemaphoreType.DMA((4,)),
-            pltpu.SemaphoreType.DMA((2,)),
+            pltpu.SemaphoreType.DMA((4,)),
+            pltpu.SemaphoreType.DMA((3,)),
         ],
         compiler_params=pltpu.CompilerParams(vmem_limit_bytes=VMEM_BYTES),
         name="middle_pass",
@@ -1244,11 +1258,11 @@
 
 def close_kernel(
     slot_ref, x_ref, vec_ref, marks_ref, chunk_ref, incoming_ref, suffix_ref, key_ref, value_ref,
-    in_key, in_value, in_recept, resid_grad, wkv, gw, full_num, full_den, full_max, own_share,
-    back_num, back_den, back_max, recept_grad, sums_two_ref, pool_ref, grads_in,
+    in_key, in_value, in_recept, resid_grad, wkv, gw, own_share, recept_grad, sums_two_ref, full_ref, back_ref,
+    pool_ref, grads_in,
     input_ref, sums_ref, slot_grad,
     ext, unit, inverse, key_wide, value_wide, key_grad, value_grad, grad_key_in, grad_value_in, grad_recept_in,
-    carried, wide, store, stage, sem, stage_sem,
+    carried, wide, store, sem, out_sem,
 ):
     rows, features = x_ref.shape
     own = rows - ROW_TILE
@@ -1273,11 +1287,11 @@
     def token(i, sums):
         at = rows_at(i, CHUNKS)
         distance = (length - 1 - i).astype(jnp.float32)
-        state = merge((back_num[at], back_den[at], back_max[at]), aged(carry, distance, marks_ref[at, 3:4], rate))
+        state = merge(tuple(back_ref[k, at] for k in range(3)), aged(carry, distance, marks_ref[at, 3:4], rate))
         key_g, value_g, bonus_grad = spread_back(state, key_ref[at], value_ref[at], own_share[at], gw[at], wkv[at])
         key_wide[at] = key_g
         value_wide[at] = value_g
-        fade = jnp.exp(state[2] + full_max[at] - rate) * (state[0] * full_num[at] + state[1] * full_den[at])
+        fade = jnp.exp(state[2] + full_ref[2, at] - rate) * (state[0] * full_ref[0, at] + state[1] * full_ref[1, at])
         return sums[0] + fade, sums[1] + bonus_grad
 
     blank = jnp.zeros((CHUNKS, features), jnp.float32)
@@ -1294,51 +1308,52 @@
     key_wide[own:rows] = key_g
     value_wide[own:rows] = value_g
 
-    def pack(j, c):
-        at = rows_at(j)
+    def pack(first, size):
+        at = pl.ds(first, size)
         key_grad[at] = key_wide[at].astype(jnp.bfloat16)
         value_grad[at] = value_wide[at].astype(jnp.bfloat16)
-        return c
-
-    lax.fori_loop(0, tiles, pack, 0)
-    weight_gradient(in_recept, recept_grad, own, slot_ref, slot_grad, stage, stage_sem, 2 * per)
-    weight_gradient(in_key, key_grad, own, slot_ref, slot_grad, stage, stage_sem, 0)
-    weight_gradient(in_value, value_grad, own, slot_ref, slot_grad, stage, stage_sem, per)
-    for m, (left, out) in enumerate(((key_grad, grad_key_in), (value_grad, grad_value_in), (recept_grad, grad_recept_in))):
+
+    for_rows(rows, pack)
+    pack(own, ROW_TILE)
+    products = (
+        (key_grad, grad_key_in, in_key),
+        (value_grad, grad_value_in, in_value),
+        (recept_grad, grad_recept_in, in_recept),
+    )
+    for m, (left, out, inputs) in enumerate(products):
         await_blocks(pool_ref, store, sem.at[m], m * per, per)
 
         def write(cols, piece, out=out):
             out[:, cols] = piece
 
         times_weight_back(left, store, m * per, per, write)
-
-    def norm(j, c):
-        out, inv = unit_norm(x_ref[rows_at(j)].astype(jnp.float32))
-        unit[rows_at(j)] = out
-        inverse[rows_at(j)] = inv
-        ext[pl.ds(pl.multiple_of(j * ROW_TILE + 8, 8), ROW_TILE)] = out * vec_ref[0:1] + vec_ref[1:2]
-        return c
-
-    lax.fori_loop(0, tiles, norm, 0)
+        weight_gradient(inputs, left, own, slot_ref, slot_grad, store, out_sem.at[m], m * per, m * per)
+
+    def norm(first, size):
+        at = pl.ds(first, size)
+        out, inv = unit_norm(x_ref[at].astype(jnp.float32))
+        unit[at] = out
+        inverse[at] = inv
+        ext[pl.ds(pl.multiple_of(first + 8, 8), size)] = out * vec_ref[0:1] + vec_ref[1:2]
+
+    for_rows(rows, norm)
+    norm(own, ROW_TILE)
     shift_in(ext, own)
     mixes = tuple(vec_ref[k : k + 1] for k in (2, 3, 4))
 
-    def carry_over(j, c):
-        at = rows_at(j)
+    def carry_over(first, size):
+        at = pl.ds(first, size)
         total = (1.0 - mixes[0]) * grad_key_in[at] + (1.0 - mixes[1]) * grad_value_in[at] + (1.0 - mixes[2]) * grad_recept_in[at]
         carried[at] = marks_ref[at, 1:2] * total
-        return c
-
-    lax.fori_loop(0, tiles, carry_over, 0)
+
+    for_rows(rows, carry_over)
+    carry_over(own, ROW_TILE)
     carried[own : own + 8] = jnp.concatenate([carried[1:8], carried[own : own + 1]], axis=0)
 
-    def fold(piece):
-        return piece[:8] + piece[8:]
-
-    def back_step(j, sums):
-        at = rows_at(j)
+    def back_step(first, size, *sums):
+        at = pl.ds(first, size)
         grads = (grad_key_in[at], grad_value_in[at], grad_recept_in[at])
-        grad = carried[pl.ds(pl.multiple_of(j * ROW_TILE + 8, 8), ROW_TILE)]
+        grad = carried[pl.ds(pl.multiple_of(first + 8, 8), size)]
         for weight, piece in zip(mixes, grads):
             grad = grad + weight * piece
         scaled = grad * vec_ref[0:1]
@@ -1348,24 +1363,25 @@
             - unit[at] * jnp.mean(scaled * unit[at], axis=1, keepdims=True)
         )
         out = resid_grad[at] + inner * inverse[at]
-        for k in range(2):
-            put_step(wide, 2 * j + k, length, out[8 * k : 8 * k + 8])
-        here, before = normed_pair(ext, marks_ref, j)
+        for k in range(size // CHUNKS):
+            put_step(wide, first // CHUNKS + k, length, out[CHUNKS * k : CHUNKS * (k + 1)])
+        here, before = normed_pair(ext, marks_ref, first, size)
         spread = here - before
         return (sums[0] + fold(grad * unit[at]), sums[1] + fold(grad)) + tuple(
             s + fold(piece * spread) for s, piece in zip(sums[2:], grads)
         )
 
-    sums = lax.fori_loop(0, tiles - 1, back_step, (blank,) * 5)
+    sums = for_rows(rows, back_step, (blank,) * 5)
     for k in range(5):
         sums_ref[k : k + 1] = jnp.sum(sums[k], axis=0, keepdims=True)
     sums_ref[7:] = sums_two_ref[...]
 
-    def emit(j, c):
-        input_ref[rows_at(j)] = take_rows(wide, rows_at(j))
-        return c
-
-    lax.fori_loop(0, tiles - 1, emit, 0)
+    def emit(first, size):
+        input_ref[pl.ds(first, size)] = take_rows(wide, pl.ds(first, size))
+
+    for_rows(rows, emit)
+    for m in range(3):
+        await_gradient(store, slot_grad, out_sem.at[m], m * per, per)
 
 
 def close_pass(slots, x_rows, vectors, marks, chunk_marks, incoming, suffix, key, value, lows, kept, pool, slot_grad):
@@ -1400,9 +1416,8 @@
             f32(rows, features),
             f32(features // LANES, own, LANES),
             b16(3 * EMBED_SIZE // BLOCK_ROWS, BLOCK_ROWS, features),
-            b16(2, 256 // BLOCK_ROWS, BLOCK_ROWS, features),
             pltpu.SemaphoreType.DMA((3,)),
-            pltpu.SemaphoreType.DMA((2,)),
+            pltpu.SemaphoreType.DMA((3,)),
         ],
         compiler_params=pltpu.CompilerParams(vmem_limit_bytes=VMEM_BYTES),
         name="close_pass",
@@ -1532,8 +1547,8 @@
     ) = open_pass(devices, block_slot, doc_lengths, tokens_in, out_grad, halo, vectors, gathered)
     incoming = chain_state(summary, vectors, links, flags, True, tokens, 3)
     (
-        layer_out, resid_grad, wkv, gw, full_num, full_den, full_max, own_share, back_num, back_den, back_max,
-        recept_grad, suffix, back_summary, sums_two, slot_grad,
+        layer_out, resid_grad, wkv, gw, own_share, recept_grad, suffix, back_summary, sums_two,
+        full_state, back_state, slot_grad,
     ) = middle_pass(
         block_slot, x_rows, grad_rows, vectors, marks, chunk_marks, incoming,
         (key, value, recept, num, den, top, prefix), gathered,
@@ -1542,7 +1557,7 @@
     input_grad, stacked, slot_grad = close_pass(
         block_slot, x_rows, vectors, marks, chunk_marks, back_incoming, suffix, key, value,
         (in_key, in_value, in_recept),
-        (resid_grad, wkv, gw, full_num, full_den, full_max, own_share, back_num, back_den, back_max, recept_grad, sums_two),
+        (resid_grad, wkv, gw, own_share, recept_grad, sums_two, full_state, back_state),
         gathered, slot_grad,
     )
     own_slots = device_place * masters.shape[0] + jnp.arange(masters.shape[0], dtype=jnp.int32)

time: 417 us -> 371 us (0.89)
  Pallas kernels: 403 us -> 357 us
    pallas_call x1, Pallas kernels: 73.9 us -> 44 us  [middle_pass(): pl.pallas_call(middle_kernel, out_shape=(jax.ShapeDtypeStruct((own, featu...]
    pallas_call x1, Pallas kernels: 31.3 us -> 19.4 us  [close_pass(): pl.pallas_call(close_kernel, out_shape=(jax.ShapeDtypeStruct((own, featur...]
where the time goes in v3:
time: 371 us; the launch traced here: 370 us
  Pallas kernels  357 us (96%)
  other arithmetic  12.5 us (3%)
    pallas_call x1, Pallas kernels, scatter_blocks(): pl.pallas_call(functools.partial(scatter_kernel, slots), out_shape=(jax.S...  129 us
    pallas_call x1, Pallas kernels, gather_blocks(): pl.pallas_call(functools.partial(gather_kernel, slots), out_shape=(jax.Sh...  121 us
    pallas_call x1, Pallas kernels, middle_pass(): pl.pallas_call(middle_kernel, out_shape=(jax.ShapeDtypeStruct((own, featu...  44 us
    pallas_call x2, Pallas kernels, chain_state(): pl.pallas_call(functools.partial(chain_kernel, forward, tokens), out_shap...  29.1 us
    pallas_call x1, Pallas kernels, close_pass(): pl.pallas_call(close_kernel, out_shape=(jax.ShapeDtypeStruct((own, featur...  19.4 us
    pallas_call x1, Pallas kernels, open_pass(): pl.pallas_call(functools.partial(open_kernel, devices), out_shape=(low, l...  14.9 us

profile of v3, /device:TPU:0, one launch (start us, length us, event | category | flops | bytes accessed | tf_op | source)
XLA Modules:
  0.0 370.3 jit_solution(8354132717616719733)
XLA Ops:
  0.6 0.7 convert_element_type.9
  1.3 1.9 broadcast_multiply_fusion.grad_ref.grads_ref
  3.3 2.6 convert_element_type.10.own_ref
  5.9 120.6 %gather_blocks.1 = (bf16[32,15,32,1024]{3,2,1,0:T(8,128)(2,1)}, bf16[16,1024]{1,0:T(8,128)(2,1)}, bf16[16,1024]{1,0:T(8,128)(2,1)}, bf16[16,1024]{1,0:T(8,128)(2,1)}) custom-call(bf16[15,32,1024]{2,1,0:T(8,128)(2,1)} %convert_element_type.10.own_ref, bf16[256,1024]{1,0:T(8,128)(2,1)} %tokens_ref.1, bf16[256,1024]{1,0:T(8,128)(2,1)} %broadcast_multiply_fusion.grad_ref.grads_ref), custom_call_target="tpu_custom_call" | custom-call | tf_op jit(solution)/shard_map/gather_blocks/pallas_call | solution.py:299
  126.5 14.9 %open_pass.1 = (bf16[272,1024]{1,0:T(8,128)(2,1)}, bf16[272,1024]{1,0:T(8,128)(2,1)}, f32[272,4]{1,0:T(8,128)}, f32[8,6]{1,0:T(8,128)}, f32[16,4]{1,0:T(8,128)},...) custom-call(s32[416]{0:T(512)} %slot_ref.5, ...), custom_call_target="tpu_custom_call" | custom-call | tf_op jit(solution)/shard_map/open_pass/pallas_call | solution.py:924
  141.4 13.6 %chain_forward.1.incoming_ref = f32[3,1024]{1,0:T(4,128)} custom-call(f32[3,1024]{1,0:T(4,128)} %get-tuple-element.54.own_ref, f32[11,1024]{1,0:T(8,128)} %vec_ref.9, f32[16,4]{1,0:T(8,128)} %get-tuple-element.55.link_ref, f32[1,4]{1,0:T(1,128)} %get-tuple-element.56.flag_ref), custom_call_target="tpu_custom_call" | custom-call | tf_op jit(solution)/shard_map/chain_forward/pallas_call | solution.py:1499
  155.0 44.0 %middle_pass.1 = (bf16[256,1024]{1,0:T(8,128)(2,1)}, f32[272,1024]{1,0:T(8,128)}, f32[272,1024]{1,0:T(8,128)}, f32[272,1024]{1,0:T(8,128)}, f32[272,1024]{1,0:T(...) custom-call(s32[416]{0:T(512)} %slot_ref.5, ...), custom_call_target="tpu_custom_call" | custom-call | tf_op jit(solution)/shard_map/middle_pass/pallas_call | solution.py:1215
  199.0 15.5 %chain_backward.1.incoming_ref = f32[3,1024]{1,0:T(4,128)} custom-call(f32[3,1024]{1,0:T(4,128)} %get-tuple-element.65.own_ref, f32[11,1024]{1,0:T(8,128)} %vec_ref.9, f32[16,4]{1,0:T(8,128)} %get-tuple-element.55.link_ref, f32[1,4]{1,0:T(1,128)} %get-tuple-element.56.flag_ref), custom_call_target="tpu_custom_call" | custom-call | tf_op jit(solution)/shard_map/chain_backward/pallas_call | solution.py:1499
  214.5 19.4 %close_pass.1 = (f32[256,1024]{1,0:T(8,128)}, f32[11,1024]{1,0:T(8,128)}, bf16[480,32,1024]{2,1,0:T(8,128)(2,1)}) custom-call(s32[416]{0:T(512)} %slot_ref.5, bf16[272,1024]{1,0:T(8,128)(2,1)} %get-tuple-element.50.x_ref, f32[11,1024]{1,0:T(8,128)} %vec_ref.9, f32[272,4]{1,0:T(8,128)} %get-tuple-element.52.marks_ref, ...), custom_call_target="tpu_custom_call", output_to_operand_aliasing={{2}: (21, {})} | custom-call | tf_op jit(solution)/shard_map/close_pass/pallas_call | solution.py:1395
  233.9 0.0 copy-start.5
  233.9 0.0 copy-start
  233.9 129.0 %scatter_blocks.1 = (bf16[15,32,1024]{2,1,0:T(8,128)(2,1)}, f32[11,1024]{1,0:T(8,128)}) custom-call(bf16[32,15,32,1024]{3,2,1,0:T(8,128)(2,1)} %bitcast.5, f32[11,1024]{1,0:T(8,128)} %get-tuple-element.81.rows_ref), custom_call_target="tpu_custom_call" | custom-call | tf_op jit(solution)/shard_map/scatter_blocks/pallas_call | solution.py:570
  363.0 0.0 copy-done.5
  363.0 0.2 compare_reduce_fusion
  363.2 0.0 copy-done
  363.2 0.0 copy-start.1
  363.2 0.0 copy-start.2
  363.2 0.0 copy-start.3
  363.2 0.0 copy-start.4
  363.2 0.0 copy-start.6
  363.2 6.3 %multiply_subtract_fusion = (f32[15,32,1024]{2,1,0:T(8,128)}, f32[15,32,1024]{2,1,0:T(8,128)}, f32[15,32,1024]{2,1,0:T(8,128)}) fusion(f32[15,32,1024]{2,1,0:T(8,128)S(1)} %copy-done, bf16[15,32,1024]{2,1,0:T(8,128)(2,1)} %get-tuple-element.82, pred[15]{0:T(512)(128)(4,1)S(1)} %compare_reduce_fusion, f32[15,32,1024]{2,1,0:T(8,128)} %param.18, ...), kind=kLoop, calls=%fused_computation.2 | loop fusion | flops 8355840 | bytes 12779535 | tf_op jit(solution)/shard_map/sub | solution.py:53
  369.5 0.0 copy-done.1
  369.5 0.0 copy-done.2
  369.5 0.0 copy-done.3
  369.6 0.0 copy-done.4
  369.6 0.0 copy-done.6
  369.6 0.7 multiply_subtract_fusion.1
  (1 shorter events, 0.0 us)
Async XLA Ops:
  233.9 129.1 %copy-start.5 = (s32[416]{0:T(512)S(1)}, s32[416]{0:T(512)}, u32[]{:S(2)}) copy-start(s32[416]{0:T(512)} %slot_ref.5) | copy-start | bytes 4996
  233.9 129.3 %copy-start = (f32[15,32,1024]{2,1,0:T(8,128)S(1)}, f32[15,32,1024]{2,1,0:T(8,128)}, u32[]{:S(2)}) copy-start(f32[15,32,1024]{2,1,0:T(8,128)} %param.16) | copy-start | bytes 5898244
  363.2 6.4 %copy-start.1 = (f32[11,1024]{1,0:T(8,128)S(1)}, f32[11,1024]{1,0:T(8,128)}, u32[]{:S(2)}) copy-start(f32[11,1024]{1,0:T(8,128)} %vec_ref.9) | copy-start | bytes 135172
  363.2 6.4 %copy-start.2 = (f32[11,1024]{1,0:T(8,128)S(1)}, f32[11,1024]{1,0:T(8,128)}, u32[]{:S(2)}) copy-start(f32[11,1024]{1,0:T(8,128)} %param.22) | copy-start | bytes 135172
  363.2 6.4 %copy-start.3 = (f32[11,1024]{1,0:T(8,128)S(1)}, f32[11,1024]{1,0:T(8,128)}, u32[]{:S(2)}) copy-start(f32[11,1024]{1,0:T(8,128)} %param.21) | copy-start | bytes 135172
  363.2 6.4 %copy-start.4 = (f32[11,1024]{1,0:T(8,128)S(1)}, f32[11,1024]{1,0:T(8,128)}, u32[]{:S(2)}) copy-start(f32[11,1024]{1,0:T(8,128)} %get-tuple-element.83) | copy-start | bytes 135172
  363.2 6.4 %copy-start.6 = (f32[11]{0:T(128)S(1)}, f32[11]{0:T(128)}, u32[]{:S(2)}) copy-start(f32[11]{0:T(128)} %constant.10.clone) | copy-start | bytes 136

commit v4 on v3

--- a/solution.py
+++ b/solution.py
@@ -65,7 +65,12 @@
     cuts = [0, side, 2 * side, slots]
     return [(cuts[i], cuts[i + 1] - cuts[i]) for i in range(3)]
 
-def gather_kernel(slots, own_ref, x_ref, grad_ref, out_ref, after_ref, after_grad_ref, before_ref, *scratch):
+def gather_kernel(
+    slots, doc_ref, master_ref, tokens_ref, cot_ref, pad_ref, vec_ref,
+    out_ref, x_ref, grad_ref, marks_ref, chunk_ref, link_ref, flag_ref, in_key, in_value, in_recept,
+    column, ext, wide, wide_grad, own_ref, head_grad, after_ref, after_grad_ref, before_ref,
+    *scratch,
+):
     send_sem, recv_sem, sib_send, sib_recv, own_sem, halo_send, halo_recv = scratch
     me, core, x, y, z = grid_place()
     sib = me + 1 - 2 * core
@@ -93,15 +98,22 @@
     def _():
         pl.semaphore_signal(bar, inc=1, device_id=(me - 1,), device_id_type=MESH)
 
+    def lower(s, carry):
+        own_ref[s] = master_ref[s].astype(own_ref.dtype)
+        return carry
+
+    lax.fori_loop(0, slots, lower, 0)
+    mask_column(pad_ref, column)
+    head_grad[...] = (cot_ref[0:ROW_TILE].astype(jnp.float32) * column[0:ROW_TILE]).astype(jnp.bfloat16)
     halos = jnp.where(more, 1, 0) + jnp.where(less, 1, 0)
     pl.semaphore_wait(bar, 4 + jnp.where((z > 0) & (z < 3), 1, 0) + halos)
-    tokens = x_ref.shape[0]
+    tokens = tokens_ref.shape[0]
 
     def halo_copy(k):
         src, dst, peer = (
-            (x_ref.at[pl.ds(0, 16)], after_ref, me - 1),
-            (grad_ref.at[pl.ds(0, 16)], after_grad_ref, me - 1),
-            (x_ref.at[pl.ds(tokens - 16, 16)], before_ref, me + 1),
+            (tokens_ref.at[pl.ds(0, ROW_TILE)], after_ref, me - 1),
+            (head_grad, after_grad_ref, me - 1),
+            (tokens_ref.at[pl.ds(tokens - ROW_TILE, ROW_TILE)], before_ref, me + 1),
         )[k]
         return pltpu.make_async_remote_copy(src_ref=src, dst_ref=dst, send_sem=halo_send.at[k],
             recv_sem=halo_recv.at[k], device_id=(peer,), device_id_type=MESH)
@@ -160,6 +172,20 @@
     for color in range(3):
         go(send_sib(x, y, z, color, True))
 
+    @pl.when(less)
+    def _():
+        for k in (0, 1):
+            halo_copy(k).start()
+
+    @pl.when(more)
+    def _():
+        halo_copy(2).start()
+
+    marks = (marks_ref, chunk_ref, link_ref, flag_ref)
+    prepare_own(
+        GRID_DEVICES, doc_ref, tokens_ref, cot_ref, column, vec_ref, x_ref, grad_ref, marks, ext, wide, wide_grad
+    )
+
     def arrive(cx, cy, cz, color):
         send(cx, cy, cz, color, 0).wait_recv()
 
@@ -187,6 +213,19 @@
     arrive(px, py, z, 2)
     last(px, py, z)
     sibling(px, py, z, 2)
+
+    def wait_halo():
+        @pl.when(less)
+        def _():
+            for k in (0, 1):
+                halo_copy(k).wait_send()
+            halo_copy(2).wait_recv()
+
+        @pl.when(more)
+        def _():
+            halo_copy(2).wait_send()
+            for k in (0, 1):
+                halo_copy(k).wait_recv()
 
     for dist in (1, 2, 3):
         sides = []
@@ -224,6 +263,12 @@
             tail_list = [(z, None)]
         else:
             tail_list = []
+        if dist == 1:
+            wait_halo()
+            lows = (in_key, in_value, in_recept)
+            prepare_halo(
+                GRID_DEVICES, after_ref, after_grad_ref, before_ref, vec_ref, x_ref, grad_ref, marks_ref, lows, ext
+            )
         def terminal(q):
             for cx, cy, color in ((x, y2, 0), (x2, y2, 0), (x2, y, 1), (x2, y2, 1), (qx, qy, 2), (x2, y2, 2)):
                 arrive(cx, cy, q, color)
@@ -238,27 +283,6 @@
             for sign in (1, -1):
                 q = z + sign * 3
                 pl.when((q >= 0) & (q < 4))(lambda q=q: terminal(q))
-    @pl.when(less)
-    def _():
-        for k in (0, 1):
-            halo_copy(k).start()
-
-    @pl.when(more)
-    def _():
-        halo_copy(2).start()
-
-    @pl.when(less)
-    def _():
-        for k in (0, 1):
-            halo_copy(k).wait_send()
-        halo_copy(2).wait_recv()
-
-    @pl.when(more)
-    def _():
-        halo_copy(2).wait_send()
-        for k in (0, 1):
-            halo_copy(k).wait_recv()
-
     for cp in own_copies:
         cp.wait()
     for color in range(3):
@@ -292,16 +316,20 @@
                     cp.wait_send()
                     cp.wait_recv()
 
-def gather_blocks(owned, tokens_in, out_grad, cid=1):
-    slots = owned.shape[0]
+def gather_blocks(masters, doc_lengths, tokens_in, cotangent, pad_rows, vectors, cid=1):
+    slots = masters.shape[0]
+    shapes, scratch = prepared_shapes(GRID_DEVICES, *tokens_in.shape)
     anywhere = pl.BlockSpec(memory_space=pl.ANY)
-    halo = jax.ShapeDtypeStruct((16,) + tokens_in.shape[1:], tokens_in.dtype)
+    vmem = pl.BlockSpec(memory_space=pltpu.VMEM)
+    halo = pltpu.VMEM((ROW_TILE,) + tokens_in.shape[1:], jnp.bfloat16)
     return pl.pallas_call(
         functools.partial(gather_kernel, slots),
-        out_shape=(jax.ShapeDtypeStruct((GRID_DEVICES,) + owned.shape, owned.dtype), halo, halo, halo),
-        in_specs=[anywhere] * 3,
-        out_specs=(anywhere,) * 4,
-        scratch_shapes=[
+        out_shape=(jax.ShapeDtypeStruct((GRID_DEVICES,) + masters.shape, jnp.bfloat16),) + shapes,
+        in_specs=[pl.BlockSpec(memory_space=pltpu.SMEM)] + [vmem] * 5,
+        out_specs=(anywhere,) + (vmem,) * len(shapes),
+        scratch_shapes=scratch + [
+            pltpu.VMEM(masters.shape, jnp.bfloat16),
+            halo, halo, halo, halo,
             pltpu.SemaphoreType.DMA((16, 3, 4)),
             pltpu.SemaphoreType.DMA((16, 3)),
             pltpu.SemaphoreType.DMA((16, 3)),
@@ -310,9 +338,9 @@
             pltpu.SemaphoreType.DMA((3,)),
             pltpu.SemaphoreType.DMA((3,)),
         ],
-        compiler_params=pltpu.CompilerParams(collective_id=cid, has_side_effects=True),
+        compiler_params=pltpu.CompilerParams(collective_id=cid, has_side_effects=True, vmem_limit_bytes=VMEM_BYTES),
         name="gather_blocks",
-    )(owned, tokens_in, out_grad)
+    )(doc_lengths, masters, tokens_in, cotangent, pad_rows, vectors)
 
 
 def scatter_kernel(
@@ -823,62 +851,118 @@
     flag_ref[:, 3:4] = none_between(offsets, pair + own + 1, pair + 2 * own)
 
 
-def open_kernel(
-    devices,
-    slot_ref, doc_ref, tokens_ref, grads_ref, after_ref, after_grad_ref, before_ref, vec_ref, pool_ref,
-    x_ref, grad_ref, marks_ref, chunk_ref, link_ref, flag_ref,
-    key_ref, value_ref, recept_ref, num_ref, den_ref, max_ref, in_key, in_value, in_recept, prefix_ref, summary_ref,
-    ext, wide, wide_grad, store, sem,
-):
+def mask_column(pad_ref, column):
+    for k in range(pad_ref.shape[0]):
+        row = pad_ref[k : k + 1].astype(jnp.float32)
+        column[k * LANES : (k + 1) * LANES] = jnp.broadcast_to(row, (LANES, LANES)).T[:, 0:1]
+
+
+def normed_rows(x_ref, vec_ref, ext, first, size, tile):
+    x_ref[pl.ds(first, size)] = tile.astype(jnp.bfloat16)
+    unit, _ = unit_norm(tile)
+    ext[pl.ds(pl.multiple_of(first + 8, 8), size)] = unit * vec_ref[0:1] + vec_ref[1:2]
+
+
+def prepare_own(devices, doc_ref, tokens_ref, grads_ref, column, vec_ref, x_ref, grad_ref, marks, ext, wide, wide_grad):
+    rows = x_ref.shape[0]
+    own = rows - ROW_TILE
+    length = own // CHUNKS
+    write_marks(doc_ref, *marks, own, devices)
+
+    def widen(first, size):
+        at = pl.ds(first, size)
+        put_rows(wide, at, tokens_ref[at].astype(jnp.float32))
+        put_rows(wide_grad, at, grads_ref[at].astype(jnp.float32) * column[at])
+
+    for_rows(rows, widen)
+
+    def arrange(first, size):
+        steps = [first // CHUNKS + k for k in range(size // CHUNKS)]
+        tile = jnp.concatenate([take_step(wide, i, length) for i in steps], axis=0)
+        normed_rows(x_ref, vec_ref, ext, first, size, tile)
+        tile = jnp.concatenate([take_step(wide_grad, i, length) for i in steps], axis=0)
+        grad_ref[pl.ds(first, size)] = tile.astype(jnp.bfloat16)
+
+    for_rows(rows, arrange)
+
+
+def prepare_halo(devices, after_ref, after_grad_ref, before_ref, vec_ref, x_ref, grad_ref, marks_ref, lows, ext):
     rows, features = x_ref.shape
     own = rows - ROW_TILE
-    tiles = rows // ROW_TILE
+    me = lax.axis_index("seq")
+    more, less = me < devices - 1, me > 0
+    later = jnp.where(more, after_ref[...].astype(jnp.float32), 0.0)[0:2]
+    earlier = jnp.where(less, before_ref[...].astype(jnp.float32), 0.0)
+    blank_rows = jnp.zeros((ROW_TILE - 4, features), jnp.float32)
+    tile = jnp.concatenate(
+        [later, earlier[ROW_TILE - 1 :], earlier[ROW_TILE - 2 : ROW_TILE - 1], blank_rows], axis=0
+    )
+    normed_rows(x_ref, vec_ref, ext, own, ROW_TILE, tile)
+    later_grad = jnp.where(more, after_grad_ref[...].astype(jnp.float32), 0.0)[0:2]
+    grad_ref[own:rows] = jnp.concatenate([later_grad, blank_rows, blank_rows[:2]], axis=0).astype(jnp.bfloat16)
+    shift_in(ext, own)
+
+    def mix(first, size, here, before):
+        for row, ref in zip((2, 3, 4), lows):
+            weight = vec_ref[row : row + 1]
+            ref[pl.ds(first, size)] = (weight * here + (1.0 - weight) * before).astype(jnp.bfloat16)
+
+    for_rows(rows, lambda first, size: mix(first, size, *normed_pair(ext, marks_ref, first, size)))
+    mix(own, ROW_TILE, ext[own + 8 : own + 8 + ROW_TILE], halo_previous(ext, own, features) * marks_ref[own:rows, 1:2])
+
+
+def prepared_shapes(devices, own, features):
+    rows = own + ROW_TILE
+    count = devices // 2 if devices == GRID_DEVICES else devices
+    low = jax.ShapeDtypeStruct((rows, features), jnp.bfloat16)
+    small = lambda *shape: jax.ShapeDtypeStruct(shape, jnp.float32)
+    shapes = (low, low, small(rows, 4), small(CHUNKS, 6), small(count, 4), small(1, 4), low, low, low)
+    scratch = [
+        pltpu.VMEM((own, 1), jnp.float32),
+        pltpu.VMEM((rows + 8, features), jnp.float32),
+        pltpu.VMEM((features // LANES, own, LANES), jnp.float32),
+        pltpu.VMEM((features // LANES, own, LANES), jnp.float32),
+    ]
+    return shapes, scratch
+
+
+def prepare_kernel(
+    devices, doc_ref, tokens_ref, grads_ref, pad_ref, after_ref, after_grad_ref, before_ref, vec_ref,
+    x_ref, grad_ref, marks_ref, chunk_ref, link_ref, flag_ref, in_key, in_value, in_recept,
+    column, ext, wide, wide_grad,
+):
+    mask_column(pad_ref, column)
+    marks = (marks_ref, chunk_ref, link_ref, flag_ref)
+    prepare_own(devices, doc_ref, tokens_ref, grads_ref, column, vec_ref, x_ref, grad_ref, marks, ext, wide, wide_grad)
+    lows = (in_key, in_value, in_recept)
+    prepare_halo(devices, after_ref, after_grad_ref, before_ref, vec_ref, x_ref, grad_ref, marks_ref, lows, ext)
+
+
+def prepare_pass(devices, doc_lengths, tokens_in, cotangent, pad_rows, halo, vectors):
+    shapes, scratch = prepared_shapes(devices, *tokens_in.shape)
+    vmem = pl.BlockSpec(memory_space=pltpu.VMEM)
+    return pl.pallas_call(
+        functools.partial(prepare_kernel, devices),
+        out_shape=shapes,
+        in_specs=[pl.BlockSpec(memory_space=pltpu.SMEM)] + [vmem] * 7,
+        out_specs=(vmem,) * len(shapes),
+        scratch_shapes=scratch,
+        compiler_params=pltpu.CompilerParams(vmem_limit_bytes=VMEM_BYTES),
+        name="prepare_pass",
+    )(doc_lengths, tokens_in, cotangent, pad_rows, *halo, vectors)
+
+
+def open_kernel(
+    slot_ref, vec_ref, marks_ref, chunk_ref, in_key, in_value, in_recept, pool_ref,
+    key_ref, value_ref, recept_ref, num_ref, den_ref, max_ref, prefix_ref, summary_ref,
+    store, sem,
+):
+    rows, features = in_key.shape
+    own = rows - ROW_TILE
     length = own // CHUNKS
     per = EMBED_SIZE // BLOCK_ROWS
     for m in range(3):
         fetch_blocks(slot_ref, pool_ref, store, sem.at[m], m * per, m * per, per)
-    write_marks(doc_ref, marks_ref, chunk_ref, link_ref, flag_ref, own, devices)
-    me = lax.axis_index("seq")
-
-    def widen(first, size):
-        at = pl.ds(first, size)
-        put_rows(wide, at, tokens_ref[at].astype(jnp.float32))
-        put_rows(wide_grad, at, grads_ref[at].astype(jnp.float32))
-
-    for_rows(rows, widen)
-
-    def norm(first, size, tile):
-        x_ref[pl.ds(first, size)] = tile.astype(jnp.bfloat16)
-        unit, _ = unit_norm(tile)
-        ext[pl.ds(pl.multiple_of(first + 8, 8), size)] = unit * vec_ref[0:1] + vec_ref[1:2]
-
-    def arrange(first, size):
-        steps = [first // CHUNKS + k for k in range(size // CHUNKS)]
-        norm(first, size, jnp.concatenate([take_step(wide, i, length) for i in steps], axis=0))
-        tile = jnp.concatenate([take_step(wide_grad, i, length) for i in steps], axis=0)
-        grad_ref[pl.ds(first, size)] = tile.astype(jnp.bfloat16)
-
-    for_rows(rows, arrange)
-    more, less = me < devices - 1, me > 0
-    later = jnp.where(more, after_ref[...].astype(jnp.float32), 0.0)[0:2]
-    earlier = jnp.where(less, before_ref[...].astype(jnp.float32), 0.0)
-    blank_rows = jnp.zeros((ROW_TILE - 4, features), jnp.float32)
-    norm(
-        own,
-        ROW_TILE,
-        jnp.concatenate([later, earlier[ROW_TILE - 1 :], earlier[ROW_TILE - 2 : ROW_TILE - 1], blank_rows], axis=0),
-    )
-    later_grad = jnp.where(more, after_grad_ref[...].astype(jnp.float32), 0.0)[0:2]
-    grad_ref[own:rows] = jnp.concatenate([later_grad, blank_rows, blank_rows[:2]], axis=0).astype(jnp.bfloat16)
-    shift_in(ext, own)
-
-    def mix(first, size, here, before):
-        for row, ref in ((2, in_key), (3, in_value), (4, in_recept)):
-            weight = vec_ref[row : row + 1]
-            ref[pl.ds(first, size)] = (weight * here + (1.0 - weight) * before).astype(jnp.bfloat16)
-
-    for_rows(rows, lambda first, size: mix(first, size, *normed_pair(ext, marks_ref, first, size)))
-    mix(own, ROW_TILE, ext[own + 8 : own + 8 + ROW_TILE], halo_previous(ext, own, features) * marks_ref[own:rows, 1:2])
     for m, (left, out) in enumerate(((in_key, key_ref), (in_value, value_ref), (in_recept, recept_ref))):
         await_blocks(pool_ref, store, sem.at[m], m * per, per)
 
@@ -911,34 +995,25 @@
     summary_ref[...] = jnp.concatenate(last, axis=0)
 
 
-def open_pass(devices, slots, doc_lengths, tokens_in, out_grad, halo, vectors, pool):
-    own, features = tokens_in.shape
-    rows = own + ROW_TILE
-    count = devices // 2 if devices == GRID_DEVICES else devices
+def open_pass(slots, vectors, marks, chunk_marks, lows, pool):
+    rows, features = lows[0].shape
+    own = rows - ROW_TILE
     full = jax.ShapeDtypeStruct((rows, features), jnp.float32)
     part = jax.ShapeDtypeStruct((own, features), jnp.float32)
-    low = jax.ShapeDtypeStruct((rows, features), jnp.bfloat16)
     small = lambda *shape: jax.ShapeDtypeStruct(shape, jnp.float32)
     vmem = pl.BlockSpec(memory_space=pltpu.VMEM)
-    smem = pl.BlockSpec(memory_space=pltpu.SMEM)
     return pl.pallas_call(
-        functools.partial(open_kernel, devices),
-        out_shape=(
-            low, low, small(rows, 4), small(CHUNKS, 6), small(count, 4), small(1, 4),
-            full, full, full, part, part, part, low, low, low, small(3, CHUNKS, features), small(3, features),
-        ),
-        in_specs=[smem] * 2 + [vmem] * 6 + [pl.BlockSpec(memory_space=pl.ANY)],
-        out_specs=(vmem,) * 17,
+        open_kernel,
+        out_shape=(full, full, full, part, part, part, small(3, CHUNKS, features), small(3, features)),
+        in_specs=[pl.BlockSpec(memory_space=pltpu.SMEM)] + [vmem] * 6 + [pl.BlockSpec(memory_space=pl.ANY)],
+        out_specs=(vmem,) * 8,
         scratch_shapes=[
-            pltpu.VMEM((rows + 8, features), jnp.float32),
-            pltpu.VMEM((features // LANES, own, LANES), jnp.float32),
-            pltpu.VMEM((features // LANES, own, LANES), jnp.float32),
             pltpu.VMEM((3 * EMBED_SIZE // BLOCK_ROWS, BLOCK_ROWS, features), jnp.bfloat16),
             pltpu.SemaphoreType.DMA((3,)),
         ],
         compiler_params=pltpu.CompilerParams(vmem_limit_bytes=VMEM_BYTES),
         name="open_pass",
-    )(slots, doc_lengths, tokens_in, out_grad, *halo, vectors, pool)
+    )(slots, vectors, marks, chunk_marks, *lows, pool)
 
 
 def middle_kernel(
@@ -1529,22 +1604,24 @@
     tokens, features = tokens_in.shape
     devices = lax.axis_size("seq")
     device_place = lax.axis_index("seq")
-    owned_rows = masters.astype(jnp.bfloat16)
-    out_grad = cotangent * pad_mask.astype(cotangent.dtype)[:, None]
+    pad_rows = pad_mask.reshape(-1, LANES)
     if devices == GRID_DEVICES:
-        gathered, *halo = gather_blocks(owned_rows, tokens_in, out_grad)
+        gathered, *prepared = gather_blocks(masters, doc_lengths, tokens_in, cotangent, pad_rows, vectors)
         gathered = gathered.reshape(-1, BLOCK_ROWS, features)
     else:
-        gathered = lax.all_gather(owned_rows, "seq", axis=0, tiled=True)
+        gathered = lax.all_gather(masters.astype(jnp.bfloat16), "seq", axis=0, tiled=True)
+        head_grad = cotangent[:ROW_TILE] * pad_mask[:ROW_TILE].astype(cotangent.dtype)[:, None]
         halo = [
             shifted(tokens_in[:ROW_TILE], "seq", -1),
-            shifted(out_grad[:ROW_TILE], "seq", -1),
+            shifted(head_grad, "seq", -1),
             shifted(tokens_in[tokens - ROW_TILE :], "seq", 1),
         ]
-    (
-        x_rows, grad_rows, marks, chunk_marks, links, flags,
-        key, value, recept, num, den, top, in_key, in_value, in_recept, prefix, summary,
-    ) = open_pass(devices, block_slot, doc_lengths, tokens_in, out_grad, halo, vectors, gathered)
+        prepared = prepare_pass(devices, doc_lengths, tokens_in, cotangent, pad_rows, halo, vectors)
+    x_rows, grad_rows, marks, chunk_marks, links, flags, *lows = prepared
+    lows = tuple(lows)
+    key, value, recept, num, den, top, prefix, summary = open_pass(
+        block_slot, vectors, marks, chunk_marks, lows, gathered
+    )
     incoming = chain_state(summary, vectors, links, flags, True, tokens, 3)
     (
         layer_out, resid_grad, wkv, gw, own_share, recept_grad, suffix, back_summary, sums_two,
@@ -1556,7 +1633,7 @@
     back_incoming = chain_state(back_summary, vectors, links, flags, False, tokens, 4)
     input_grad, stacked, slot_grad = close_pass(
         block_slot, x_rows, vectors, marks, chunk_marks, back_incoming, suffix, key, value,
-        (in_key, in_value, in_recept),
+        lows,
         (resid_grad, wkv, gw, own_share, recept_grad, sums_two, full_state, back_state),
         gathered, slot_grad,
     )

time: 371 us -> 364 us (0.981)
  other arithmetic: 12.5 us -> 7.22 us
where the time goes in v4:
time: 364 us
  Pallas kernels  356 us (98%)
  other arithmetic  7.22 us (2%)
    pallas_call x1, Pallas kernels, scatter_blocks(): pl.pallas_call(functools.partial(scatter_kernel, slots), out_shape=(jax.S...  129 us
    pallas_call x1, Pallas kernels, gather_blocks(): pl.pallas_call(functools.partial(gather_kernel, slots), out_shape=(jax.Sh...  124 us
    pallas_call x1, Pallas kernels, middle_pass(): pl.pallas_call(middle_kernel, out_shape=(jax.ShapeDtypeStruct((own, featu...  43.9 us
    pallas_call x2, Pallas kernels, chain_state(): pl.pallas_call(functools.partial(chain_kernel, forward, tokens), out_shap...  27.8 us
    pallas_call x1, Pallas kernels, close_pass(): pl.pallas_call(close_kernel, out_shape=(jax.ShapeDtypeStruct((own, featur...  19.4 us
    pallas_call x1, Pallas kernels, open_pass(): pl.pallas_call(open_kernel, out_shape=(full, full, full, part, part, part...  11.6 us

profile of v4, /device:TPU:0, one launch (start us, length us, event | category | flops | bytes accessed | tf_op | source)
XLA Modules:
  0.0 363.9 jit_solution(496598938640806420)
XLA Ops:
  0.6 124.1 %gather_blocks.1 = (bf16[32,15,32,1024]{3,2,1,0:T(8,128)(2,1)}, bf16[272,1024]{1,0:T(8,128)(2,1)}, bf16[272,1024]{1,0:T(8,128)(2,1)}, f32[272,4]{1,0:T(8,128)}, ...) custom-call(s32[7]{0:T(128)} %doc_ref.1, ...), custom_call_target="tpu_custom_call" | custom-call | tf_op jit(solution)/shard_map/gather_blocks/pallas_call | solution.py:325
  124.8 11.6 %open_pass.1 = (f32[272,1024]{1,0:T(8,128)}, f32[272,1024]{1,0:T(8,128)}, f32[272,1024]{1,0:T(8,128)}, f32[256,1024]{1,0:T(8,128)}, f32[256,1024]{1,0:T(8,128)},...) custom-call(s32[416]{0:T(512)} %slot_ref.5, f32[11,1024]{1,0:T(8,128)} %vec_ref.11, ...), custom_call_target="tpu_custom_call" | custom-call | tf_op jit(solution)/shard_map/open_pass/pallas_call | solution.py:1005
  136.3 12.4 %chain_forward.1.incoming_ref = f32[3,1024]{1,0:T(4,128)} custom-call(f32[3,1024]{1,0:T(4,128)} %get-tuple-element.51.own_ref, f32[11,1024]{1,0:T(8,128)} %vec_ref.11, f32[16,4]{1,0:T(8,128)} %get-tuple-element.52.link_ref, f32[1,4]{1,0:T(1,128)} %get-tuple-element.53.flag_ref), custom_call_target="tpu_custom_call" | custom-call | tf_op jit(solution)/shard_map/chain_forward/pallas_call | solution.py:1574
  148.8 43.9 %middle_pass.1 = (bf16[256,1024]{1,0:T(8,128)(2,1)}, f32[272,1024]{1,0:T(8,128)}, f32[272,1024]{1,0:T(8,128)}, f32[272,1024]{1,0:T(8,128)}, f32[272,1024]{1,0:T(...) custom-call(s32[416]{0:T(512)} %slot_ref.5, ...), custom_call_target="tpu_custom_call" | custom-call | tf_op jit(solution)/shard_map/middle_pass/pallas_call | solution.py:1290
  192.7 15.4 %chain_backward.1.incoming_ref = f32[3,1024]{1,0:T(4,128)} custom-call(f32[3,1024]{1,0:T(4,128)} %get-tuple-element.62.own_ref, f32[11,1024]{1,0:T(8,128)} %vec_ref.11, f32[16,4]{1,0:T(8,128)} %get-tuple-element.52.link_ref, f32[1,4]{1,0:T(1,128)} %get-tuple-element.53.flag_ref), custom_call_target="tpu_custom_call" | custom-call | tf_op jit(solution)/shard_map/chain_backward/pallas_call | solution.py:1574
  208.1 19.4 %close_pass.1 = (f32[256,1024]{1,0:T(8,128)}, f32[11,1024]{1,0:T(8,128)}, bf16[480,32,1024]{2,1,0:T(8,128)(2,1)}) custom-call(s32[416]{0:T(512)} %slot_ref.5, bf16[272,1024]{1,0:T(8,128)(2,1)} %get-tuple-element.43.x_ref, f32[11,1024]{1,0:T(8,128)} %vec_ref.11, f32[272,4]{1,0:T(8,128)} %get-tuple-element.45.marks_ref, ...), custom_call_target="tpu_custom_call", output_to_operand_aliasing={{2}: (21, {})} | custom-call | tf_op jit(solution)/shard_map/close_pass/pallas_call | solution.py:1470
  227.6 0.0 copy-start.5
  227.6 0.0 copy-start
  227.6 129.0 %scatter_blocks.1 = (bf16[15,32,1024]{2,1,0:T(8,128)(2,1)}, f32[11,1024]{1,0:T(8,128)}) custom-call(bf16[32,15,32,1024]{3,2,1,0:T(8,128)(2,1)} %bitcast.6, f32[11,1024]{1,0:T(8,128)} %get-tuple-element.75.rows_ref), custom_call_target="tpu_custom_call" | custom-call | tf_op jit(solution)/shard_map/scatter_blocks/pallas_call | solution.py:598
  356.6 0.0 copy-done.5
  356.6 0.2 compare_reduce_fusion
  356.8 0.0 copy-done
  356.8 0.0 copy-start.1
  356.8 0.0 copy-start.2
  356.9 0.0 copy-start.3
  356.9 0.0 copy-start.4
  356.9 0.0 copy-start.6
  356.9 6.3 %multiply_subtract_fusion = (f32[15,32,1024]{2,1,0:T(8,128)}, f32[15,32,1024]{2,1,0:T(8,128)}, f32[15,32,1024]{2,1,0:T(8,128)}) fusion(f32[15,32,1024]{2,1,0:T(8,128)S(1)} %copy-done, bf16[15,32,1024]{2,1,0:T(8,128)(2,1)} %get-tuple-element.76, pred[15]{0:T(512)(128)(4,1)S(1)} %compare_reduce_fusion, f32[15,32,1024]{2,1,0:T(8,128)} %param.18, ...), kind=kLoop, calls=%fused_computation.2 | loop fusion | flops 8355840 | bytes 12779535 | tf_op jit(solution)/shard_map/sub | solution.py:53
  363.2 0.0 copy-done.1
  363.2 0.0 copy-done.2
  363.2 0.0 copy-done.3
  363.2 0.0 copy-done.4
  363.2 0.0 copy-done.6
  363.2 0.7 multiply_subtract_fusion.1
  (1 shorter events, 0.0 us)
Async XLA Ops:
  227.6 129.1 %copy-start.5 = (s32[416]{0:T(512)S(1)}, s32[416]{0:T(512)}, u32[]{:S(2)}) copy-start(s32[416]{0:T(512)} %slot_ref.5) | copy-start | bytes 4996
  227.6 129.3 %copy-start = (f32[15,32,1024]{2,1,0:T(8,128)S(1)}, f32[15,32,1024]{2,1,0:T(8,128)}, u32[]{:S(2)}) copy-start(f32[15,32,1024]{2,1,0:T(8,128)} %master_ref.1) | copy-start | bytes 5898244
  356.8 6.4 %copy-start.1 = (f32[11,1024]{1,0:T(8,128)S(1)}, f32[11,1024]{1,0:T(8,128)}, u32[]{:S(2)}) copy-start(f32[11,1024]{1,0:T(8,128)} %vec_ref.11) | copy-start | bytes 135172
  356.8 6.4 %copy-start.2 = (f32[11,1024]{1,0:T(8,128)S(1)}, f32[11,1024]{1,0:T(8,128)}, u32[]{:S(2)}) copy-start(f32[11,1024]{1,0:T(8,128)} %param.22) | copy-start | bytes 135172
  356.9 6.4 %copy-start.3 = (f32[11,1024]{1,0:T(8,128)S(1)}, f32[11,1024]{1,0:T(8,128)}, u32[]{:S(2)}) copy-start(f32[11,1024]{1,0:T(8,128)} %param.21) | copy-start | bytes 135172
  356.9 6.4 %copy-start.4 = (f32[11,1024]{1,0:T(8,128)S(1)}, f32[11,1024]{1,0:T(8,128)}, u32[]{:S(2)}) copy-start(f32[11,1024]{1,0:T(8,128)} %get-tuple-element.77) | copy-start | bytes 135172
  356.9 6.4 %copy-start.6 = (f32[11]{0:T(128)S(1)}, f32[11]{0:T(128)}, u32[]{:S(2)}) copy-start(f32[11]{0:T(128)} %constant.10.clone) | copy-start | bytes 136

commit v5 on v4

--- a/solution.py
+++ b/solution.py
@@ -67,7 +67,7 @@
 
 def gather_kernel(
     slots, doc_ref, master_ref, tokens_ref, cot_ref, pad_ref, vec_ref,
-    out_ref, x_ref, grad_ref, marks_ref, chunk_ref, link_ref, flag_ref, in_key, in_value, in_recept,
+    out_ref, x_ref, grad_ref, marks_ref, chunk_ref, link_ref, in_key, in_value, in_recept,
     column, ext, wide, wide_grad, own_ref, head_grad, after_ref, after_grad_ref, before_ref,
     *scratch,
 ):
@@ -181,7 +181,7 @@
     def _():
         halo_copy(2).start()
 
-    marks = (marks_ref, chunk_ref, link_ref, flag_ref)
+    marks = (marks_ref, chunk_ref, link_ref)
     prepare_own(
         GRID_DEVICES, doc_ref, tokens_ref, cot_ref, column, vec_ref, x_ref, grad_ref, marks, ext, wide, wide_grad
     )
@@ -343,9 +343,19 @@
     )(doc_lengths, masters, tokens_in, cotangent, pad_rows, vectors)
 
 
+def scatter_spans(slots):
+    side = 4 * slots // 15
+    cuts = [0, side, 2 * side, 2 * side + (slots - 2 * side + 1) // 2, slots]
+    return [(cuts[i], cuts[i + 1] - cuts[i]) for i in range(4)]
+
+
 def scatter_kernel(
-    slots, part_ref, rows_ref, out_ref, total_ref, acc, sib, xin, yin, zin, sums,
-    load_sem, sib_send, sib_recv, send_sem, xsem, ysem, zsem, row_send, row_recv,
+    slots, part_ref, rows_ref, vec_ref, marks_ref, x_hbm, resid_hbm, key_hbm, value_hbm, recept_hbm, weights_hbm,
+    out_ref, total_ref, input_hbm,
+    acc, ring, ub, uc, ud, va, vc, vd, zs, zc, zd, sums,
+    x_ref, resid_ref, key_grad, value_grad, recept_grad, weights, grad_key_in, grad_value_in, grad_recept_in,
+    ext, unit, inverse, carried, wide, input_ref,
+    load_sem, sib_send, sib_recv, send_sem, usem, vsem, zsem, row_send, row_recv, tail_sem, input_sem,
 ):
     me, core, x, y, z = grid_place()
     sibling = me + 1 - 2 * core
@@ -365,10 +375,19 @@
     far = me + 16 - 32 * (z // 2)
     pl.semaphore_signal(bar, inc=1, device_id=(far,), device_id_type=MESH)
     row_peers = (sibling, x_peer, y_peer, me + 8 - 16 * lax.rem(z, 2), far)
-    sums[0] = rows_ref[...]
-    span = spans(slots)
-    x2, y2 = 1 - x, 1 - y
-    is0, is1 = core == 0, core == 1
+    tail_loads = [
+        pltpu.make_async_copy(src, dst, tail_sem.at[k])
+        for k, (src, dst) in enumerate(
+            (
+                (key_hbm, key_grad), (value_hbm, value_grad), (recept_hbm, recept_grad),
+                (x_hbm, x_ref), (resid_hbm, resid_ref), (weights_hbm, weights),
+            )
+        )
+    ]
+    span = scatter_spans(slots)
+    u, v = jnp.where(core == 0, x, y), jnp.where(core == 0, y, x)
+    u_peer, v_peer = jnp.where(core == 0, x_peer, y_peer), jnp.where(core == 0, y_peer, x_peer)
+    u2, v2 = 1 - u, 1 - v
 
     def row_copy(k):
         return pltpu.make_async_remote_copy(src_ref=sums.at[2 * k], dst_ref=sums.at[2 * k + 1],
@@ -380,11 +399,16 @@
         if k < 4:
             row_copy(k + 1).start()
 
-    def load(chip):
-        return pltpu.make_async_copy(part_ref.at[2 * chip + core], acc.at[chip], load_sem.at[chip])
+    def load(i, q):
+        chip = 4 * q + plane_order()[i]
+        return pltpu.make_async_copy(part_ref.at[2 * chip + core], ring.at[i], load_sem.at[i])
+
+    def next_level(q):
+        inner = jnp.where(q == 3, jnp.where(z == 1, 2, 1), jnp.where(q == 0, jnp.where(z == 1, 1, 3), jnp.where(z == 1, 0, 2)))
+        return jnp.where(z == 0, q - 1, jnp.where(z == 3, q + 1, inner))
 
     def give(chip):
-        return pltpu.make_async_remote_copy(src_ref=part_ref.at[2 * chip + 1 - core], dst_ref=sib.at[chip],
+        return pltpu.make_async_remote_copy(src_ref=part_ref.at[2 * chip + 1 - core], dst_ref=acc.at[chip],
             send_sem=sib_send.at[chip], recv_sem=sib_recv.at[chip], device_id=(sibling,), device_id_type=MESH)
 
     levels = []
@@ -403,232 +427,282 @@
             if d == dist:
                 pl.when(have)(functools.partial(work, q, sign, dist))
 
-    def begin_loads(q):
-        for i in plane_order():
-            load(4 * q + i).start()
-
     def begin_gives(q):
         for i in plane_order():
             give(4 * q + i).start()
 
+    def chip_of(cu, cv, cz):
+        return cz * 4 + jnp.where(core == 0, cv * 2 + cu, cu * 2 + cv)
+
     def plane_order():
-        return (2 * y2 + x2, 2 * y + x2, 2 * y2 + x, 2 * y + x)
-
-    run(3, begin_loads)
-    run(2, begin_loads)
-    run(1, begin_loads)
-    begin_loads(z)
+        return (chip_of(u2, v2, 0), chip_of(u2, v, 0), chip_of(u, v2, 0), chip_of(u, v, 0))
+
+    for i in range(4):
+        load(i, jnp.where(z >= 2, 0, 3)).start()
+    for copy in tail_loads:
+        copy.start()
     pl.semaphore_wait(bar, 5 + jnp.where(zup & zdown, 1, 0))
-    row_copy(0).start()
     run(3, begin_gives)
     run(2, begin_gives)
 
-    def ready(cx, cy, q):
-        chip = chip_of(cx, cy, q)
-        load(chip).wait()
+    def ready(i, q):
+        chip = 4 * q + plane_order()[i]
+        load(i, q).wait()
         give(chip).wait_recv()
 
-        def step(s, _):
-            total = acc[chip, s].astype(jnp.float32) + sib[chip, s].astype(jnp.float32)
+        def step(s, carry):
+            total = acc[chip, s].astype(jnp.float32) + ring[i, s].astype(jnp.float32)
             acc[chip, s] = total.astype(acc.dtype)
-            return 0
+            return carry
 
         lax.fori_loop(0, slots, step, 0)
 
-    def chip_of(cx, cy, cz):
-        return (cz * 2 + cy) * 2 + cx
-
-    def out_copy(cx, cy, cz, color, target, buf, index, sem):
+        @pl.when(q != z)
+        def _():
+            load(i, next_level(q)).start()
+
+    def out_copy(cu, cv, cz, color, target, place):
         lo, n = span[color]
-        chip = chip_of(cx, cy, cz)
-        return pltpu.make_async_remote_copy(src_ref=acc.at[chip, pl.ds(lo, n)], dst_ref=buf.at[index, pl.ds(0, n)],
-            send_sem=send_sem.at[chip, color], recv_sem=sem.at[index], device_id=(target,), device_id_type=MESH)
-
-    def arrived(buf, index, sem, color):
+        chip = chip_of(cu, cv, cz)
+        buf, index, sem, flag = place
+        return pltpu.make_async_remote_copy(src_ref=acc.at[chip, pl.ds(lo, n)], dst_ref=buf.at[index],
+            send_sem=send_sem.at[chip, color], recv_sem=sem.at[flag], device_id=(target,), device_id_type=MESH)
+
+    def arrived(place, color):
         lo, n = span[color]
-        pltpu.make_async_remote_copy(src_ref=acc.at[0, pl.ds(lo, n)], dst_ref=buf.at[index, pl.ds(0, n)],
-            send_sem=send_sem.at[0, color], recv_sem=sem.at[index], device_id=(sibling,), device_id_type=MESH).wait_recv()
-
-    def add(cx, cy, cz, color, pieces):
+        buf, index, sem, flag = place
+        pltpu.make_async_remote_copy(src_ref=acc.at[0, pl.ds(lo, n)], dst_ref=buf.at[index],
+            send_sem=send_sem.at[0, color], recv_sem=sem.at[flag], device_id=(sibling,), device_id_type=MESH).wait_recv()
+
+    def add(cu, cv, cz, color, pieces):
         lo, n = span[color]
-        chip = chip_of(cx, cy, cz)
-        for buf, index, sem in pieces:
-            arrived(buf, index, sem, color)
-        def step(s, _):
+        chip = chip_of(cu, cv, cz)
+        for place in pieces:
+            arrived(place, color)
+
+        def step(s, carry):
             total = acc[chip, lo + s].astype(jnp.float32)
-            for buf, index, _sem in pieces:
+            for buf, index, _, _ in pieces:
                 total = total + buf[index, s].astype(jnp.float32)
             acc[chip, lo + s] = total.astype(acc.dtype)
-            return 0
+            return carry
+
         lax.fori_loop(0, n, step, 0)
 
-    def X(i): return (xin, i, xsem)
-    def Y(i): return (yin, i, ysem)
-    def Z(i): return (zin, i, zsem)
-
-    def term_x(q, color, i):
-        cy = (y, y2)[i]
-        out_copy(x2, cy, q, color, x_peer, xin, (8 if color == 2 else 0) + 2 * q + i, xsem).start()
-
-    def term_y(q, color, i):
-        cx = (x, x2)[i]
-        out_copy(cx, y2, q, color, y_peer, yin, (8 if color == 2 else 0) + 2 * q + i, ysem).start()
+    def UB(q, i): return (ub, 2 * q + i, usem, 2 * q + i)
+    def UD(q, i): return (ud, 2 * q + i, usem, 9 + 2 * q + i)
+    def UC(q): return (uc, q, usem, 17 + q)
+    def VA(q, i): return (va, 2 * q + i, vsem, 2 * q + i)
+    def VC(q, i): return (vc, 2 * q + i, vsem, 9 + 2 * q + i)
+    def VD(q): return (vd, q, vsem, 17 + q)
+    def Z(q, k): return ((zc, zd, zs)[min(k, 2)], q if k < 2 else 4 * q + k - 2, zsem, 6 * q + k)
+
+    def send_u(q, color, i):
+        out_copy(u2, (v, v2)[i], q, color, u_peer, UB(q, i) if color == 1 else UD(q, i)).start()
+
+    def send_v(q, color, i):
+        out_copy((u, u2)[i], v2, q, color, v_peer, VA(q, i) if color == 0 else VC(q, i)).start()
 
     def term_a(q):
-        ready(x2, y2, q)
-        term_x(q, 1, 1)
-        term_y(q, 0, 1)
+        ready(0, q)
+        send_u(q, 1, 1)
+        send_v(q, 0, 1)
 
     def term_c(q):
-
-        @pl.when(is0)
-        def _():
-            term_y(q, 2, 1)
-            term_y(q, 2, 0)
-
-        @pl.when(is1)
-        def _():
-            term_x(q, 2, 1)
-            term_x(q, 2, 0)
-
-        ready(x, y, q)
+        send_v(q, 2, 1)
+        send_u(q, 3, 1)
 
     def term_b(q):
-        ready(x2, y, q)
-        term_x(q, 1, 0)
-        ready(x, y2, q)
-        term_y(q, 0, 0)
+        ready(1, q)
+        send_u(q, 1, 0)
+        ready(2, q)
+        send_v(q, 0, 0)
+
+    def term_d(q):
+        send_u(q, 3, 0)
+        send_v(q, 2, 0)
+        ready(3, q)
 
     def plane_two(q):
-        @pl.when(is0)
-        def _():
-            add(x2, y, q, 2, [Y(8 + 2 * q + 1)])
-            out_copy(x2, y, q, 2, x_peer, xin, 8 + 2 * q, xsem).start()
-        @pl.when(is1)
-        def _():
-            add(x, y2, q, 2, [X(8 + 2 * q + 1)])
-            out_copy(x, y2, q, 2, y_peer, yin, 8 + 2 * q, ysem).start()
+        add(u2, v, q, 2, [VC(q, 1)])
+        out_copy(u2, v, q, 2, u_peer, UC(q)).start()
+        add(u, v2, q, 3, [UD(q, 1)])
+        out_copy(u, v2, q, 3, v_peer, VD(q)).start()
 
     def column(part, q, sign, dist):
         target = up if sign == 1 else down
         more = zdown if sign == 1 else zup
-        at_target = dist == 1
-        base_out = (20 if (at_target and sign == 1) else 5 * q)
+        level = 4 if (dist == 1 and sign == 1) else q
         kinds = (
-            (0, x, y, 2, [X(8 + 2 * q), Y(8 + 2 * q)]),
-            (1, x, y, 0, [Y(2 * q)]),
-            (2, x, y, 1, [X(2 * q)]),
-            (3, x2, y, 0, [Y(2 * q + 1)]),
-            (4, x, y2, 1, [X(2 * q + 1)]),
+            (0, u, v, 2, [UC(q), VC(q, 0)]),
+            (1, u, v, 3, [VD(q), UD(q, 0)]),
+            (2, u, v, 0, [VA(q, 0)]),
+            (3, u, v, 1, [UB(q, 0)]),
+            (4, u2, v, 0, [VA(q, 1)]),
+            (5, u, v2, 1, [UB(q, 1)]),
         )
-        for k, cx, cy, color, pieces in ((kinds[4], kinds[3], kinds[2], kinds[1]), (kinds[0],))[part]:
+        for k, cu, cv, color, pieces in ((kinds[5], kinds[4], kinds[3], kinds[2]), (kinds[0], kinds[1]))[part]:
             @pl.when(more)
             def _():
-                add(cx, cy, q, color, pieces + [Z(5 * q + k)])
+                add(cu, cv, q, color, pieces + [Z(q, k)])
+
             @pl.when(jnp.logical_not(more))
             def _():
-                add(cx, cy, q, color, pieces)
-            out_copy(cx, cy, q, color, target, zin, base_out + k, zsem).start()
+                add(cu, cv, q, color, pieces)
+
+            out_copy(cu, cv, q, color, target, Z(level, k)).start()
 
     planes = functools.partial(column, 0)
     last = functools.partial(column, 1)
+    def begin_tail():
+        for copy in tail_loads:
+            copy.wait()
+        sums[0] = rows_ref[...]
+
+    tail = tail_steps(
+        x_ref, vec_ref, marks_ref, resid_ref, (key_grad, value_grad, recept_grad), weights,
+        (grad_key_in, grad_value_in, grad_recept_in), ext, unit, inverse, carried, wide, input_ref, sums.at[0],
+    )
+    send_input = pltpu.make_async_copy(input_ref, input_hbm, input_sem)
     run(3, term_a)
+    run(3, term_c)
     run(3, term_b)
-    run(3, term_c)
-    row_step(0)
+    run(3, term_d)
+    begin_tail()
+    tail[0]()
     run_signed(3, planes)
+    tail[1]()
     run(2, term_a)
-    run(2, term_b)
     run(2, term_c)
     run(3, plane_two)
+    run(2, term_b)
+    run(2, term_d)
+    tail[2]()
     run(1, begin_gives)
     run_signed(3, last)
+    tail[3]()
     run(1, term_a)
-    run(1, term_b)
     run(1, term_c)
-    row_step(1)
     run_signed(2, planes)
     begin_gives(z)
+    tail[4]()
     run(2, plane_two)
+    run(1, term_b)
+    run(1, term_d)
+    run_signed(2, last)
     term_a(z)
+    term_c(z)
+    tail[5]()
+    row_copy(0).start()
+    run_signed(1, planes)
+    row_step(0)
+    run(1, plane_two)
     term_b(z)
-    term_c(z)
-    run_signed(2, last)
+    term_d(z)
+    row_step(1)
+    run_signed(1, last)
+    tail[6]()
+    send_input.start()
     row_step(2)
-    run_signed(1, planes)
-    run(1, plane_two)
-    run_signed(1, last)
+    plane_two(z)
     row_step(3)
-    plane_two(z)
+
+    def own(k, cu, cv, color, pieces):
+        @pl.when(zup & zdown)
+        def _():
+            add(cu, cv, z, color, pieces + [Z(z, k), Z(4, k)])
+
+        @pl.when(zup & jnp.logical_not(zdown))
+        def _():
+            add(cu, cv, z, color, pieces + [Z(z, k)])
+
+        @pl.when(zdown & jnp.logical_not(zup))
+        def _():
+            add(cu, cv, z, color, pieces + [Z(4, k)])
+
+    own(4, u2, v, 0, [VA(z, 1)])
+    out_copy(u2, v, z, 0, u_peer, UB(4, 0)).start()
+    own(5, u, v2, 1, [UB(z, 1)])
+    out_copy(u, v2, z, 1, v_peer, VA(4, 0)).start()
+    own(0, u, v, 2, [UC(z), VC(z, 0)])
+    own(1, u, v, 3, [VD(z), UD(z, 0)])
     row_step(4)
     total_ref[...] = sums[10]
-
-    def own(k, cx, cy, color, pieces):
-        @pl.when(zup & zdown)
-        def _():
-            add(cx, cy, z, color, pieces + [Z(5 * z + k), Z(20 + k)])
-        @pl.when(zup & jnp.logical_not(zdown))
-        def _():
-            add(cx, cy, z, color, pieces + [Z(5 * z + k)])
-        @pl.when(zdown & jnp.logical_not(zup))
-        def _():
-            add(cx, cy, z, color, pieces + [Z(20 + k)])
-    own(3, x2, y, 0, [Y(2 * z + 1)])
-    out_copy(x2, y, z, 0, x_peer, xin, 16, xsem).start()
-    own(4, x, y2, 1, [X(2 * z + 1)])
-    out_copy(x, y2, z, 1, y_peer, yin, 16, ysem).start()
-    own(0, x, y, 2, [X(8 + 2 * z), Y(8 + 2 * z)])
-    own(1, x, y, 0, [Y(2 * z), X(16)])
-    own(2, x, y, 1, [X(2 * z), Y(16)])
-    pltpu.sync_copy(acc.at[chip_of(x, y, z)], out_ref)
+    own(2, u, v, 0, [VA(z, 0), UB(4, 0)])
+    own(3, u, v, 1, [UB(z, 0), VA(4, 0)])
+    pltpu.sync_copy(acc.at[chip_of(u, v, z)], out_ref)
+    send_input.wait()
     for chip in range(16):
         give(chip).wait_send()
-        for color in range(3):
-            @pl.when(chip != chip_of(x, y, z))
+        for color in range(4):
+            @pl.when(chip != chip_of(u, v, z))
             def _():
                 lo, n = span[color]
-                pltpu.make_async_remote_copy(src_ref=acc.at[chip, pl.ds(lo, n)], dst_ref=xin.at[0, pl.ds(0, n)],
-                    send_sem=send_sem.at[chip, color], recv_sem=xsem.at[0], device_id=(sibling,), device_id_type=MESH).wait_send()
-
-def scatter_blocks(part, rows, cid=2):
+                pltpu.make_async_remote_copy(src_ref=acc.at[chip, pl.ds(lo, n)], dst_ref=acc.at[chip, pl.ds(lo, n)],
+                    send_sem=send_sem.at[chip, color], recv_sem=usem.at[0], device_id=(sibling,), device_id_type=MESH).wait_send()
+
+def scatter_blocks(part, rows, tail, cid=2):
+    vectors, marks, x_rows, resid_grad, *grads, weights = tail
     _, slots, height, feats = part.shape
-    most = max(n for _, n in spans(slots))
-    chunk = (most, height, feats)
+    own = x_rows.shape[0] - ROW_TILE
+    size_a, size_b, size_c, size_d = (n for _, n in scatter_spans(slots))
     dt = part.dtype
+    block = lambda *shape: pltpu.VMEM(shape + (height, feats), dt)
+    like = lambda array: pltpu.VMEM(array.shape, array.dtype)
+    anywhere = pl.BlockSpec(memory_space=pl.ANY)
+    vmem = pl.BlockSpec(memory_space=pltpu.VMEM)
+    wide_shapes, tail_scratch = tail_shapes(x_rows.shape)
     return pl.pallas_call(
         functools.partial(scatter_kernel, slots),
         out_shape=(
             jax.ShapeDtypeStruct(part.shape[1:], dt),
             jax.ShapeDtypeStruct(rows.shape, rows.dtype),
+            jax.ShapeDtypeStruct((own, feats), jnp.float32),
         ),
-        in_specs=[pl.BlockSpec(memory_space=pl.ANY), pl.BlockSpec(memory_space=pltpu.VMEM)],
-        out_specs=(pl.BlockSpec(memory_space=pl.ANY), pl.BlockSpec(memory_space=pltpu.VMEM)),
+        in_specs=[anywhere] + [vmem] * 3 + [anywhere] * 6,
+        out_specs=(anywhere, vmem, anywhere),
         scratch_shapes=[
-            pltpu.VMEM((16, slots, height, feats), dt),
-            pltpu.VMEM((16, slots, height, feats), dt),
-            pltpu.VMEM((17,) + chunk, dt),
-            pltpu.VMEM((17,) + chunk, dt),
-            pltpu.VMEM((25,) + chunk, dt),
+            block(16, slots),
+            block(4, slots),
+            block(9, size_b),
+            block(4, size_c),
+            block(8, size_d),
+            block(9, size_a),
+            block(8, size_c),
+            block(4, size_d),
+            block(20, size_a),
+            block(5, size_c),
+            block(5, size_d),
             pltpu.VMEM((11,) + rows.shape, rows.dtype),
+            like(x_rows), like(resid_grad), *(like(g) for g in grads), like(weights),
+            *wide_shapes,
+            *tail_scratch,
+            pltpu.VMEM((own, feats), jnp.float32),
+            pltpu.SemaphoreType.DMA((4,)),
             pltpu.SemaphoreType.DMA((16,)),
             pltpu.SemaphoreType.DMA((16,)),
-            pltpu.SemaphoreType.DMA((16,)),
-            pltpu.SemaphoreType.DMA((16, 3)),
-            pltpu.SemaphoreType.DMA((17,)),
-            pltpu.SemaphoreType.DMA((17,)),
-            pltpu.SemaphoreType.DMA((25,)),
+            pltpu.SemaphoreType.DMA((16, 4)),
+            pltpu.SemaphoreType.DMA((21,)),
+            pltpu.SemaphoreType.DMA((21,)),
+            pltpu.SemaphoreType.DMA((30,)),
             pltpu.SemaphoreType.DMA((5,)),
             pltpu.SemaphoreType.DMA((5,)),
+            pltpu.SemaphoreType.DMA((6,)),
+            pltpu.SemaphoreType.DMA,
         ],
-        compiler_params=pltpu.CompilerParams(collective_id=cid, has_side_effects=True, vmem_limit_bytes=58 * 2**20),
+        compiler_params=pltpu.CompilerParams(collective_id=cid, has_side_effects=True, vmem_limit_bytes=VMEM_BYTES),
         name="scatter_blocks",
-    )(part, rows)
+    )(part, rows, vectors, marks, x_rows, resid_grad, *grads, weights)
 
 
 ROW_TILE = 16
 BIG_TILE = 64
+PIECES = 4
+STEP_TILE = 32
 CHUNKS = 8
 LANES = 128
+PLANE = 8
+PLANES = GRID_DEVICES // PLANE
 VMEM_BYTES = 60 * 2**20
 
 
@@ -705,6 +779,25 @@
     pltpu.make_async_copy(
         store_ref.at[pl.ds(place, count)], grad_ref.at[pl.ds(0, count)], sem
     ).wait()
+
+
+def start_pieces(pairs, sems, own):
+    for p in range(PIECES + 1):
+        for k, (src, dst) in enumerate(pairs):
+            if p < PIECES or dst.shape[0] > own:
+                piece_copy(src, dst, sems, own, k, p).start()
+
+
+def piece_copy(src, dst, sems, own, k, p):
+    size = own // PIECES
+    at = pl.ds(p * size, size) if p < PIECES else pl.ds(own, ROW_TILE)
+    return pltpu.make_async_copy(src.at[at], dst.at[at], sems.at[k, p])
+
+
+def wait_piece(pairs, sems, own, p):
+    for k, (src, dst) in enumerate(pairs):
+        if p < PIECES or dst.shape[0] > own:
+            piece_copy(src, dst, sems, own, k, p).wait()
 
 
 def for_rows(rows, work, sums=()):
@@ -806,7 +899,7 @@
     return jnp.where(hit, 0.0, 1.0)
 
 
-def write_marks(doc_ref, marks_ref, chunk_ref, link_ref, flag_ref, own, devices):
+def write_marks(doc_ref, marks_ref, chunk_ref, link_ref, own, devices):
     rows = marks_ref.shape[0]
     length = own // CHUNKS
     total = own * devices
@@ -835,20 +928,35 @@
     chunk_ref[:, 3:4] = (1 + chunk * length).astype(jnp.float32)
     chunk_ref[:, 4:5] = jnp.where(first + own < total, none_between(offsets, end + 1, first + own), 0.0)
     chunk_ref[:, 5:6] = (1 + (CHUNKS - 1 - chunk) * length).astype(jnp.float32)
-    count = link_ref.shape[0]
-    group = devices // count
-    span = own * group
-    here = me // group
-    other = lax.broadcasted_iota(jnp.int32, (count, 1), 0)
-    link_ref[:, 0:1] = jnp.where(other < here, none_between(offsets, span * (other + 1) - 1, span * here - 2), 0.0)
-    link_ref[:, 1:2] = (span * (here - 1 - other)).astype(jnp.float32)
-    link_ref[:, 2:3] = jnp.where(other > here, none_between(offsets, span * (here + 1) + 1, span * other), 0.0)
-    link_ref[:, 3:4] = (span * (other - here - 1)).astype(jnp.float32)
-    pair = span * here + jnp.zeros((1, 1), jnp.int32)
-    flag_ref[:, 0:1] = none_between(offsets, pair + own - 1, pair + 2 * own - 2)
-    flag_ref[:, 1:2] = none_between(offsets, pair - 1, pair + own - 2)
-    flag_ref[:, 2:3] = none_between(offsets, pair + 1, pair + own)
-    flag_ref[:, 3:4] = none_between(offsets, pair + own + 1, pair + 2 * own)
+    def put(rows, col, valid, distance):
+        link_ref[rows, col : col + 1] = valid
+        link_ref[rows, col + 1 : col + 2] = distance.astype(jnp.float32)
+
+    if devices != GRID_DEVICES:
+        other = lax.broadcasted_iota(jnp.int32, (devices, 1), 0)
+        every = slice(0, devices)
+        put(every, 0, jnp.where(other < me, none_between(offsets, own * (other + 1) - 1, own * me - 2), 0.0), own * (me - 1 - other))
+        put(every, 2, jnp.where(other > me, none_between(offsets, own * (me + 1) + 1, own * other), 0.0), own * (other - me - 1))
+        return
+    z = me // PLANE
+    base = z * PLANE
+    end = base + PLANE
+    other = base + lax.broadcasted_iota(jnp.int32, (PLANE, 1), 0)
+    rows = slice(0, PLANE)
+    put(rows, 0, jnp.where(other < me, none_between(offsets, own * (other + 1) - 1, own * me - 2), 0.0), own * (me - 1 - other))
+    put(rows, 2, jnp.where(other > me, none_between(offsets, own * (me + 1) + 1, own * other), 0.0), own * (other - me - 1))
+    rows = slice(PLANE, 2 * PLANE)
+    put(rows, 0, none_between(offsets, own * (other + 1) - 1, own * end - 2), own * (end - 1 - other))
+    put(rows, 2, none_between(offsets, own * base + 1, own * other), own * (other - base))
+    rows = slice(2 * PLANE, 2 * PLANE + PLANES)
+    far = lax.broadcasted_iota(jnp.int32, (PLANES, 1), 0)
+    span = own * PLANE
+    put(rows, 0, jnp.where(far < z, none_between(offsets, span * (far + 1) - 1, span * z - 2), 0.0), span * (z - 1 - far))
+    put(rows, 2, jnp.where(far > z, none_between(offsets, span * (z + 1) + 1, span * far), 0.0), span * (far - z - 1))
+    rows = slice(2 * PLANE + PLANES, 2 * PLANE + PLANES + 1)
+    here = me + jnp.zeros((1, 1), jnp.int32)
+    put(rows, 0, none_between(offsets, own * base - 1, own * here - 2), own * (here - base))
+    put(rows, 2, none_between(offsets, own * (here + 1) + 1, own * end), own * (end - 1 - here))
 
 
 def mask_column(pad_ref, column):
@@ -913,10 +1021,10 @@
 
 def prepared_shapes(devices, own, features):
     rows = own + ROW_TILE
-    count = devices // 2 if devices == GRID_DEVICES else devices
+    count = 2 * PLANE + PLANES + 1 if devices == GRID_DEVICES else devices
     low = jax.ShapeDtypeStruct((rows, features), jnp.bfloat16)
     small = lambda *shape: jax.ShapeDtypeStruct(shape, jnp.float32)
-    shapes = (low, low, small(rows, 4), small(CHUNKS, 6), small(count, 4), small(1, 4), low, low, low)
+    shapes = (low, low, small(rows, 4), small(CHUNKS, 6), small(count, 4), low, low, low)
     scratch = [
         pltpu.VMEM((own, 1), jnp.float32),
         pltpu.VMEM((rows + 8, features), jnp.float32),
@@ -928,11 +1036,11 @@
 
 def prepare_kernel(
     devices, doc_ref, tokens_ref, grads_ref, pad_ref, after_ref, after_grad_ref, before_ref, vec_ref,
-    x_ref, grad_ref, marks_ref, chunk_ref, link_ref, flag_ref, in_key, in_value, in_recept,
+    x_ref, grad_ref, marks_ref, chunk_ref, link_ref, in_key, in_value, in_recept,
     column, ext, wide, wide_grad,
 ):
     mask_column(pad_ref, column)
-    marks = (marks_ref, chunk_ref, link_ref, flag_ref)
+    marks = (marks_ref, chunk_ref, link_ref)
     prepare_own(devices, doc_ref, tokens_ref, grads_ref, column, vec_ref, x_ref, grad_ref, marks, ext, wide, wide_grad)
     lows = (in_key, in_value, in_recept)
     prepare_halo(devices, after_ref, after_grad_ref, before_ref, vec_ref, x_ref, grad_ref, marks_ref, lows, ext)
@@ -954,8 +1062,8 @@
 
 def open_kernel(
     slot_ref, vec_ref, marks_ref, chunk_ref, in_key, in_value, in_recept, pool_ref,
-    key_ref, value_ref, recept_ref, num_ref, den_ref, max_ref, prefix_ref, summary_ref,
-    store, sem,
+    prefix_ref, summary_ref, key_out, value_out, recept_out, state_out, weights_ref,
+    key_ref, value_ref, recept_ref, num_ref, den_ref, max_ref, store, sem, out_sem,
 ):
     rows, features = in_key.shape
     own = rows - ROW_TILE
@@ -970,6 +1078,17 @@
             out[:, cols] = piece
 
         times_weight(left, store, m * per, per, write)
+    sent = [
+        pltpu.make_async_copy(src, dst, out_sem.at[k])
+        for k, (src, dst) in enumerate(
+            (
+                (key_ref, key_out), (value_ref, value_out), (recept_ref, recept_out), (store, weights_ref),
+                (num_ref, state_out.at[0]), (den_ref, state_out.at[1]), (max_ref, state_out.at[2]),
+            )
+        )
+    ]
+    for copy in sent[:4]:
+        copy.start()
     rate = jnp.exp(vec_ref[5:6])
 
     def token(i, state, key, value):
@@ -984,6 +1103,8 @@
     state = lax.fori_loop(0, length - 1, step, (blank, blank, blank + NEGATIVE))
     late = tuple(item[CHUNKS - 1 :] for item in state)
     ends = step(length - 1, state)
+    for copy in sent[4:]:
+        copy.start()
     prior = (value_ref[own + 2 : own + 3], jnp.ones((1, features), jnp.float32), key_ref[own + 2 : own + 3])
     for c in range(CHUNKS):
         for k in range(3):
@@ -993,23 +1114,31 @@
             prior = merge(tuple(item[c : c + 1] for item in ends), old)
     last = merge(late, aged(prior, float(length - 1), chunk_ref[CHUNKS - 1 :, 2:3], rate))
     summary_ref[...] = jnp.concatenate(last, axis=0)
+    for copy in sent:
+        copy.wait()
 
 
 def open_pass(slots, vectors, marks, chunk_marks, lows, pool):
     rows, features = lows[0].shape
     own = rows - ROW_TILE
     full = jax.ShapeDtypeStruct((rows, features), jnp.float32)
-    part = jax.ShapeDtypeStruct((own, features), jnp.float32)
     small = lambda *shape: jax.ShapeDtypeStruct(shape, jnp.float32)
     vmem = pl.BlockSpec(memory_space=pltpu.VMEM)
+    anywhere = pl.BlockSpec(memory_space=pl.ANY)
+    f32 = lambda *shape: pltpu.VMEM(shape, jnp.float32)
+    blocks = (3 * EMBED_SIZE // BLOCK_ROWS, BLOCK_ROWS, features)
     return pl.pallas_call(
         open_kernel,
-        out_shape=(full, full, full, part, part, part, small(3, CHUNKS, features), small(3, features)),
-        in_specs=[pl.BlockSpec(memory_space=pltpu.SMEM)] + [vmem] * 6 + [pl.BlockSpec(memory_space=pl.ANY)],
-        out_specs=(vmem,) * 8,
-        scratch_shapes=[
-            pltpu.VMEM((3 * EMBED_SIZE // BLOCK_ROWS, BLOCK_ROWS, features), jnp.bfloat16),
+        out_shape=(
+            small(3, CHUNKS, features), small(3, features), full, full, full, small(3, own, features),
+            jax.ShapeDtypeStruct(blocks, jnp.bfloat16),
+        ),
+        in_specs=[pl.BlockSpec(memory_space=pltpu.SMEM)] + [vmem] * 6 + [anywhere],
+        out_specs=(vmem,) * 2 + (anywhere,) * 5,
+        scratch_shapes=[f32(rows, features)] * 3 + [f32(own, features)] * 3 + [
+            pltpu.VMEM(blocks, jnp.bfloat16),
             pltpu.SemaphoreType.DMA((3,)),
+            pltpu.SemaphoreType.DMA((7,)),
         ],
         compiler_params=pltpu.CompilerParams(vmem_limit_bytes=VMEM_BYTES),
         name="open_pass",
@@ -1017,12 +1146,13 @@
 
 
 def middle_kernel(
-    slot_ref, x_ref, grad_ref, vec_ref, marks_ref, chunk_ref, incoming_ref, prefix_ref,
-    key_ref, value_ref, recept_ref, num_ref, den_ref, max_ref, pool_ref,
-    layer_ref, resid_grad, wkv, gw, own_share, recept_grad, suffix_ref, summary_ref, sums_ref,
-    full_out, back_out, slot_grad,
+    slot_ref, vec_ref, marks_ref, chunk_ref, incoming_ref, prefix_ref,
+    x_in, grad_in, key_in, value_in, recept_in, state_in, pool_ref,
+    suffix_ref, summary_ref, sums_ref, fade_ref,
+    layer_out, resid_out, key_out, value_out, recept_out, slot_grad,
+    x_ref, grad_ref, key_ref, value_ref, recept_ref, layer_ref, resid_grad, wkv, gw, own_share, recept_grad,
     full_num, full_den, full_max, mixed, ext, unit, inverse, low_key, low_recept, hidden, squared, value_acc, gate, gcv, gcg, hidden_grad,
-    attn_grad, top_log, wide, store, sem, out_sem, state_sem,
+    attn_grad, top_log, wide, store, sem, out_sem, in_sem, piece_sem, done_sem,
 ):
     rows, features = x_ref.shape
     own = rows - ROW_TILE
@@ -1031,7 +1161,23 @@
     per = EMBED_SIZE // BLOCK_ROWS
     ff = FF // BLOCK_ROWS
     at_out, at_recept, at_key, at_value = 0, per, 2 * per, 2 * per + ff
+    pairs = [(key_in, key_ref), (value_in, value_ref), (recept_in, recept_ref)]
+    pairs += [(state_in.at[k], ref) for k, ref in enumerate((full_num, full_den, full_max))]
+    start_pieces(pairs, piece_sem, own)
+    arrive_x = pltpu.make_async_copy(x_in, x_ref, in_sem.at[0])
+    arrive_grad = pltpu.make_async_copy(grad_in, grad_ref, in_sem.at[1])
+    sent = [
+        pltpu.make_async_copy(src, dst, done_sem.at[k])
+        for k, (src, dst) in enumerate(
+            (
+                (layer_ref, layer_out), (resid_grad, resid_out), (recept_grad, recept_out),
+                (gw, key_out), (own_share, value_out),
+            )
+        )
+    ]
     fetch_blocks(slot_ref, pool_ref, store, sem.at[0], 3 * per, at_out, per)
+    arrive_x.start()
+    arrive_grad.start()
     fetch_blocks(slot_ref, pool_ref, store, sem.at[1], 5 * per, at_key, ff)
     fetch_blocks(slot_ref, pool_ref, store, sem.at[2], 5 * per + ff, at_value, ff)
     fetch_blocks(slot_ref, pool_ref, store, sem.at[3], 4 * per, at_recept, per)
@@ -1055,25 +1201,27 @@
         value_acc[rows_at(j, size)] = scale
         ext[rows_at(j, size)] = jax.nn.sigmoid(recept) * out
 
+    carry_wide = tuple(jnp.concatenate([item] * (STEP_TILE // CHUNKS), axis=0) for item in carry)
+    ramp = lax.broadcasted_iota(jnp.int32, (STEP_TILE, 1), 0) // CHUNKS
+
     def attend_step(i, state_carry):
-        at = rows_at(i, CHUNKS)
+        at = rows_at(i, STEP_TILE)
         alive = marks_ref[at, 2:3]
-        distance = jnp.float32(i) if isinstance(i, int) else i.astype(jnp.float32)
-        state = merge((num_ref[at], den_ref[at], max_ref[at]), aged(carry, distance, alive, rate))
+        distance = (i * (STEP_TILE // CHUNKS) + ramp).astype(jnp.float32)
+        state = merge((full_num[at], full_den[at], full_max[at]), aged(carry_wide, distance, alive, rate))
         full_num[at], full_den[at], full_max[at] = state
-        attend(i, CHUNKS, state, key_ref[at], value_ref[at], recept_ref[at])
+        attend(i, STEP_TILE, state, key_ref[at], value_ref[at], recept_ref[at])
         return state_carry
 
-    lax.fori_loop(0, length, attend_step, 0)
+    for p in range(PIECES):
+        wait_piece(pairs, piece_sem, own, p)
+        count = own // STEP_TILE
+        lax.fori_loop(p * count // PIECES, (p + 1) * count // PIECES, attend_step, 0)
+    wait_piece(pairs, piece_sem, own, PIECES)
 
     def row(ref, r):
         return ref[r : r + 1]
 
-    def state_copy(k, target):
-        return pltpu.make_async_copy((full_num, full_den, full_max)[k], target.at[k], state_sem.at[k])
-
-    for k in range(3):
-        state_copy(k, full_out).start()
     end = advance(
         (row(full_num, own - 1), row(full_den, own - 1), row(full_max, own - 1)),
         row(key_ref, own - 1), row(value_ref, own - 1), rate,
@@ -1098,6 +1246,7 @@
     for_rows(rows, pack)
     pack(own, ROW_TILE)
     await_blocks(pool_ref, store, sem.at[0], at_out, per)
+    arrive_x.wait()
 
     def write_resid(cols, piece):
         unit[:, cols] = x_ref[:, cols].astype(jnp.float32) + piece
@@ -1146,6 +1295,8 @@
 
     times_weight(low_recept, store, at_recept, per, write_gate)
 
+    arrive_grad.wait()
+
     def finish(first, size):
         at = pl.ds(first, size)
         opened = jax.nn.sigmoid(gate[at])
@@ -1167,6 +1318,7 @@
         layer_ref[pl.ds(first, size)] = take_rows(wide, pl.ds(first, size)).astype(jnp.bfloat16)
 
     for_rows(rows, emit)
+    sent[0].start()
 
     def write_hidden_grad(cols, piece):
         hidden_grad[:, cols] = (piece * (2.0 * hidden[:, cols])).astype(jnp.bfloat16)
@@ -1222,6 +1374,7 @@
     for k in range(4):
         sums_ref[k : k + 1] = jnp.sum(sums[k], axis=0, keepdims=True)
     norm_back(own, ROW_TILE, halo_next)
+    sent[1].start()
 
     times_weight_back(attn_grad, store, at_out, per, write_gate)
     weight_gradient(mixed, attn_grad, own, slot_ref, slot_grad, store, out_sem.at[0], 3 * per, at_out)
@@ -1236,6 +1389,7 @@
 
     for_rows(rows, gate_back)
     gate_back(own, ROW_TILE)
+    sent[2].start()
 
     def back_token(state, share, out, top, start):
         older = state[2] - rate
@@ -1243,19 +1397,37 @@
         old, new = jnp.exp(older - high), jnp.exp(-top - high)
         return reset((old * state[0] + new * share, old * state[1] - new * share * out, high), start)
 
-    for k in range(3):
-        state_copy(k, full_out).wait()
-    back_num, back_den, back_max = full_num, full_den, full_max
-
-    def back_scan(n, state):
+    def back_scan(n, items):
+        state, joint, sums = items[:3], items[3:6], items[6:]
         i = length - 1 - n
         at = rows_at(i, CHUNKS)
-        back_num[at], back_den[at], back_max[at] = state
-        return back_token(state, ext[at], wkv[at], top_log[at], marks_ref[at, 0:1])
-
-    heads = lax.fori_loop(0, length, back_scan, (blank, blank, blank + NEGATIVE))
+        value, out = value_ref[at], wkv[at]
+        direct = own_share[at] * gw[at]
+        bonus_grad = direct * (value - out)
+        lift = jnp.exp(key_ref[at] + state[2])
+        gw[at] = bonus_grad + lift * (state[0] * value + state[1])
+        own_share[at] = direct + lift * state[0]
+        whole = (full_num[at], full_den[at], full_max[at])
+        fade = jnp.exp(state[2] + whole[2] - rate) * (state[0] * whole[0] + state[1] * whole[1])
+        joint = merge(joint, aged(whole, (length - i).astype(jnp.float32), marks_ref[at, 3:4], rate))
+        state = back_token(state, ext[at], out, top_log[at], marks_ref[at, 0:1])
+        return state + joint + (sums[0] + fade, sums[1] + bonus_grad)
+
+    empty = (blank, blank, blank + NEGATIVE)
+    items = lax.fori_loop(0, length - 1, back_scan, empty + empty + (blank, blank))
+    first = tuple(item[0:1] for item in items[:3])
+    items = back_scan(jnp.int32(length - 1), items)
+    heads = items[:3]
     for k in range(3):
-        state_copy(k, back_out).start()
+        fade_ref[k] = items[3 + k]
+    for k in range(2):
+        sums_ref[4 + k : 5 + k] = jnp.sum(items[6 + k], axis=0, keepdims=True)
+    tile = slice(own, rows)
+    direct = own_share[tile] * gw[tile]
+    gw[tile] = direct * (value_ref[tile] - wkv[tile])
+    own_share[tile] = direct
+    sent[3].start()
+    sent[4].start()
     nothing = jnp.zeros((1, features), jnp.float32)
     after = back_token(
         (nothing, nothing, nothing + NEGATIVE),
@@ -1267,21 +1439,19 @@
         if c > 0:
             old = aged(after, float(length), chunk_ref[c : c + 1, 0:1], rate)
             after = merge(tuple(item[c : c + 1] for item in heads), old)
-    first = (row(back_num, 0), row(back_den, 0), row(back_max, 0))
     last = merge(first, aged(after, float(length - 1), marks_ref[0:1, 3:4], rate))
     summary_ref[...] = jnp.concatenate(last, axis=0)
     for k, (place, count) in enumerate(((at_out, per), (at_key, ff), (at_value, ff), (at_recept, per))):
         await_gradient(store, slot_grad, out_sem.at[k], place, count)
-    for k in range(3):
-        state_copy(k, back_out).wait()
+    for copy in sent:
+        copy.wait()
 
 
 def middle_pass(slots, x_rows, grad_rows, vectors, marks, chunk_marks, incoming, opened, pool):
-    key, value, recept, num, den, top, prefix = opened
+    key, value, recept, states, prefix = opened
     rows, features = x_rows.shape
     own = rows - ROW_TILE
     full = jax.ShapeDtypeStruct((rows, features), jnp.float32)
-    part = jax.ShapeDtypeStruct((own, features), jnp.float32)
     low = jax.ShapeDtypeStruct((rows, features), jnp.bfloat16)
     vmem = pl.BlockSpec(memory_space=pltpu.VMEM)
     anywhere = pl.BlockSpec(memory_space=pl.ANY)
@@ -1290,18 +1460,28 @@
     return pl.pallas_call(
         middle_kernel,
         out_shape=(
-            jax.ShapeDtypeStruct((own, features), jnp.bfloat16),
-            full, full, full, full, low,
             jax.ShapeDtypeStruct((3, CHUNKS, features), jnp.float32),
             jax.ShapeDtypeStruct((3, features), jnp.float32),
-            jax.ShapeDtypeStruct((4, features), jnp.float32),
-            jax.ShapeDtypeStruct((3, own, features), jnp.float32),
-            jax.ShapeDtypeStruct((3, own, features), jnp.float32),
+            jax.ShapeDtypeStruct((6, features), jnp.float32),
+            jax.ShapeDtypeStruct((3, CHUNKS, features), jnp.float32),
+            jax.ShapeDtypeStruct((own, features), jnp.bfloat16),
+            full, full, full, low,
             jax.ShapeDtypeStruct(pool.shape, jnp.bfloat16),
         ),
-        in_specs=[pl.BlockSpec(memory_space=pltpu.SMEM)] + [vmem] * 13 + [anywhere],
-        out_specs=(vmem,) * 9 + (anywhere,) * 3,
+        in_specs=[pl.BlockSpec(memory_space=pltpu.SMEM)] + [vmem] * 5 + [anywhere] * 7,
+        out_specs=(vmem,) * 4 + (anywhere,) * 6,
         scratch_shapes=[
+            b16(rows, features),
+            b16(rows, features),
+            f32(rows, features),
+            f32(rows, features),
+            f32(rows, features),
+            b16(own, features),
+            f32(rows, features),
+            f32(rows, features),
+            f32(rows, features),
+            f32(rows, features),
+            b16(rows, features),
             f32(own, features),
             f32(own, features),
             f32(own, features),
@@ -1324,85 +1504,41 @@
             b16((2 * EMBED_SIZE + 2 * FF) // BLOCK_ROWS, BLOCK_ROWS, features),
             pltpu.SemaphoreType.DMA((4,)),
             pltpu.SemaphoreType.DMA((4,)),
-            pltpu.SemaphoreType.DMA((3,)),
+            pltpu.SemaphoreType.DMA((2,)),
+            pltpu.SemaphoreType.DMA((6, PIECES + 1)),
+            pltpu.SemaphoreType.DMA((5,)),
         ],
         compiler_params=pltpu.CompilerParams(vmem_limit_bytes=VMEM_BYTES),
         name="middle_pass",
-    )(slots, x_rows, grad_rows, vectors, marks, chunk_marks, incoming, prefix, key, value, recept, num, den, top, pool)
-
-
-def close_kernel(
-    slot_ref, x_ref, vec_ref, marks_ref, chunk_ref, incoming_ref, suffix_ref, key_ref, value_ref,
-    in_key, in_value, in_recept, resid_grad, wkv, gw, own_share, recept_grad, sums_two_ref, full_ref, back_ref,
-    pool_ref, grads_in,
-    input_ref, sums_ref, slot_grad,
-    ext, unit, inverse, key_wide, value_wide, key_grad, value_grad, grad_key_in, grad_value_in, grad_recept_in,
-    carried, wide, store, sem, out_sem,
-):
+    )(slots, vectors, marks, chunk_marks, incoming, prefix, x_rows, grad_rows, key, value, recept, states, pool)
+
+
+def tail_shapes(shape):
+    rows, features = shape
+    own = rows - ROW_TILE
+    f32 = lambda *dims: pltpu.VMEM(dims, jnp.float32)
+    grads = [f32(rows, features)] * 3
+    rest = [
+        f32(rows + 8, features),
+        f32(rows, features),
+        f32(rows, 1),
+        f32(rows, features),
+        f32(features // LANES, own, LANES),
+    ]
+    return grads, rest
+
+
+def tail_steps(x_ref, vec_ref, marks_ref, resid_ref, lows, weights, outs, ext, unit, inverse, carried, wide, input_ref, sums_ref):
     rows, features = x_ref.shape
     own = rows - ROW_TILE
-    tiles = rows // ROW_TILE
     length = own // CHUNKS
     per = EMBED_SIZE // BLOCK_ROWS
-    for m in range(3):
-        fetch_blocks(slot_ref, pool_ref, store, sem.at[m], m * per, m * per, per)
-    rate = jnp.exp(vec_ref[5:6])
-    incoming = tuple(incoming_ref[k : k + 1] for k in range(3))
-    carry = merge(
-        tuple(suffix_ref[k] for k in range(3)),
-        aged(tuple(jnp.broadcast_to(v, (CHUNKS, features)) for v in incoming), chunk_ref[:, 5:6], chunk_ref[:, 4:5], rate),
-    )
-
-    def spread_back(state, key, value, share, grad, out):
-        direct = share * grad
-        bonus_grad = direct * (value - out)
-        lift = jnp.exp(key + state[2])
-        return bonus_grad + lift * (state[0] * value + state[1]), direct + lift * state[0], bonus_grad
-
-    def token(i, sums):
-        at = rows_at(i, CHUNKS)
-        distance = (length - 1 - i).astype(jnp.float32)
-        state = merge(tuple(back_ref[k, at] for k in range(3)), aged(carry, distance, marks_ref[at, 3:4], rate))
-        key_g, value_g, bonus_grad = spread_back(state, key_ref[at], value_ref[at], own_share[at], gw[at], wkv[at])
-        key_wide[at] = key_g
-        value_wide[at] = value_g
-        fade = jnp.exp(state[2] + full_ref[2, at] - rate) * (state[0] * full_ref[0, at] + state[1] * full_ref[1, at])
-        return sums[0] + fade, sums[1] + bonus_grad
-
-    blank = jnp.zeros((CHUNKS, features), jnp.float32)
-    fade, bonus_sum = lax.fori_loop(0, length, token, (blank, blank))
-    sums_ref[5:6] = -rate * jnp.sum(fade, axis=0, keepdims=True)
-    sums_ref[6:7] = jnp.sum(bonus_sum, axis=0, keepdims=True)
-    halo = tuple(
-        jnp.concatenate([incoming[k], jnp.zeros((ROW_TILE - 1, features), jnp.float32) + (NEGATIVE if k == 2 else 0.0)], axis=0)
-        for k in range(3)
-    )
-    key_g, value_g, _ = spread_back(
-        halo, key_ref[own:rows], value_ref[own:rows], own_share[own:rows], gw[own:rows], wkv[own:rows]
-    )
-    key_wide[own:rows] = key_g
-    value_wide[own:rows] = value_g
-
-    def pack(first, size):
-        at = pl.ds(first, size)
-        key_grad[at] = key_wide[at].astype(jnp.bfloat16)
-        value_grad[at] = value_wide[at].astype(jnp.bfloat16)
-
-    for_rows(rows, pack)
-    pack(own, ROW_TILE)
-    products = (
-        (key_grad, grad_key_in, in_key),
-        (value_grad, grad_value_in, in_value),
-        (recept_grad, grad_recept_in, in_recept),
-    )
-    for m, (left, out, inputs) in enumerate(products):
-        await_blocks(pool_ref, store, sem.at[m], m * per, per)
-
-        def write(cols, piece, out=out):
-            out[:, cols] = piece
-
-        times_weight_back(left, store, m * per, per, write)
-        weight_gradient(inputs, left, own, slot_ref, slot_grad, store, out_sem.at[m], m * per, m * per)
+
+    def back(m):
+        def write(cols, piece):
+            outs[m][:, cols] = piece
+
+        times_weight_back(lows[m], weights, m * per, per, write)
 
     def norm(first, size):
         at = pl.ds(first, size)
@@ -1411,23 +1547,26 @@
         inverse[at] = inv
         ext[pl.ds(pl.multiple_of(first + 8, 8), size)] = out * vec_ref[0:1] + vec_ref[1:2]
 
-    for_rows(rows, norm)
-    norm(own, ROW_TILE)
-    shift_in(ext, own)
+    def norms():
+        for_rows(rows, norm)
+        norm(own, ROW_TILE)
+        shift_in(ext, own)
+
     mixes = tuple(vec_ref[k : k + 1] for k in (2, 3, 4))
 
     def carry_over(first, size):
         at = pl.ds(first, size)
-        total = (1.0 - mixes[0]) * grad_key_in[at] + (1.0 - mixes[1]) * grad_value_in[at] + (1.0 - mixes[2]) * grad_recept_in[at]
+        total = (1.0 - mixes[0]) * outs[0][at] + (1.0 - mixes[1]) * outs[1][at] + (1.0 - mixes[2]) * outs[2][at]
         carried[at] = marks_ref[at, 1:2] * total
 
-    for_rows(rows, carry_over)
-    carry_over(own, ROW_TILE)
-    carried[own : own + 8] = jnp.concatenate([carried[1:8], carried[own : own + 1]], axis=0)
+    def carry_all():
+        for_rows(rows, carry_over)
+        carry_over(own, ROW_TILE)
+        carried[own : own + 8] = jnp.concatenate([carried[1:8], carried[own : own + 1]], axis=0)
 
     def back_step(first, size, *sums):
         at = pl.ds(first, size)
-        grads = (grad_key_in[at], grad_value_in[at], grad_recept_in[at])
+        grads = (outs[0][at], outs[1][at], outs[2][at])
         grad = carried[pl.ds(pl.multiple_of(first + 8, 8), size)]
         for weight, piece in zip(mixes, grads):
             grad = grad + weight * piece
@@ -1437,7 +1576,7 @@
             - jnp.mean(scaled, axis=1, keepdims=True)
             - unit[at] * jnp.mean(scaled * unit[at], axis=1, keepdims=True)
         )
-        out = resid_grad[at] + inner * inverse[at]
+        out = resid_ref[at] + inner * inverse[at]
         for k in range(size // CHUNKS):
             put_step(wide, first // CHUNKS + k, length, out[CHUNKS * k : CHUNKS * (k + 1)])
         here, before = normed_pair(ext, marks_ref, first, size)
@@ -1446,120 +1585,222 @@
             s + fold(piece * spread) for s, piece in zip(sums[2:], grads)
         )
 
-    sums = for_rows(rows, back_step, (blank,) * 5)
-    for k in range(5):
-        sums_ref[k : k + 1] = jnp.sum(sums[k], axis=0, keepdims=True)
-    sums_ref[7:] = sums_two_ref[...]
+    def back_all():
+        blank = jnp.zeros((CHUNKS, features), jnp.float32)
+        sums = for_rows(rows, back_step, (blank,) * 5)
+        for k in range(5):
+            sums_ref[k : k + 1] = jnp.sum(sums[k], axis=0, keepdims=True)
 
     def emit(first, size):
         input_ref[pl.ds(first, size)] = take_rows(wide, pl.ds(first, size))
 
-    for_rows(rows, emit)
+    return [
+        functools.partial(back, 0), functools.partial(back, 1), functools.partial(back, 2),
+        norms, carry_all, back_all, lambda: for_rows(rows, emit),
+    ]
+
+
+def tail_kernel(
+    vec_ref, marks_ref, x_ref, resid_ref, key_grad, value_grad, recept_grad, weights, rows_ref,
+    input_ref, sums_ref, grad_key_in, grad_value_in, grad_recept_in, ext, unit, inverse, carried, wide,
+):
+    sums_ref[...] = rows_ref[...]
+    steps = tail_steps(
+        x_ref, vec_ref, marks_ref, resid_ref, (key_grad, value_grad, recept_grad), weights,
+        (grad_key_in, grad_value_in, grad_recept_in), ext, unit, inverse, carried, wide, input_ref, sums_ref,
+    )
+    for step in steps:
+        step()
+
+
+def tail_pass(rows, tail):
+    x_rows = tail[2]
+    own, features = x_rows.shape[0] - ROW_TILE, x_rows.shape[1]
+    grads, rest = tail_shapes(x_rows.shape)
+    vmem = pl.BlockSpec(memory_space=pltpu.VMEM)
+    return pl.pallas_call(
+        tail_kernel,
+        out_shape=(jax.ShapeDtypeStruct((own, features), jnp.float32), jax.ShapeDtypeStruct(rows.shape, rows.dtype)),
+        in_specs=[vmem] * 9,
+        out_specs=(vmem, vmem),
+        scratch_shapes=grads + rest,
+        compiler_params=pltpu.CompilerParams(vmem_limit_bytes=VMEM_BYTES),
+        name="tail_pass",
+    )(*tail, rows)
+
+
+def close_kernel(
+    slot_ref, vec_ref, marks_ref, chunk_ref, incoming_ref, suffix_ref, sums_two_ref, fade_ref,
+    key_hbm, value_hbm, in_key_hbm, in_value_hbm, in_recept_hbm, key_part_hbm, value_part_hbm, recept_hbm, grads_in,
+    key_grad, value_grad, sums_ref, slot_grad,
+    key_ref, value_ref, in_key, in_value, in_recept, key_wide, value_wide, recept_grad,
+    store, out_sem, in_sem, piece_sem,
+):
+    rows, features = key_ref.shape
+    own = rows - ROW_TILE
+    length = own // CHUNKS
+    per = EMBED_SIZE // BLOCK_ROWS
+    early = [
+        pltpu.make_async_copy(src, dst, in_sem.at[k])
+        for k, (src, dst) in enumerate(
+            ((in_recept_hbm, in_recept), (recept_hbm, recept_grad), (in_key_hbm, in_key), (in_value_hbm, in_value))
+        )
+    ]
+    early[0].start()
+    early[1].start()
+    pairs = [(key_hbm, key_ref), (value_hbm, value_ref), (key_part_hbm, key_wide), (value_part_hbm, value_wide)]
+    start_pieces(pairs, piece_sem, own)
+    early[2].start()
+    early[3].start()
+    early[0].wait()
+    early[1].wait()
+    weight_gradient(in_recept, recept_grad, own, slot_ref, slot_grad, store, out_sem.at[2], 2 * per, 2 * per)
+    rate = jnp.exp(vec_ref[5:6])
+    incoming = tuple(incoming_ref[k : k + 1] for k in range(3))
+    carry = merge(
+        tuple(suffix_ref[k] for k in range(3)),
+        aged(tuple(jnp.broadcast_to(v, (CHUNKS, features)) for v in incoming), chunk_ref[:, 5:6], chunk_ref[:, 4:5], rate),
+    )
+    fade = jnp.exp(carry[2] + fade_ref[2]) * (carry[0] * fade_ref[0] + carry[1] * fade_ref[1])
+    sums_ref[0:5] = jnp.zeros((5, features), jnp.float32)
+    sums_ref[5:6] = -rate * (sums_two_ref[4:5] + jnp.sum(fade, axis=0, keepdims=True))
+    sums_ref[6:7] = sums_two_ref[5:6]
+    sums_ref[7:] = sums_two_ref[0:4]
+
+    def spread_back(at, state):
+        value = value_ref[at]
+        lift = jnp.exp(key_ref[at] + state[2])
+        key_grad[at] = (key_wide[at] + lift * (state[0] * value + state[1])).astype(jnp.bfloat16)
+        value_grad[at] = (value_wide[at] + lift * state[0]).astype(jnp.bfloat16)
+
+    carry_wide = tuple(jnp.concatenate([item] * (STEP_TILE // CHUNKS), axis=0) for item in carry)
+    ramp = lax.broadcasted_iota(jnp.int32, (STEP_TILE, 1), 0) // CHUNKS
+
+    def token(i, c):
+        at = rows_at(i, STEP_TILE)
+        distance = (length - 1 - i * (STEP_TILE // CHUNKS) - ramp).astype(jnp.float32)
+        spread_back(at, aged(carry_wide, distance, marks_ref[at, 3:4], rate))
+        return c
+
+    for p in range(PIECES):
+        wait_piece(pairs, piece_sem, own, p)
+        count = own // STEP_TILE
+        lax.fori_loop(p * count // PIECES, (p + 1) * count // PIECES, token, 0)
+    wait_piece(pairs, piece_sem, own, PIECES)
+    halo = tuple(
+        jnp.concatenate([incoming[k], jnp.zeros((ROW_TILE - 1, features), jnp.float32) + (NEGATIVE if k == 2 else 0.0)], axis=0)
+        for k in range(3)
+    )
+    spread_back(slice(own, rows), halo)
+    early[2].wait()
+    early[3].wait()
+    weight_gradient(in_key, key_grad, own, slot_ref, slot_grad, store, out_sem.at[0], 0, 0)
+    weight_gradient(in_value, value_grad, own, slot_ref, slot_grad, store, out_sem.at[1], per, per)
     for m in range(3):
         await_gradient(store, slot_grad, out_sem.at[m], m * per, per)
 
 
-def close_pass(slots, x_rows, vectors, marks, chunk_marks, incoming, suffix, key, value, lows, kept, pool, slot_grad):
-    rows, features = x_rows.shape
-    own = rows - ROW_TILE
+def close_pass(slots, vectors, marks, chunk_marks, incoming, suffix, sums_two, fade, kept, slot_grad):
+    rows, features = kept[0].shape
     vmem = pl.BlockSpec(memory_space=pltpu.VMEM)
     anywhere = pl.BlockSpec(memory_space=pl.ANY)
-    f32 = lambda *shape: pltpu.VMEM(shape, jnp.float32)
-    b16 = lambda *shape: pltpu.VMEM(shape, jnp.bfloat16)
-    operands = (slots, x_rows, vectors, marks, chunk_marks, incoming, suffix, key, value) + lows + kept + (pool, slot_grad)
+    low = jax.ShapeDtypeStruct((rows, features), jnp.bfloat16)
+    operands = (slots, vectors, marks, chunk_marks, incoming, suffix, sums_two, fade) + kept + (slot_grad,)
     return pl.pallas_call(
         close_kernel,
         out_shape=(
-            jax.ShapeDtypeStruct((own, features), jnp.float32),
+            low,
+            low,
             jax.ShapeDtypeStruct(vectors.shape, jnp.float32),
-            jax.ShapeDtypeStruct(pool.shape, jnp.bfloat16),
+            jax.ShapeDtypeStruct(slot_grad.shape, jnp.bfloat16),
         ),
-        in_specs=[pl.BlockSpec(memory_space=pltpu.SMEM)] + [vmem] * (len(operands) - 3) + [anywhere] * 2,
-        out_specs=(vmem, vmem, anywhere),
-        input_output_aliases={len(operands) - 1: 2},
-        scratch_shapes=[
-            f32(rows + 8, features),
-            f32(rows, features),
-            f32(rows, 1),
-            f32(rows, features),
-            f32(rows, features),
-            b16(rows, features),
-            b16(rows, features),
-            f32(rows, features),
-            f32(rows, features),
-            f32(rows, features),
-            f32(rows, features),
-            f32(features // LANES, own, LANES),
-            b16(3 * EMBED_SIZE // BLOCK_ROWS, BLOCK_ROWS, features),
+        in_specs=[pl.BlockSpec(memory_space=pltpu.SMEM)] + [vmem] * 7 + [anywhere] * (len(kept) + 1),
+        out_specs=(vmem, vmem, vmem, anywhere),
+        input_output_aliases={len(operands) - 1: 3},
+        scratch_shapes=[pltpu.VMEM(k.shape, k.dtype) for k in kept] + [
+            pltpu.VMEM((3 * EMBED_SIZE // BLOCK_ROWS, BLOCK_ROWS, features), jnp.bfloat16),
             pltpu.SemaphoreType.DMA((3,)),
-            pltpu.SemaphoreType.DMA((3,)),
+            pltpu.SemaphoreType.DMA((4,)),
+            pltpu.SemaphoreType.DMA((4, PIECES + 1)),
         ],
         compiler_params=pltpu.CompilerParams(vmem_limit_bytes=VMEM_BYTES),
         name="close_pass",
     )(*operands)
 
 
-def chain_kernel(forward, tokens, own_ref, vec_ref, link_ref, flag_ref, out_ref, near, chips, joint, send_sem, recv_sem):
-    me, core, _, _, _ = grid_place()
-    chip = me // 2
-    count = GRID_DEVICES // 2
-    sign = 1 if forward else -1
-    before = chip if forward else count - 1 - chip
-    sibling = me + 1 - 2 * core
-    chips[...] = jnp.zeros_like(chips)
+def chain_kernel(forward, own_ref, vec_ref, link_ref, out_ref, plane, planes, joint, send_sem, recv_sem, far_send, far_recv):
+    me, _, _, _, z = grid_place()
+    place = lax.rem(me, PLANE)
+    base = me - place
+    at = 0 if forward else 2
+    before = z if forward else PLANES - 1 - z
+    step = PLANE if forward else -PLANE
+    planes[...] = jnp.zeros_like(planes)
     bar = pltpu.get_barrier_semaphore()
-    pl.semaphore_signal(bar, inc=1, device_id=(sibling,), device_id_type=MESH)
-    for o in range(1, count):
+    for o in range(1, PLANE):
+        peer = base + lax.rem(place + o, PLANE)
+        pl.semaphore_signal(bar, inc=1, device_id=(peer,), device_id_type=MESH)
+    for o in range(1, PLANES):
         @pl.when(o <= before)
         def _():
-            pl.semaphore_signal(bar, inc=1, device_id=(me - 2 * sign * o,), device_id_type=MESH)
-    pl.semaphore_wait(bar, count - before)
-    swap = pltpu.make_async_remote_copy(
-        src_ref=own_ref, dst_ref=near, send_sem=send_sem.at[0], recv_sem=recv_sem.at[0],
-        device_id=(sibling,), device_id_type=MESH,
-    )
-    swap.start()
+            pl.semaphore_signal(bar, inc=1, device_id=(me - step * o,), device_id_type=MESH)
+    plane[pl.ds(place, 1)] = own_ref[...][None]
     rate = jnp.exp(vec_ref[5:6])
-    at = 0 if forward else 2
-    swap.wait()
-    mine = tuple(own_ref[k : k + 1] for k in range(3))
-    other = tuple(near[k : k + 1] for k in range(3))
-    second = (core == 1) if forward else (core == 0)
-    one = tuple(jnp.where(second, b, a) for a, b in zip(mine, other))
-    two = tuple(jnp.where(second, a, b) for a, b in zip(mine, other))
-    joint[...] = jnp.concatenate(merge(two, aged(one, float(tokens), flag_ref[0:1, at : at + 1], rate)), axis=0)
-
-    def copy(o, place, peer):
+    pl.semaphore_wait(bar, PLANE - 1 + PLANES - 1 - before)
+
+    def near_copy(o, source, peer):
         return pltpu.make_async_remote_copy(
-            src_ref=joint, dst_ref=chips.at[place], send_sem=send_sem.at[o], recv_sem=recv_sem.at[o],
+            src_ref=own_ref, dst_ref=plane.at[source], send_sem=send_sem.at[o], recv_sem=recv_sem.at[o],
             device_id=(peer,), device_id_type=MESH,
         )
 
-    for o in range(1, count):
-        @pl.when(o < count - before)
+    def far_copy(o, source, peer):
+        return pltpu.make_async_remote_copy(
+            src_ref=joint, dst_ref=planes.at[source], send_sem=far_send.at[o], recv_sem=far_recv.at[o],
+            device_id=(peer,), device_id_type=MESH,
+        )
+
+    for o in range(PLANE - 1, 0, -1):
+        near_copy(o, place, base + lax.rem(place + o, PLANE)).start()
+    for o in range(1, PLANE):
+        source = lax.rem(place - o + PLANE, PLANE)
+        near_copy(o, source, base + source).wait_recv()
+
+    def gather_states(ref, first, count):
+        valid = link_ref[first : first + count, at : at + 1]
+        logs = jnp.where(valid > 0.5, ref[:, 2] - link_ref[first : first + count, at + 1 : at + 2] * rate, NEGATIVE)
+        top = jnp.max(logs, axis=0, keepdims=True)
+        weight = jnp.exp(logs - top)
+        return (
+            jnp.sum(weight * ref[:, 0], axis=0, keepdims=True),
+            jnp.sum(weight * ref[:, 1], axis=0, keepdims=True),
+            top,
+        )
+
+    joint[...] = jnp.concatenate(gather_states(plane, PLANE, PLANE), axis=0)
+    for o in range(PLANES - 1, 0, -1):
+        @pl.when(o < PLANES - before)
         def _():
-            copy(o, chip, me + 2 * sign * o).start()
-    for o in range(1, count):
+            far_copy(o, z, me + step * o).start()
+    near = gather_states(plane, 0, PLANE)
+    for o in range(1, PLANES):
         @pl.when(o <= before)
         def _():
-            copy(o, chip - sign * o, sibling).wait_recv()
-    logs = jnp.where(link_ref[:, at : at + 1] > 0.5, chips[:, 2] - link_ref[:, at + 1 : at + 2] * rate, NEGATIVE)
-    top = jnp.max(logs, axis=0, keepdims=True)
-    weight = jnp.exp(logs - top)
-    prior = (
-        jnp.sum(weight * chips[:, 0], axis=0, keepdims=True),
-        jnp.sum(weight * chips[:, 1], axis=0, keepdims=True),
-        top,
-    )
-    beside = merge(one, aged(prior, float(tokens), flag_ref[0:1, at + 1 : at + 2], rate))
-    out_ref[...] = jnp.concatenate([jnp.where(second, b, a) for a, b in zip(prior, beside)], axis=0)
-    for o in range(1, count):
-        @pl.when(o < count - before)
+            source = z - o if forward else z + o
+            far_copy(o, source, me - step * o).wait_recv()
+    last = 2 * PLANE + PLANES
+    old = gather_states(planes, 2 * PLANE, PLANES)
+    old = aged(old, link_ref[last : last + 1, at + 1 : at + 2], link_ref[last : last + 1, at : at + 1], rate)
+    out_ref[...] = jnp.concatenate(merge(near, old), axis=0)
+    for o in range(1, PLANE):
+        near_copy(o, place, base + lax.rem(place + o, PLANE)).wait_send()
+    for o in range(1, PLANES):
+        @pl.when(o < PLANES - before)
         def _():
-            copy(o, chip, me + 2 * sign * o).wait_send()
-
-
-def chain_state(rows, vectors, links, flags, forward, tokens, cid):
+            far_copy(o, z, me + step * o).wait_send()
+
+
+def chain_state(rows, vectors, links, forward, cid):
     devices = lax.axis_size("seq")
     if devices != GRID_DEVICES:
         every = lax.all_gather(rows[None], "seq", axis=0, tiled=True)
@@ -1569,23 +1810,24 @@
         top = jnp.max(logs, axis=0)
         weight = jnp.exp(logs - top)
         return jnp.stack([jnp.sum(weight * every[:, 0], axis=0), jnp.sum(weight * every[:, 1], axis=0), top])
-    count = devices // 2
     vmem = pl.BlockSpec(memory_space=pltpu.VMEM)
     return pl.pallas_call(
-        functools.partial(chain_kernel, forward, tokens),
+        functools.partial(chain_kernel, forward),
         out_shape=jax.ShapeDtypeStruct(rows.shape, jnp.float32),
-        in_specs=[vmem] * 4,
+        in_specs=[vmem] * 3,
         out_specs=vmem,
         scratch_shapes=[
+            pltpu.VMEM((PLANE,) + rows.shape, jnp.float32),
+            pltpu.VMEM((PLANES,) + rows.shape, jnp.float32),
             pltpu.VMEM(rows.shape, jnp.float32),
-            pltpu.VMEM((count,) + rows.shape, jnp.float32),
-            pltpu.VMEM(rows.shape, jnp.float32),
-            pltpu.SemaphoreType.DMA((count,)),
-            pltpu.SemaphoreType.DMA((count,)),
+            pltpu.SemaphoreType.DMA((PLANE,)),
+            pltpu.SemaphoreType.DMA((PLANE,)),
+            pltpu.SemaphoreType.DMA((PLANES,)),
+            pltpu.SemaphoreType.DMA((PLANES,)),
         ],
         compiler_params=pltpu.CompilerParams(collective_id=cid, has_side_effects=True),
         name="chain_forward" if forward else "chain_backward",
-    )(rows, vectors, links, flags)
+    )(rows, vectors, links)
 
 
 def body(
@@ -1617,32 +1859,34 @@
             shifted(tokens_in[tokens - ROW_TILE :], "seq", 1),
         ]
         prepared = prepare_pass(devices, doc_lengths, tokens_in, cotangent, pad_rows, halo, vectors)
-    x_rows, grad_rows, marks, chunk_marks, links, flags, *lows = prepared
+    x_rows, grad_rows, marks, chunk_marks, links, *lows = prepared
     lows = tuple(lows)
-    key, value, recept, num, den, top, prefix, summary = open_pass(
+    prefix, summary, key, value, recept, states, weights = open_pass(
         block_slot, vectors, marks, chunk_marks, lows, gathered
     )
-    incoming = chain_state(summary, vectors, links, flags, True, tokens, 3)
+    incoming = chain_state(summary, vectors, links, True, 3)
     (
-        layer_out, resid_grad, wkv, gw, own_share, recept_grad, suffix, back_summary, sums_two,
-        full_state, back_state, slot_grad,
+        suffix, back_summary, sums_two, fade,
+        layer_out, resid_grad, key_part, value_part, recept_grad, slot_grad,
     ) = middle_pass(
         block_slot, x_rows, grad_rows, vectors, marks, chunk_marks, incoming,
-        (key, value, recept, num, den, top, prefix), gathered,
-    )
-    back_incoming = chain_state(back_summary, vectors, links, flags, False, tokens, 4)
-    input_grad, stacked, slot_grad = close_pass(
-        block_slot, x_rows, vectors, marks, chunk_marks, back_incoming, suffix, key, value,
-        lows,
-        (resid_grad, wkv, gw, own_share, recept_grad, sums_two, full_state, back_state),
-        gathered, slot_grad,
-    )
+        (key, value, recept, states, prefix), gathered,
+    )
+    back_incoming = chain_state(back_summary, vectors, links, False, 4)
+    key_grad, value_grad, stacked, slot_grad = close_pass(
+        block_slot, vectors, marks, chunk_marks, back_incoming, suffix, sums_two, fade,
+        (key, value) + lows + (key_part, value_part, recept_grad), slot_grad,
+    )
+    tail = (vectors, marks, x_rows, resid_grad, key_grad, value_grad, recept_grad, weights)
     own_slots = device_place * masters.shape[0] + jnp.arange(masters.shape[0], dtype=jnp.int32)
     named = jnp.any(own_slots[:, None] == block_slot[None, :], axis=1)
     if devices == GRID_DEVICES:
-        owner_grad, vector_grad = scatter_blocks(slot_grad.reshape((devices,) + masters.shape), stacked)
+        owner_grad, vector_grad, input_grad = scatter_blocks(
+            slot_grad.reshape((devices,) + masters.shape), stacked, tail
+        )
         owner_grad = owner_grad.astype(jnp.float32)
     else:
+        input_grad, stacked = tail_pass(stacked, tail)
         owner_grad = lax.psum_scatter(
             slot_grad.astype(jnp.float32), "seq", scatter_dimension=0, tiled=True
         )

time: 364 us -> 349 us (0.959)
  Pallas kernels: 356 us -> 339 us
    pallas_call x5, Pallas kernels: 103 us -> 84.7 us  [the longest x1 39.7 us: middle_pass(): pl.pallas_call(middle_kernel, out_shape=(jax.ShapeDtypeStruct((3, CHUNKS,...]
where the time goes in v5:
time: 349 us; the launch traced here: 348 us
  Pallas kernels  339 us (97%)
  other arithmetic  7.23 us (2%)
    pallas_call x1, Pallas kernels, scatter_blocks(): pl.pallas_call(functools.partial(scatter_kernel, slots), out_shape=(jax.S...  131 us
    pallas_call x1, Pallas kernels, gather_blocks(): pl.pallas_call(functools.partial(gather_kernel, slots), out_shape=(jax.Sh...  124 us
    pallas_call x1, Pallas kernels, middle_pass(): pl.pallas_call(middle_kernel, out_shape=(jax.ShapeDtypeStruct((3, CHUNKS,...  39.7 us
    pallas_call x2, Pallas kernels, chain_state(): pl.pallas_call(functools.partial(chain_kernel, forward), out_shape=jax.Sh...  23.9 us
    pallas_call x1, Pallas kernels, open_pass(): pl.pallas_call(open_kernel, out_shape=(small(3, CHUNKS, features), small(...  11.3 us
    pallas_call x1, Pallas kernels, close_pass(): pl.pallas_call(close_kernel, out_shape=(low, low, jax.ShapeDtypeStruct(ve...  9.78 us
    sub x2, other arithmetic, adam_update(): weight - step_rate * (first_fixed / (jnp.sqrt(second_fixed) + ADAM_EPS) +...  7.04 us

profile of v5, /device:TPU:0, one launch (start us, length us, event | category | flops | bytes accessed | tf_op | source)
XLA Modules:
  0.0 348.5 jit_solution(12364245301630248159)
XLA Ops:
  0.6 124.1 %gather_blocks.1 = (bf16[32,15,32,1024]{3,2,1,0:T(8,128)(2,1)}, bf16[272,1024]{1,0:T(8,128)(2,1)}, bf16[272,1024]{1,0:T(8,128)(2,1)}, f32[272,4]{1,0:T(8,128)}, ...) custom-call(s32[7]{0:T(128)} %doc_ref.1, ...), custom_call_target="tpu_custom_call" | custom-call | tf_op jit(solution)/shard_map/gather_blocks/pallas_call | solution.py:325
  124.8 11.3 %open_pass.1 = (f32[3,8,1024]{2,1,0:T(8,128)}, f32[3,1024]{1,0:T(4,128)}, f32[272,1024]{1,0:T(8,128)}, f32[272,1024]{1,0:T(8,128)}, f32[272,1024]{1,0:T(8,128)},...) custom-call(s32[416]{0:T(512)} %slot_ref.5, f32[11,1024]{1,0:T(8,128)} %vec_ref.13, ...), custom_call_target="tpu_custom_call" | custom-call | tf_op jit(solution)/shard_map/open_pass/pallas_call | solution.py:1130
  136.0 11.0 %chain_forward.1.incoming_ref = f32[3,1024]{1,0:T(4,128)} custom-call(f32[3,1024]{1,0:T(4,128)} %get-tuple-element.47.own_ref, f32[11,1024]{1,0:T(8,128)} %vec_ref.13, f32[21,4]{1,0:T(8,128)} %get-tuple-element.48.link_ref), custom_call_target="tpu_custom_call" | custom-call | tf_op jit(solution)/shard_map/chain_forward/pallas_call | solution.py:1814
  147.1 39.7 %middle_pass.1 = (f32[3,8,1024]{2,1,0:T(8,128)}, f32[3,1024]{1,0:T(4,128)}, f32[6,1024]{1,0:T(8,128)}, f32[3,8,1024]{2,1,0:T(8,128)}, bf16[256,1024]{1,0:T(8,128...) custom-call(s32[416]{0:T(512)} %slot_ref.5, ...), custom_call_target="tpu_custom_call" | custom-call | tf_op jit(solution)/shard_map/middle_pass/pallas_call | solution.py:1460
  186.8 12.9 %chain_backward.1.incoming_ref = f32[3,1024]{1,0:T(4,128)} custom-call(f32[3,1024]{1,0:T(4,128)} %get-tuple-element.57.own_ref, f32[11,1024]{1,0:T(8,128)} %vec_ref.13, f32[21,4]{1,0:T(8,128)} %get-tuple-element.48.link_ref), custom_call_target="tpu_custom_call" | custom-call | tf_op jit(solution)/shard_map/chain_backward/pallas_call | solution.py:1814
  199.7 9.8 %close_pass.1 = (bf16[272,1024]{1,0:T(8,128)(2,1)}, bf16[272,1024]{1,0:T(8,128)(2,1)}, f32[11,1024]{1,0:T(8,128)}, bf16[480,32,1024]{2,1,0:T(8,128)(2,1)}) custom-call(s32[416]{0:T(512)} %slot_ref.5, f32[11,1024]{1,0:T(8,128)} %vec_ref.13, f32[272,4]{1,0:T(8,128)} %get-tuple-element.41.marks_ref, ...), custom_call_target="tpu_custom_call", output_to_operand_aliasing={{3}: (16, {})} | custom-call | tf_op jit(solution)/shard_map/close_pass/pallas_call | solution.py:1709
  209.5 0.0 copy-start.6
  209.5 0.0 copy-start
  209.5 130.7 %scatter_blocks.1 = (bf16[15,32,1024]{2,1,0:T(8,128)(2,1)}, f32[11,1024]{1,0:T(8,128)}, f32[256,1024]{1,0:T(8,128)}) custom-call(bf16[32,15,32,1024]{3,2,1,0:T(8,128)(2,1)} %bitcast.5, f32[11,1024]{1,0:T(8,128)} %get-tuple-element.66.rows_ref, f32[11,1024]{1,0:T(8,128)} %vec_ref.13, f32[272,4]{1,0:T(8,128)} %get-tuple-element.41.marks_ref, ...), custom_call_target="tpu_custom_call" | custom-call | tf_op jit(solution)/shard_map/scatter_blocks/pallas_call | solution.py:655
  340.2 0.0 copy-done.6
  340.2 0.2 compare_reduce_fusion
  340.4 0.0 copy-done
  340.4 0.0 copy-start.1
  340.4 0.0 copy-start.3
  340.4 0.0 copy-start.4
  340.4 0.0 copy-start.5
  340.4 0.0 copy-start.7
  340.4 0.0 copy-start.2
  340.4 6.3 %multiply_subtract_fusion = (f32[15,32,1024]{2,1,0:T(8,128)}, f32[15,32,1024]{2,1,0:T(8,128)}, f32[15,32,1024]{2,1,0:T(8,128)}) fusion(f32[15,32,1024]{2,1,0:T(8,128)S(1)} %copy-done, bf16[15,32,1024]{2,1,0:T(8,128)(2,1)} %get-tuple-element.72, pred[15]{0:T(512)(128)(4,1)S(1)} %compare_reduce_fusion, f32[15,32,1024]{2,1,0:T(8,128)} %param.18, ...), kind=kLoop, calls=%fused_computation.2 | loop fusion | flops 8355840 | bytes 12779535 | tf_op jit(solution)/shard_map/sub | solution.py:53
  346.8 0.0 copy-done.1
  346.8 0.0 copy-done.3
  346.8 0.0 copy-done.4
  346.8 0.0 copy-done.5
  346.8 0.0 copy-done.7
  346.8 0.7 multiply_subtract_fusion.1
  347.5 0.0 copy-done.2
  347.5 1.0 copy.23
  (1 shorter events, 0.0 us)
Async XLA Ops:
  209.5 130.7 %copy-start.6 = (s32[416]{0:T(512)S(1)}, s32[416]{0:T(512)}, u32[]{:S(2)}) copy-start(s32[416]{0:T(512)} %slot_ref.5) | copy-start | bytes 4996
  209.5 130.9 %copy-start = (f32[15,32,1024]{2,1,0:T(8,128)S(1)}, f32[15,32,1024]{2,1,0:T(8,128)}, u32[]{:S(2)}) copy-start(f32[15,32,1024]{2,1,0:T(8,128)} %master_ref.1) | copy-start | bytes 5898244
  340.4 6.4 %copy-start.1 = (f32[11,1024]{1,0:T(8,128)S(1)}, f32[11,1024]{1,0:T(8,128)}, u32[]{:S(2)}) copy-start(f32[11,1024]{1,0:T(8,128)} %vec_ref.13) | copy-start | bytes 135172
  340.4 6.4 %copy-start.3 = (f32[11,1024]{1,0:T(8,128)S(1)}, f32[11,1024]{1,0:T(8,128)}, u32[]{:S(2)}) copy-start(f32[11,1024]{1,0:T(8,128)} %param.22) | copy-start | bytes 135172
  340.4 6.4 %copy-start.4 = (f32[11,1024]{1,0:T(8,128)S(1)}, f32[11,1024]{1,0:T(8,128)}, u32[]{:S(2)}) copy-start(f32[11,1024]{1,0:T(8,128)} %param.21) | copy-start | bytes 135172
  340.4 6.4 %copy-start.5 = (f32[11,1024]{1,0:T(8,128)S(1)}, f32[11,1024]{1,0:T(8,128)}, u32[]{:S(2)}) copy-start(f32[11,1024]{1,0:T(8,128)} %get-tuple-element.73) | copy-start | bytes 135172
  340.4 6.4 %copy-start.7 = (f32[11]{0:T(128)S(1)}, f32[11]{0:T(128)}, u32[]{:S(2)}) copy-start(f32[11]{0:T(128)} %constant.10.clone) | copy-start | bytes 136
  340.4 7.1 %copy-start.2 = (f32[256,1024]{1,0:T(8,128)S(1)}, f32[256,1024]{1,0:T(8,128)}, u32[]{:S(2)}) copy-start(f32[256,1024]{1,0:T(8,128)} %get-tuple-element.89) | copy-start | bytes 3145732

commit v6 on v5

--- a/solution.py
+++ b/solution.py
@@ -403,6 +403,8 @@
         chip = 4 * q + plane_order()[i]
         return pltpu.make_async_copy(part_ref.at[2 * chip + core], ring.at[i], load_sem.at[i])
 
+    first_level = jnp.where(z >= 2, 0, 3)
+
     def next_level(q):
         inner = jnp.where(q == 3, jnp.where(z == 1, 2, 1), jnp.where(q == 0, jnp.where(z == 1, 1, 3), jnp.where(z == 1, 0, 2)))
         return jnp.where(z == 0, q - 1, jnp.where(z == 3, q + 1, inner))
@@ -427,23 +429,22 @@
             if d == dist:
                 pl.when(have)(functools.partial(work, q, sign, dist))
 
-    def begin_gives(q):
-        for i in plane_order():
-            give(4 * q + i).start()
-
     def chip_of(cu, cv, cz):
         return cz * 4 + jnp.where(core == 0, cv * 2 + cu, cu * 2 + cv)
 
     def plane_order():
         return (chip_of(u2, v2, 0), chip_of(u2, v, 0), chip_of(u, v2, 0), chip_of(u, v, 0))
 
+    def sibling_order():
+        return tuple(plane_order()[i] for i in (0, 2, 1, 3))
+
     for i in range(4):
-        load(i, jnp.where(z >= 2, 0, 3)).start()
+        load(i, first_level).start()
     for copy in tail_loads:
         copy.start()
     pl.semaphore_wait(bar, 5 + jnp.where(zup & zdown, 1, 0))
-    run(3, begin_gives)
-    run(2, begin_gives)
+    for i in range(2):
+        give(4 * first_level + sibling_order()[i]).start()
 
     def ready(i, q):
         chip = 4 * q + plane_order()[i]
@@ -457,9 +458,15 @@
 
         lax.fori_loop(0, slots, step, 0)
 
+        if i < 2:
+            @pl.when(q == first_level)
+            def _():
+                give(4 * q + sibling_order()[i + 2]).start()
+
         @pl.when(q != z)
         def _():
             load(i, next_level(q)).start()
+            give(4 * next_level(q) + sibling_order()[i]).start()
 
     def out_copy(cu, cv, cz, color, target, place):
         lo, n = span[color]
@@ -541,7 +548,7 @@
             (4, u2, v, 0, [VA(q, 1)]),
             (5, u, v2, 1, [UB(q, 1)]),
         )
-        for k, cu, cv, color, pieces in ((kinds[5], kinds[4], kinds[3], kinds[2]), (kinds[0], kinds[1]))[part]:
+        for k, cu, cv, color, pieces in ((kinds[5], kinds[4], kinds[3], kinds[2]), (kinds[0], kinds[1]), (kinds[5], kinds[4]), (kinds[3], kinds[2]))[part]:
             @pl.when(more)
             def _():
                 add(cu, cv, q, color, pieces + [Z(q, k)])
@@ -570,40 +577,41 @@
     run(3, term_d)
     begin_tail()
     tail[0]()
-    run_signed(3, planes)
+    run_signed(3, functools.partial(column, 2))
+    run(2, term_a)
+    run_signed(3, functools.partial(column, 3))
     tail[1]()
-    run(2, term_a)
+    run(3, plane_two)
     run(2, term_c)
-    run(3, plane_two)
+    run_signed(3, last)
+    tail[2]()
     run(2, term_b)
     run(2, term_d)
-    tail[2]()
-    run(1, begin_gives)
-    run_signed(3, last)
     tail[3]()
+    run_signed(2, functools.partial(column, 2))
     run(1, term_a)
-    run(1, term_c)
-    run_signed(2, planes)
-    begin_gives(z)
+    run_signed(2, functools.partial(column, 3))
     tail[4]()
     run(2, plane_two)
+    run(1, term_c)
+    run_signed(2, last)
+    tail[5]()
     run(1, term_b)
     run(1, term_d)
-    run_signed(2, last)
+    row_copy(0).start()
+    run_signed(1, functools.partial(column, 2))
     term_a(z)
+    row_step(0)
+    run_signed(1, functools.partial(column, 3))
+    run(1, plane_two)
     term_c(z)
-    tail[5]()
-    row_copy(0).start()
-    run_signed(1, planes)
-    row_step(0)
-    run(1, plane_two)
+    row_step(1)
+    run_signed(1, last)
     term_b(z)
     term_d(z)
-    row_step(1)
-    run_signed(1, last)
+    row_step(2)
     tail[6]()
     send_input.start()
-    row_step(2)
     plane_two(z)
     row_step(3)
 

time: 349 us -> 343 us (0.983)
  Pallas kernels: 339 us -> 334 us
    pallas_call x1, Pallas kernels: 131 us -> 125 us  [scatter_blocks(): pl.pallas_call(functools.partial(scatter_kernel, slots), out_shape=(jax.S...]
where the time goes in v6:
time: 343 us
  Pallas kernels  334 us (97%)
  other arithmetic  7.23 us (2%)
    pallas_call x1, Pallas kernels, scatter_blocks(): pl.pallas_call(functools.partial(scatter_kernel, slots), out_shape=(jax.S...  125 us
    pallas_call x1, Pallas kernels, gather_blocks(): pl.pallas_call(functools.partial(gather_kernel, slots), out_shape=(jax.Sh...  124 us
    pallas_call x1, Pallas kernels, middle_pass(): pl.pallas_call(middle_kernel, out_shape=(jax.ShapeDtypeStruct((3, CHUNKS,...  39.6 us
    pallas_call x2, Pallas kernels, chain_state(): pl.pallas_call(functools.partial(chain_kernel, forward), out_shape=jax.Sh...  23.9 us
    pallas_call x1, Pallas kernels, open_pass(): pl.pallas_call(open_kernel, out_shape=(small(3, CHUNKS, features), small(...  11.3 us
    pallas_call x1, Pallas kernels, close_pass(): pl.pallas_call(close_kernel, out_shape=(low, low, jax.ShapeDtypeStruct(ve...  9.75 us
    sub x2, other arithmetic, adam_update(): weight - step_rate * (first_fixed / (jnp.sqrt(second_fixed) + ADAM_EPS) +...  7.04 us

profile of v6, /device:TPU:0, one launch (start us, length us, event | category | flops | bytes accessed | tf_op | source)
XLA Modules:
  0.0 343.0 jit_solution(10426376816968474506)
XLA Ops:
  0.6 124.1 %gather_blocks.1 = (bf16[32,15,32,1024]{3,2,1,0:T(8,128)(2,1)}, bf16[272,1024]{1,0:T(8,128)(2,1)}, bf16[272,1024]{1,0:T(8,128)(2,1)}, f32[272,4]{1,0:T(8,128)}, ...) custom-call(s32[7]{0:T(128)} %doc_ref.1, ...), custom_call_target="tpu_custom_call" | custom-call | tf_op jit(solution)/shard_map/gather_blocks/pallas_call | solution.py:325
  124.8 11.3 %open_pass.1 = (f32[3,8,1024]{2,1,0:T(8,128)}, f32[3,1024]{1,0:T(4,128)}, f32[272,1024]{1,0:T(8,128)}, f32[272,1024]{1,0:T(8,128)}, f32[272,1024]{1,0:T(8,128)},...) custom-call(s32[416]{0:T(512)} %slot_ref.5, f32[11,1024]{1,0:T(8,128)} %vec_ref.13, ...), custom_call_target="tpu_custom_call" | custom-call | tf_op jit(solution)/shard_map/open_pass/pallas_call | solution.py:1138
  136.0 11.0 %chain_forward.1.incoming_ref = f32[3,1024]{1,0:T(4,128)} custom-call(f32[3,1024]{1,0:T(4,128)} %get-tuple-element.47.own_ref, f32[11,1024]{1,0:T(8,128)} %vec_ref.13, f32[21,4]{1,0:T(8,128)} %get-tuple-element.48.link_ref), custom_call_target="tpu_custom_call" | custom-call | tf_op jit(solution)/shard_map/chain_forward/pallas_call | solution.py:1822
  147.1 39.6 %middle_pass.1 = (f32[3,8,1024]{2,1,0:T(8,128)}, f32[3,1024]{1,0:T(4,128)}, f32[6,1024]{1,0:T(8,128)}, f32[3,8,1024]{2,1,0:T(8,128)}, bf16[256,1024]{1,0:T(8,128...) custom-call(s32[416]{0:T(512)} %slot_ref.5, ...), custom_call_target="tpu_custom_call" | custom-call | tf_op jit(solution)/shard_map/middle_pass/pallas_call | solution.py:1468
  186.6 12.9 %chain_backward.1.incoming_ref = f32[3,1024]{1,0:T(4,128)} custom-call(f32[3,1024]{1,0:T(4,128)} %get-tuple-element.57.own_ref, f32[11,1024]{1,0:T(8,128)} %vec_ref.13, f32[21,4]{1,0:T(8,128)} %get-tuple-element.48.link_ref), custom_call_target="tpu_custom_call" | custom-call | tf_op jit(solution)/shard_map/chain_backward/pallas_call | solution.py:1822
  199.5 9.8 %close_pass.1 = (bf16[272,1024]{1,0:T(8,128)(2,1)}, bf16[272,1024]{1,0:T(8,128)(2,1)}, f32[11,1024]{1,0:T(8,128)}, bf16[480,32,1024]{2,1,0:T(8,128)(2,1)}) custom-call(s32[416]{0:T(512)} %slot_ref.5, f32[11,1024]{1,0:T(8,128)} %vec_ref.13, f32[272,4]{1,0:T(8,128)} %get-tuple-element.41.marks_ref, ...), custom_call_target="tpu_custom_call", output_to_operand_aliasing={{3}: (16, {})} | custom-call | tf_op jit(solution)/shard_map/close_pass/pallas_call | solution.py:1717
  209.3 0.0 copy-start.6
  209.3 0.0 copy-start
  209.3 125.3 %scatter_blocks.1 = (bf16[15,32,1024]{2,1,0:T(8,128)(2,1)}, f32[11,1024]{1,0:T(8,128)}, f32[256,1024]{1,0:T(8,128)}) custom-call(bf16[32,15,32,1024]{3,2,1,0:T(8,128)(2,1)} %bitcast.5, f32[11,1024]{1,0:T(8,128)} %get-tuple-element.66.rows_ref, f32[11,1024]{1,0:T(8,128)} %vec_ref.13, f32[272,4]{1,0:T(8,128)} %get-tuple-element.41.marks_ref, ...), custom_call_target="tpu_custom_call" | custom-call | tf_op jit(solution)/shard_map/scatter_blocks/pallas_call | solution.py:663
  334.7 0.0 copy-done.6
  334.7 0.2 compare_reduce_fusion
  334.9 0.0 copy-done
  334.9 0.0 copy-start.1
  334.9 0.0 copy-start.3
  334.9 0.0 copy-start.4
  334.9 0.0 copy-start.5
  334.9 0.0 copy-start.7
  334.9 0.0 copy-start.2
  335.0 6.3 %multiply_subtract_fusion = (f32[15,32,1024]{2,1,0:T(8,128)}, f32[15,32,1024]{2,1,0:T(8,128)}, f32[15,32,1024]{2,1,0:T(8,128)}) fusion(f32[15,32,1024]{2,1,0:T(8,128)S(1)} %copy-done, bf16[15,32,1024]{2,1,0:T(8,128)(2,1)} %get-tuple-element.72, pred[15]{0:T(512)(128)(4,1)S(1)} %compare_reduce_fusion, f32[15,32,1024]{2,1,0:T(8,128)} %param.18, ...), kind=kLoop, calls=%fused_computation.2 | loop fusion | flops 8355840 | bytes 12779535 | tf_op jit(solution)/shard_map/sub | solution.py:53
  341.3 0.0 copy-done.1
  341.3 0.0 copy-done.3
  341.3 0.0 copy-done.4
  341.3 0.0 copy-done.5
  341.3 0.0 copy-done.7
  341.3 0.7 multiply_subtract_fusion.1
  342.0 0.0 copy-done.2
  342.0 1.0 copy.23
  (1 shorter events, 0.0 us)
Async XLA Ops:
  209.3 125.4 %copy-start.6 = (s32[416]{0:T(512)S(1)}, s32[416]{0:T(512)}, u32[]{:S(2)}) copy-start(s32[416]{0:T(512)} %slot_ref.5) | copy-start | bytes 4996
  209.3 125.6 %copy-start = (f32[15,32,1024]{2,1,0:T(8,128)S(1)}, f32[15,32,1024]{2,1,0:T(8,128)}, u32[]{:S(2)}) copy-start(f32[15,32,1024]{2,1,0:T(8,128)} %master_ref.1) | copy-start | bytes 5898244
  334.9 6.4 %copy-start.1 = (f32[11,1024]{1,0:T(8,128)S(1)}, f32[11,1024]{1,0:T(8,128)}, u32[]{:S(2)}) copy-start(f32[11,1024]{1,0:T(8,128)} %vec_ref.13) | copy-start | bytes 135172
  334.9 6.4 %copy-start.3 = (f32[11,1024]{1,0:T(8,128)S(1)}, f32[11,1024]{1,0:T(8,128)}, u32[]{:S(2)}) copy-start(f32[11,1024]{1,0:T(8,128)} %param.22) | copy-start | bytes 135172
  334.9 6.4 %copy-start.4 = (f32[11,1024]{1,0:T(8,128)S(1)}, f32[11,1024]{1,0:T(8,128)}, u32[]{:S(2)}) copy-start(f32[11,1024]{1,0:T(8,128)} %param.21) | copy-start | bytes 135172
  334.9 6.4 %copy-start.5 = (f32[11,1024]{1,0:T(8,128)S(1)}, f32[11,1024]{1,0:T(8,128)}, u32[]{:S(2)}) copy-start(f32[11,1024]{1,0:T(8,128)} %get-tuple-element.73) | copy-start | bytes 135172
  334.9 6.4 %copy-start.7 = (f32[11]{0:T(128)S(1)}, f32[11]{0:T(128)}, u32[]{:S(2)}) copy-start(f32[11]{0:T(128)} %constant.10.clone) | copy-start | bytes 136
  334.9 7.1 %copy-start.2 = (f32[256,1024]{1,0:T(8,128)S(1)}, f32[256,1024]{1,0:T(8,128)}, u32[]{:S(2)}) copy-start(f32[256,1024]{1,0:T(8,128)} %get-tuple-element.89) | copy-start | bytes 3145732

commit v7 on v6

--- a/solution.py
+++ b/solution.py
@@ -735,7 +735,7 @@
     ).wait()
 
 
-def times_weight(left_ref, store_ref, place, count, write, width=512):
+def times_weight(left_ref, store_ref, place, count, write, width=1024):
     features = store_ref.shape[2]
 
     def step(n, carry):
@@ -1069,9 +1069,9 @@
 
 
 def open_kernel(
-    slot_ref, vec_ref, marks_ref, chunk_ref, in_key, in_value, in_recept, pool_ref,
-    prefix_ref, summary_ref, key_out, value_out, recept_out, state_out, weights_ref,
-    key_ref, value_ref, recept_ref, num_ref, den_ref, max_ref, store, sem, out_sem,
+    slot_ref, vec_ref, marks_ref, chunk_ref, in_key, in_value, pool_ref,
+    prefix_ref, summary_ref, key_out, value_out, state_out, weights_ref,
+    key_ref, value_ref, num_ref, den_ref, max_ref, store, sem, out_sem,
 ):
     rows, features = in_key.shape
     own = rows - ROW_TILE
@@ -1079,23 +1079,24 @@
     per = EMBED_SIZE // BLOCK_ROWS
     for m in range(3):
         fetch_blocks(slot_ref, pool_ref, store, sem.at[m], m * per, m * per, per)
-    for m, (left, out) in enumerate(((in_key, key_ref), (in_value, value_ref), (in_recept, recept_ref))):
+    for m, (left, out) in enumerate(((in_key, key_ref), (in_value, value_ref))):
         await_blocks(pool_ref, store, sem.at[m], m * per, per)
 
         def write(cols, piece, out=out):
             out[:, cols] = piece
 
         times_weight(left, store, m * per, per, write)
+    await_blocks(pool_ref, store, sem.at[2], 2 * per, per)
     sent = [
         pltpu.make_async_copy(src, dst, out_sem.at[k])
         for k, (src, dst) in enumerate(
             (
-                (key_ref, key_out), (value_ref, value_out), (recept_ref, recept_out), (store, weights_ref),
+                (key_ref, key_out), (value_ref, value_out), (store, weights_ref),
                 (num_ref, state_out.at[0]), (den_ref, state_out.at[1]), (max_ref, state_out.at[2]),
             )
         )
     ]
-    for copy in sent[:4]:
+    for copy in sent[:3]:
         copy.start()
     rate = jnp.exp(vec_ref[5:6])
 
@@ -1111,7 +1112,7 @@
     state = lax.fori_loop(0, length - 1, step, (blank, blank, blank + NEGATIVE))
     late = tuple(item[CHUNKS - 1 :] for item in state)
     ends = step(length - 1, state)
-    for copy in sent[4:]:
+    for copy in sent[3:]:
         copy.start()
     prior = (value_ref[own + 2 : own + 3], jnp.ones((1, features), jnp.float32), key_ref[own + 2 : own + 3])
     for c in range(CHUNKS):
@@ -1138,19 +1139,19 @@
     return pl.pallas_call(
         open_kernel,
         out_shape=(
-            small(3, CHUNKS, features), small(3, features), full, full, full, small(3, own, features),
+            small(3, CHUNKS, features), small(3, features), full, full, small(3, own, features),
             jax.ShapeDtypeStruct(blocks, jnp.bfloat16),
         ),
-        in_specs=[pl.BlockSpec(memory_space=pltpu.SMEM)] + [vmem] * 6 + [anywhere],
-        out_specs=(vmem,) * 2 + (anywhere,) * 5,
-        scratch_shapes=[f32(rows, features)] * 3 + [f32(own, features)] * 3 + [
+        in_specs=[pl.BlockSpec(memory_space=pltpu.SMEM)] + [vmem] * 5 + [anywhere],
+        out_specs=(vmem,) * 2 + (anywhere,) * 4,
+        scratch_shapes=[f32(rows, features)] * 2 + [f32(own, features)] * 3 + [
             pltpu.VMEM(blocks, jnp.bfloat16),
             pltpu.SemaphoreType.DMA((3,)),
-            pltpu.SemaphoreType.DMA((7,)),
+            pltpu.SemaphoreType.DMA((6,)),
         ],
         compiler_params=pltpu.CompilerParams(vmem_limit_bytes=VMEM_BYTES),
         name="open_pass",
-    )(slots, vectors, marks, chunk_marks, *lows, pool)
+    )(slots, vectors, marks, chunk_marks, *lows[:2], pool)
 
 
 def middle_kernel(
@@ -1736,13 +1737,27 @@
     )(*operands)
 
 
-def chain_kernel(forward, own_ref, vec_ref, link_ref, out_ref, plane, planes, joint, send_sem, recv_sem, far_send, far_recv):
+def chain_kernel(forward, own_ref, vec_ref, link_ref, *refs):
+    if forward:
+        left_hbm, weights_hbm, out_ref, product_hbm, *refs = refs
+        *refs, left, weights, product_ref, work_sem = refs
+    else:
+        out_ref, *refs = refs
+    plane, planes, joint, send_sem, recv_sem, far_send, far_recv = refs
     me, _, _, _, z = grid_place()
     place = lax.rem(me, PLANE)
     base = me - place
     at = 0 if forward else 2
     before = z if forward else PLANES - 1 - z
     step = PLANE if forward else -PLANE
+    if forward:
+        per = EMBED_SIZE // BLOCK_ROWS
+        loads = (
+            pltpu.make_async_copy(left_hbm, left, work_sem.at[0]),
+            pltpu.make_async_copy(weights_hbm.at[pl.ds(2 * per, per)], weights, work_sem.at[1]),
+        )
+        for copy in loads:
+            copy.start()
     planes[...] = jnp.zeros_like(planes)
     bar = pltpu.get_barrier_semaphore()
     for o in range(1, PLANE):
@@ -1770,6 +1785,16 @@
 
     for o in range(PLANE - 1, 0, -1):
         near_copy(o, place, base + lax.rem(place + o, PLANE)).start()
+    if forward:
+        for copy in loads:
+            copy.wait()
+
+        def write(cols, piece):
+            product_ref[:, cols] = piece
+
+        times_weight(left, weights, 0, per, write)
+        leave = pltpu.make_async_copy(product_ref, product_hbm, work_sem.at[2])
+        leave.start()
     for o in range(1, PLANE):
         source = lax.rem(place - o + PLANE, PLANE)
         near_copy(o, source, base + source).wait_recv()
@@ -1800,6 +1825,8 @@
     old = gather_states(planes, 2 * PLANE, PLANES)
     old = aged(old, link_ref[last : last + 1, at + 1 : at + 2], link_ref[last : last + 1, at : at + 1], rate)
     out_ref[...] = jnp.concatenate(merge(near, old), axis=0)
+    if forward:
+        leave.wait()
     for o in range(1, PLANE):
         near_copy(o, place, base + lax.rem(place + o, PLANE)).wait_send()
     for o in range(1, PLANES):
@@ -1808,7 +1835,7 @@
             far_copy(o, z, me + step * o).wait_send()
 
 
-def chain_state(rows, vectors, links, forward, cid):
+def chain_state(rows, vectors, links, forward, cid, work=()):
     devices = lax.axis_size("seq")
     if devices != GRID_DEVICES:
         every = lax.all_gather(rows[None], "seq", axis=0, tiled=True)
@@ -1817,13 +1844,30 @@
         logs = jnp.where(links[:, at : at + 1] > 0.5, aged_logs, NEGATIVE)
         top = jnp.max(logs, axis=0)
         weight = jnp.exp(logs - top)
-        return jnp.stack([jnp.sum(weight * every[:, 0], axis=0), jnp.sum(weight * every[:, 1], axis=0), top])
+        state = jnp.stack([jnp.sum(weight * every[:, 0], axis=0), jnp.sum(weight * every[:, 1], axis=0), top])
+        if not forward:
+            return state
+        left, weights = work
+        right = weights[2 * EMBED_SIZE // BLOCK_ROWS :].reshape(EMBED_SIZE, -1)
+        return state, jnp.dot(left, right, preferred_element_type=jnp.float32)
     vmem = pl.BlockSpec(memory_space=pltpu.VMEM)
+    anywhere = pl.BlockSpec(memory_space=pl.ANY)
+    out_shape, out_specs, extra = jax.ShapeDtypeStruct(rows.shape, jnp.float32), vmem, []
+    if forward:
+        left, weights = work
+        wide = jax.ShapeDtypeStruct(left.shape, jnp.float32)
+        out_shape, out_specs = (out_shape, wide), (vmem, anywhere)
+        extra = [
+            pltpu.VMEM(left.shape, left.dtype),
+            pltpu.VMEM((EMBED_SIZE // BLOCK_ROWS,) + weights.shape[1:], weights.dtype),
+            pltpu.VMEM(left.shape, jnp.float32),
+            pltpu.SemaphoreType.DMA((3,)),
+        ]
     return pl.pallas_call(
         functools.partial(chain_kernel, forward),
-        out_shape=jax.ShapeDtypeStruct(rows.shape, jnp.float32),
-        in_specs=[vmem] * 3,
-        out_specs=vmem,
+        out_shape=out_shape,
+        in_specs=[vmem] * 3 + [anywhere] * len(work),
+        out_specs=out_specs,
         scratch_shapes=[
             pltpu.VMEM((PLANE,) + rows.shape, jnp.float32),
             pltpu.VMEM((PLANES,) + rows.shape, jnp.float32),
@@ -1832,10 +1876,10 @@
             pltpu.SemaphoreType.DMA((PLANE,)),
             pltpu.SemaphoreType.DMA((PLANES,)),
             pltpu.SemaphoreType.DMA((PLANES,)),
-        ],
-        compiler_params=pltpu.CompilerParams(collective_id=cid, has_side_effects=True),
+        ] + extra,
+        compiler_params=pltpu.CompilerParams(collective_id=cid, has_side_effects=True, vmem_limit_bytes=VMEM_BYTES),
         name="chain_forward" if forward else "chain_backward",
-    )(rows, vectors, links)
+    )(rows, vectors, links, *work)
 
 
 def body(
@@ -1869,10 +1913,10 @@
         prepared = prepare_pass(devices, doc_lengths, tokens_in, cotangent, pad_rows, halo, vectors)
     x_rows, grad_rows, marks, chunk_marks, links, *lows = prepared
     lows = tuple(lows)
-    prefix, summary, key, value, recept, states, weights = open_pass(
+    prefix, summary, key, value, states, weights = open_pass(
         block_slot, vectors, marks, chunk_marks, lows, gathered
     )
-    incoming = chain_state(summary, vectors, links, True, 3)
+    incoming, recept = chain_state(summary, vectors, links, True, 3, (lows[2], weights))
     (
         suffix, back_summary, sums_two, fade,
         layer_out, resid_grad, key_part, value_part, recept_grad, slot_grad,

time: 343 us -> 341 us (level)
  no operation moved by 1% of the time
where the time goes in v7:
time: 341 us
  Pallas kernels  332 us (97%)
  other arithmetic  7.23 us (2%)
    pallas_call x1, Pallas kernels, scatter_blocks(): pl.pallas_call(functools.partial(scatter_kernel, slots), out_shape=(jax.S...  125 us
    pallas_call x1, Pallas kernels, gather_blocks(): pl.pallas_call(functools.partial(gather_kernel, slots), out_shape=(jax.Sh...  124 us
    pallas_call x1, Pallas kernels, middle_pass(): pl.pallas_call(middle_kernel, out_shape=(jax.ShapeDtypeStruct((3, CHUNKS,...  38.9 us
    pallas_call x2, Pallas kernels, chain_state(): pl.pallas_call(functools.partial(chain_kernel, forward), out_shape=out_sh...  23.9 us
    pallas_call x1, Pallas kernels, open_pass(): pl.pallas_call(open_kernel, out_shape=(small(3, CHUNKS, features), small(...  9.83 us
    pallas_call x1, Pallas kernels, close_pass(): pl.pallas_call(close_kernel, out_shape=(low, low, jax.ShapeDtypeStruct(ve...  9.8 us
    sub x2, other arithmetic, adam_update(): weight - step_rate * (first_fixed / (jnp.sqrt(second_fixed) + ADAM_EPS) +...  7.04 us

profile of v7, /device:TPU:0, one launch (start us, length us, event | category | flops | bytes accessed | tf_op | source)
XLA Modules:
  0.0 341.0 jit_solution(2772826125894812055)
XLA Ops:
  0.6 124.1 %gather_blocks.1 = (bf16[32,15,32,1024]{3,2,1,0:T(8,128)(2,1)}, bf16[272,1024]{1,0:T(8,128)(2,1)}, bf16[272,1024]{1,0:T(8,128)(2,1)}, f32[272,4]{1,0:T(8,128)}, ...) custom-call(s32[7]{0:T(128)} %doc_ref.1, ...), custom_call_target="tpu_custom_call" | custom-call | tf_op jit(solution)/shard_map/gather_blocks/pallas_call | solution.py:325
  124.8 9.8 %open_pass.1 = (f32[3,8,1024]{2,1,0:T(8,128)}, f32[3,1024]{1,0:T(4,128)}, f32[272,1024]{1,0:T(8,128)}, f32[272,1024]{1,0:T(8,128)}, f32[3,256,1024]{2,1,0:T(8,128)}, /*index=5*/bf16[96,32,1024]{2,1,0:T(8,128)(2,1)}) custom-call(s32[416]{0:T(512)} %slot_ref.5, f32[11,1024]{1,0:T(8,128)} %vec_ref.13, f32[272,4]{1,0:T(8,128)} %get-tuple-element.42.marks_ref, ...), custom_call_target="tpu_custom_call" | custom-call | tf_op jit(solution)/shard_map/open_pass/pallas_call | solution.py:1139
  134.6 11.0 %chain_forward.1 = (f32[3,1024]{1,0:T(4,128)}, f32[272,1024]{1,0:T(8,128)}) custom-call(f32[3,1024]{1,0:T(4,128)} %get-tuple-element.47.own_ref, f32[11,1024]{1,0:T(8,128)} %vec_ref.13, f32[21,4]{1,0:T(8,128)} %get-tuple-element.48.link_ref, bf16[272,1024]{1,0:T(8,128)(2,1)} %get-tuple-element.49.refs_0_.in_recept_hbm, ...), custom_call_target="tpu_custom_call" | custom-call | tf_op jit(solution)/shard_map/chain_forward/pallas_call | solution.py:1866
  145.7 38.9 %middle_pass.1 = (f32[3,8,1024]{2,1,0:T(8,128)}, f32[3,1024]{1,0:T(4,128)}, f32[6,1024]{1,0:T(8,128)}, f32[3,8,1024]{2,1,0:T(8,128)}, bf16[256,1024]{1,0:T(8,128...) custom-call(s32[416]{0:T(512)} %slot_ref.5, ...), custom_call_target="tpu_custom_call" | custom-call | tf_op jit(solution)/shard_map/middle_pass/pallas_call | solution.py:1469
  184.6 12.9 %chain_backward.1.incoming_ref = f32[3,1024]{1,0:T(4,128)} custom-call(f32[3,1024]{1,0:T(4,128)} %get-tuple-element.60.own_ref, f32[11,1024]{1,0:T(8,128)} %vec_ref.13, f32[21,4]{1,0:T(8,128)} %get-tuple-element.48.link_ref), custom_call_target="tpu_custom_call" | custom-call | tf_op jit(solution)/shard_map/chain_backward/pallas_call | solution.py:1866
  197.5 9.8 %close_pass.1 = (bf16[272,1024]{1,0:T(8,128)(2,1)}, bf16[272,1024]{1,0:T(8,128)(2,1)}, f32[11,1024]{1,0:T(8,128)}, bf16[480,32,1024]{2,1,0:T(8,128)(2,1)}) custom-call(s32[416]{0:T(512)} %slot_ref.5, f32[11,1024]{1,0:T(8,128)} %vec_ref.13, f32[272,4]{1,0:T(8,128)} %get-tuple-element.42.marks_ref, ...), custom_call_target="tpu_custom_call", output_to_operand_aliasing={{3}: (16, {})} | custom-call | tf_op jit(solution)/shard_map/close_pass/pallas_call | solution.py:1718
  207.3 0.0 copy-start.6
  207.3 0.0 copy-start
  207.3 125.4 %scatter_blocks.1 = (bf16[15,32,1024]{2,1,0:T(8,128)(2,1)}, f32[11,1024]{1,0:T(8,128)}, f32[256,1024]{1,0:T(8,128)}) custom-call(bf16[32,15,32,1024]{3,2,1,0:T(8,128)(2,1)} %bitcast.5, f32[11,1024]{1,0:T(8,128)} %get-tuple-element.69.rows_ref, f32[11,1024]{1,0:T(8,128)} %vec_ref.13, f32[272,4]{1,0:T(8,128)} %get-tuple-element.42.marks_ref, ...), custom_call_target="tpu_custom_call" | custom-call | tf_op jit(solution)/shard_map/scatter_blocks/pallas_call | solution.py:663
  332.7 0.0 copy-done.6
  332.7 0.2 compare_reduce_fusion
  332.9 0.0 copy-done
  332.9 0.0 copy-start.1
  332.9 0.0 copy-start.3
  332.9 0.0 copy-start.4
  332.9 0.0 copy-start.5
  332.9 0.0 copy-start.7
  333.0 0.0 copy-start.2
  333.0 6.3 %multiply_subtract_fusion = (f32[15,32,1024]{2,1,0:T(8,128)}, f32[15,32,1024]{2,1,0:T(8,128)}, f32[15,32,1024]{2,1,0:T(8,128)}) fusion(f32[15,32,1024]{2,1,0:T(8,128)S(1)} %copy-done, bf16[15,32,1024]{2,1,0:T(8,128)(2,1)} %get-tuple-element.74, pred[15]{0:T(512)(128)(4,1)S(1)} %compare_reduce_fusion, f32[15,32,1024]{2,1,0:T(8,128)} %param.18, ...), kind=kLoop, calls=%fused_computation.2 | loop fusion | flops 8355840 | bytes 12779535 | tf_op jit(solution)/shard_map/sub | solution.py:53
  339.3 0.0 copy-done.1
  339.3 0.0 copy-done.3
  339.3 0.0 copy-done.4
  339.3 0.0 copy-done.5
  339.3 0.0 copy-done.7
  339.3 0.7 multiply_subtract_fusion.1
  340.0 0.0 copy-done.2
  340.0 1.0 copy.23
  (1 shorter events, 0.0 us)
Async XLA Ops:
  207.3 125.4 %copy-start.6 = (s32[416]{0:T(512)S(1)}, s32[416]{0:T(512)}, u32[]{:S(2)}) copy-start(s32[416]{0:T(512)} %slot_ref.5) | copy-start | bytes 4996
  207.3 125.6 %copy-start = (f32[15,32,1024]{2,1,0:T(8,128)S(1)}, f32[15,32,1024]{2,1,0:T(8,128)}, u32[]{:S(2)}) copy-start(f32[15,32,1024]{2,1,0:T(8,128)} %master_ref.1) | copy-start | bytes 5898244
  332.9 6.4 %copy-start.1 = (f32[11,1024]{1,0:T(8,128)S(1)}, f32[11,1024]{1,0:T(8,128)}, u32[]{:S(2)}) copy-start(f32[11,1024]{1,0:T(8,128)} %vec_ref.13) | copy-start | bytes 135172
  332.9 6.4 %copy-start.3 = (f32[11,1024]{1,0:T(8,128)S(1)}, f32[11,1024]{1,0:T(8,128)}, u32[]{:S(2)}) copy-start(f32[11,1024]{1,0:T(8,128)} %param.22) | copy-start | bytes 135172
  332.9 6.4 %copy-start.4 = (f32[11,1024]{1,0:T(8,128)S(1)}, f32[11,1024]{1,0:T(8,128)}, u32[]{:S(2)}) copy-start(f32[11,1024]{1,0:T(8,128)} %param.21) | copy-start | bytes 135172
  332.9 6.4 %copy-start.5 = (f32[11,1024]{1,0:T(8,128)S(1)}, f32[11,1024]{1,0:T(8,128)}, u32[]{:S(2)}) copy-start(f32[11,1024]{1,0:T(8,128)} %get-tuple-element.75) | copy-start | bytes 135172
  332.9 6.4 %copy-start.7 = (f32[11]{0:T(128)S(1)}, f32[11]{0:T(128)}, u32[]{:S(2)}) copy-start(f32[11]{0:T(128)} %constant.10.clone) | copy-start | bytes 136
  333.0 7.1 %copy-start.2 = (f32[256,1024]{1,0:T(8,128)S(1)}, f32[256,1024]{1,0:T(8,128)}, u32[]{:S(2)}) copy-start(f32[256,1024]{1,0:T(8,128)} %get-tuple-element.91) | copy-start | bytes 3145732

commit v8 on v7

--- a/solution.py
+++ b/solution.py
@@ -66,12 +66,18 @@
     return [(cuts[i], cuts[i + 1] - cuts[i]) for i in range(3)]
 
 def gather_kernel(
-    slots, doc_ref, master_ref, tokens_ref, cot_ref, pad_ref, vec_ref,
+    slots, doc_ref, tokens_ref, cot_ref, pad_ref, vec_ref, master_hbm,
     out_ref, x_ref, grad_ref, marks_ref, chunk_ref, link_ref, in_key, in_value, in_recept,
-    column, ext, wide, wide_grad, own_ref, head_grad, after_ref, after_grad_ref, before_ref,
+    column, ext, wide, wide_grad, master_ref, own_ref, head_grad, after_ref, after_grad_ref, before_ref,
     *scratch,
 ):
-    send_sem, recv_sem, sib_send, sib_recv, own_sem, halo_send, halo_recv = scratch
+    send_sem, recv_sem, sib_send, sib_recv, own_sem, halo_send, halo_recv, master_sem = scratch
+    master_loads = [
+        pltpu.make_async_copy(master_hbm.at[pl.ds(lo, n)], master_ref.at[pl.ds(lo, n)], master_sem.at[k])
+        for k, (lo, n) in enumerate(spans(slots))
+    ]
+    for copy in master_loads:
+        copy.start()
     me, core, x, y, z = grid_place()
     sib = me + 1 - 2 * core
     x_peer = me + 2 - 4 * x
@@ -102,9 +108,9 @@
         own_ref[s] = master_ref[s].astype(own_ref.dtype)
         return carry
 
-    lax.fori_loop(0, slots, lower, 0)
-    mask_column(pad_ref, column)
-    head_grad[...] = (cot_ref[0:ROW_TILE].astype(jnp.float32) * column[0:ROW_TILE]).astype(jnp.bfloat16)
+    for copy, (lo, n) in zip(master_loads, spans(slots)):
+        copy.wait()
+        lax.fori_loop(lo, lo + n, lower, 0)
     halos = jnp.where(more, 1, 0) + jnp.where(less, 1, 0)
     pl.semaphore_wait(bar, 4 + jnp.where((z > 0) & (z < 3), 1, 0) + halos)
     tokens = tokens_ref.shape[0]
@@ -171,6 +177,9 @@
         go(send(x, y, z, color, way, True))
     for color in range(3):
         go(send_sib(x, y, z, color, True))
+
+    mask_column(pad_ref, column)
+    head_grad[...] = (cot_ref[0:ROW_TILE].astype(jnp.float32) * column[0:ROW_TILE]).astype(jnp.bfloat16)
 
     @pl.when(less)
     def _():
@@ -325,9 +334,10 @@
     return pl.pallas_call(
         functools.partial(gather_kernel, slots),
         out_shape=(jax.ShapeDtypeStruct((GRID_DEVICES,) + masters.shape, jnp.bfloat16),) + shapes,
-        in_specs=[pl.BlockSpec(memory_space=pltpu.SMEM)] + [vmem] * 5,
+        in_specs=[pl.BlockSpec(memory_space=pltpu.SMEM)] + [vmem] * 4 + [anywhere],
         out_specs=(anywhere,) + (vmem,) * len(shapes),
         scratch_shapes=scratch + [
+            pltpu.VMEM(masters.shape, jnp.float32),
             pltpu.VMEM(masters.shape, jnp.bfloat16),
             halo, halo, halo, halo,
             pltpu.SemaphoreType.DMA((16, 3, 4)),
@@ -337,10 +347,11 @@
             pltpu.SemaphoreType.DMA((3,)),
             pltpu.SemaphoreType.DMA((3,)),
             pltpu.SemaphoreType.DMA((3,)),
+            pltpu.SemaphoreType.DMA((3,)),
         ],
         compiler_params=pltpu.CompilerParams(collective_id=cid, has_side_effects=True, vmem_limit_bytes=VMEM_BYTES),
         name="gather_blocks",
-    )(doc_lengths, masters, tokens_in, cotangent, pad_rows, vectors)
+    )(doc_lengths, tokens_in, cotangent, pad_rows, vectors, masters)
 
 
 def scatter_spans(slots):

time: 341 us -> 341 us (level)
  no operation moved by 1% of the time
where the time goes in v8:
time: 341 us
  Pallas kernels  332 us (97%)
  other arithmetic  7.23 us (2%)
    pallas_call x1, Pallas kernels, scatter_blocks(): pl.pallas_call(functools.partial(scatter_kernel, slots), out_shape=(jax.S...  126 us
    pallas_call x1, Pallas kernels, gather_blocks(): pl.pallas_call(functools.partial(gather_kernel, slots), out_shape=(jax.Sh...  124 us
    pallas_call x1, Pallas kernels, middle_pass(): pl.pallas_call(middle_kernel, out_shape=(jax.ShapeDtypeStruct((3, CHUNKS,...  38.9 us
    pallas_call x2, Pallas kernels, chain_state(): pl.pallas_call(functools.partial(chain_kernel, forward), out_shape=out_sh...  23.9 us
    pallas_call x1, Pallas kernels, open_pass(): pl.pallas_call(open_kernel, out_shape=(small(3, CHUNKS, features), small(...  9.83 us
    pallas_call x1, Pallas kernels, close_pass(): pl.pallas_call(close_kernel, out_shape=(low, low, jax.ShapeDtypeStruct(ve...  9.75 us
    sub x2, other arithmetic, adam_update(): weight - step_rate * (first_fixed / (jnp.sqrt(second_fixed) + ADAM_EPS) +...  7.04 us

profile of v8, /device:TPU:0, one launch (start us, length us, event | category | flops | bytes accessed | tf_op | source)
XLA Modules:
  0.0 340.9 jit_solution(6028724406460235280)
XLA Ops:
  0.6 123.5 %gather_blocks.1 = (bf16[32,15,32,1024]{3,2,1,0:T(8,128)(2,1)}, bf16[272,1024]{1,0:T(8,128)(2,1)}, bf16[272,1024]{1,0:T(8,128)(2,1)}, f32[272,4]{1,0:T(8,128)}, ...) custom-call(s32[7]{0:T(128)} %doc_ref.1, ...), custom_call_target="tpu_custom_call" | custom-call | tf_op jit(solution)/shard_map/gather_blocks/pallas_call | solution.py:334
  124.2 9.8 %open_pass.1 = (f32[3,8,1024]{2,1,0:T(8,128)}, f32[3,1024]{1,0:T(4,128)}, f32[272,1024]{1,0:T(8,128)}, f32[272,1024]{1,0:T(8,128)}, f32[3,256,1024]{2,1,0:T(8,128)}, /*index=5*/bf16[96,32,1024]{2,1,0:T(8,128)(2,1)}) custom-call(s32[416]{0:T(512)} %slot_ref.5, f32[11,1024]{1,0:T(8,128)} %vec_ref.13, f32[272,4]{1,0:T(8,128)} %get-tuple-element.42.marks_ref, ...), custom_call_target="tpu_custom_call" | custom-call | tf_op jit(solution)/shard_map/open_pass/pallas_call | solution.py:1150
  134.0 11.0 %chain_forward.1 = (f32[3,1024]{1,0:T(4,128)}, f32[272,1024]{1,0:T(8,128)}) custom-call(f32[3,1024]{1,0:T(4,128)} %get-tuple-element.47.own_ref, f32[11,1024]{1,0:T(8,128)} %vec_ref.13, f32[21,4]{1,0:T(8,128)} %get-tuple-element.48.link_ref, bf16[272,1024]{1,0:T(8,128)(2,1)} %get-tuple-element.49.refs_0_.in_recept_hbm, ...), custom_call_target="tpu_custom_call" | custom-call | tf_op jit(solution)/shard_map/chain_forward/pallas_call | solution.py:1877
  145.1 38.9 %middle_pass.1 = (f32[3,8,1024]{2,1,0:T(8,128)}, f32[3,1024]{1,0:T(4,128)}, f32[6,1024]{1,0:T(8,128)}, f32[3,8,1024]{2,1,0:T(8,128)}, bf16[256,1024]{1,0:T(8,128...) custom-call(s32[416]{0:T(512)} %slot_ref.5, ...), custom_call_target="tpu_custom_call" | custom-call | tf_op jit(solution)/shard_map/middle_pass/pallas_call | solution.py:1480
  184.0 12.9 %chain_backward.1.incoming_ref = f32[3,1024]{1,0:T(4,128)} custom-call(f32[3,1024]{1,0:T(4,128)} %get-tuple-element.60.own_ref, f32[11,1024]{1,0:T(8,128)} %vec_ref.13, f32[21,4]{1,0:T(8,128)} %get-tuple-element.48.link_ref), custom_call_target="tpu_custom_call" | custom-call | tf_op jit(solution)/shard_map/chain_backward/pallas_call | solution.py:1877
  196.9 9.7 %close_pass.1 = (bf16[272,1024]{1,0:T(8,128)(2,1)}, bf16[272,1024]{1,0:T(8,128)(2,1)}, f32[11,1024]{1,0:T(8,128)}, bf16[480,32,1024]{2,1,0:T(8,128)(2,1)}) custom-call(s32[416]{0:T(512)} %slot_ref.5, f32[11,1024]{1,0:T(8,128)} %vec_ref.13, f32[272,4]{1,0:T(8,128)} %get-tuple-element.42.marks_ref, ...), custom_call_target="tpu_custom_call", output_to_operand_aliasing={{3}: (16, {})} | custom-call | tf_op jit(solution)/shard_map/close_pass/pallas_call | solution.py:1729
  206.6 0.0 copy-start.6
  206.7 0.0 copy-start
  206.7 125.9 %scatter_blocks.1 = (bf16[15,32,1024]{2,1,0:T(8,128)(2,1)}, f32[11,1024]{1,0:T(8,128)}, f32[256,1024]{1,0:T(8,128)}) custom-call(bf16[32,15,32,1024]{3,2,1,0:T(8,128)(2,1)} %bitcast.5, f32[11,1024]{1,0:T(8,128)} %get-tuple-element.69.rows_ref, f32[11,1024]{1,0:T(8,128)} %vec_ref.13, f32[272,4]{1,0:T(8,128)} %get-tuple-element.42.marks_ref, ...), custom_call_target="tpu_custom_call" | custom-call | tf_op jit(solution)/shard_map/scatter_blocks/pallas_call | solution.py:674
  332.5 0.0 copy-done.6
  332.6 0.2 compare_reduce_fusion
  332.7 0.0 copy-done
  332.7 0.0 copy-start.1
  332.8 0.0 copy-start.3
  332.8 0.0 copy-start.4
  332.8 0.0 copy-start.5
  332.8 0.0 copy-start.7
  332.8 0.0 copy-start.2
  332.8 6.3 %multiply_subtract_fusion = (f32[15,32,1024]{2,1,0:T(8,128)}, f32[15,32,1024]{2,1,0:T(8,128)}, f32[15,32,1024]{2,1,0:T(8,128)}) fusion(f32[15,32,1024]{2,1,0:T(8,128)S(1)} %copy-done, bf16[15,32,1024]{2,1,0:T(8,128)(2,1)} %get-tuple-element.74, pred[15]{0:T(512)(128)(4,1)S(1)} %compare_reduce_fusion, f32[15,32,1024]{2,1,0:T(8,128)} %param.18, ...), kind=kLoop, calls=%fused_computation.2 | loop fusion | flops 8355840 | bytes 12779535 | tf_op jit(solution)/shard_map/sub | solution.py:53
  339.1 0.0 copy-done.1
  339.2 0.0 copy-done.3
  339.2 0.0 copy-done.4
  339.2 0.0 copy-done.5
  339.2 0.0 copy-done.7
  339.2 0.7 multiply_subtract_fusion.1
  339.9 0.0 copy-done.2
  339.9 1.0 copy.23
  (1 shorter events, 0.0 us)
Async XLA Ops:
  206.6 125.9 %copy-start.6 = (s32[416]{0:T(512)S(1)}, s32[416]{0:T(512)}, u32[]{:S(2)}) copy-start(s32[416]{0:T(512)} %slot_ref.5) | copy-start | bytes 4996
  206.7 126.1 %copy-start = (f32[15,32,1024]{2,1,0:T(8,128)S(1)}, f32[15,32,1024]{2,1,0:T(8,128)}, u32[]{:S(2)}) copy-start(f32[15,32,1024]{2,1,0:T(8,128)} %master_hbm.1) | copy-start | bytes 5898244
  332.7 6.4 %copy-start.1 = (f32[11,1024]{1,0:T(8,128)S(1)}, f32[11,1024]{1,0:T(8,128)}, u32[]{:S(2)}) copy-start(f32[11,1024]{1,0:T(8,128)} %vec_ref.13) | copy-start | bytes 135172
  332.8 6.4 %copy-start.3 = (f32[11,1024]{1,0:T(8,128)S(1)}, f32[11,1024]{1,0:T(8,128)}, u32[]{:S(2)}) copy-start(f32[11,1024]{1,0:T(8,128)} %param.22) | copy-start | bytes 135172
  332.8 6.4 %copy-start.4 = (f32[11,1024]{1,0:T(8,128)S(1)}, f32[11,1024]{1,0:T(8,128)}, u32[]{:S(2)}) copy-start(f32[11,1024]{1,0:T(8,128)} %param.21) | copy-start | bytes 135172
  332.8 6.4 %copy-start.5 = (f32[11,1024]{1,0:T(8,128)S(1)}, f32[11,1024]{1,0:T(8,128)}, u32[]{:S(2)}) copy-start(f32[11,1024]{1,0:T(8,128)} %get-tuple-element.75) | copy-start | bytes 135172
  332.8 6.4 %copy-start.7 = (f32[11]{0:T(128)S(1)}, f32[11]{0:T(128)}, u32[]{:S(2)}) copy-start(f32[11]{0:T(128)} %constant.10.clone) | copy-start | bytes 136
  332.8 7.1 %copy-start.2 = (f32[256,1024]{1,0:T(8,128)S(1)}, f32[256,1024]{1,0:T(8,128)}, u32[]{:S(2)}) copy-start(f32[256,1024]{1,0:T(8,128)} %get-tuple-element.91) | copy-start | bytes 3145732
